TPU v7x, 32 devices: a whole 2x2x4 slice. The times are simulated.
32 devices in a mesh: chan: 16 (over z, x, core), stn: 2 (over y).
Axes of the slice: x: 2, y: 2, z: 4, core: 2. Of those that a mesh axis runs over, the one named last changes fastest.
Arguments:
- voltages: bfloat16 [16, 2, 256, 512], P(None, None, ('stn', 'chan')), may hold values from -6 to 6
- phase_index: int32 [256], P(('stn', 'chan')), may hold values from 0 to 1023
- int_lengths: int32 [4], replicated, may hold values from 1 to 192, 512 in all
- beam_weights: bfloat16 [2, 256, 256], replicated, may hold values from -0.375 to 0.375
Outputs:
- visibilities: bfloat16 [2, 2, 4, 16, 2, 128, 128], P('stn', None, None, 'chan')
- beam_power: float32 [4, 16, 256], P(None, 'chan', 'stn')
Inputs may be any that keep to these rules, and one draw needn't show every extreme that they name: `int_lengths`: 4 integration lengths summing to 512; the longest is exactly 192.
All inputs are finite; a program needn't handle non-finite values.
Results may differ from a plain program's by a relative error of at most 0.0055.
Values may be sent and summed in bfloat16 or wider, within the bound.
No kernel may reach another device: no remote copies, remote signals or barrier semaphores. Data moves between devices by JAX's collectives and lax.ppermute only.
A program may use at most 64 MiB of HBM per device.

v0:
```python
import math

import jax
import jax.numpy as jnp
from jax import lax
from jax.sharding import PartitionSpec as P

INTEG = 4
MOST = 192
BEAMS = 256
PHASES = 1024


full_turn = 2.0 * math.pi


def shifted(value, axis, by):
    length = lax.axis_size(axis)
    return lax.ppermute(value, axis, [(i, (i + by) % length) for i in range(length)])


def rotate(voltages, phase_index, channel):
    phase_turns = channel[:, None] * phase_index[None, :] % PHASES
    phase_angle = phase_turns.astype(jnp.float32) * (full_turn / PHASES)
    cosine = jnp.cos(phase_angle)[:, :, None]
    sine_part = jnp.sin(phase_angle)[:, :, None]
    real_in = voltages[:, 0].astype(jnp.float32)
    imag_in = voltages[:, 1].astype(jnp.float32)
    return jnp.stack(
        [real_in * cosine + imag_in * sine_part, imag_in * cosine - real_in * sine_part], axis=1
    ).astype(jnp.bfloat16)


def windows(block, starts, int_lengths):
    padded = jnp.pad(block, ((0, 0), (0, 0), (0, MOST)))
    in_range = jnp.arange(MOST, dtype=jnp.int32)
    result = []
    for period in range(INTEG):
        segment = lax.dynamic_slice_in_dim(padded, starts[period], MOST, 2)
        keep_mask = (in_range < int_lengths[period])[None, None, :]
        result.append(jnp.where(keep_mask, segment, jnp.zeros_like(segment)))
    return jnp.stack(result)


def correlate(own_parts, other, starts, int_lengths):
    padded = jnp.pad(other, ((0, 0), (0, 0), (0, MOST)))
    block_rows = own_parts.shape[2] // 2
    result = []
    for period in range(INTEG):
        segment = lax.dynamic_slice_in_dim(padded, starts[period], MOST, 2)
        products = jnp.einsum(
            "cal,cbl->cab", own_parts[period], segment, preferred_element_type=jnp.float32
        )
        real_part = products[:, :block_rows, :block_rows] + products[:, block_rows:, block_rows:]
        imag_part = products[:, block_rows:, :block_rows] - products[:, :block_rows, block_rows:]
        inverse = 1.0 / int_lengths[period].astype(jnp.float32)
        result.append((jnp.stack([real_part, imag_part], axis=1) * inverse).astype(jnp.bfloat16))
    return jnp.stack(result)


def stack_weights(beam_weights, beam_count, column_first, column_count):
    weight_real = lax.dynamic_slice(beam_weights[0], (0, column_first), (beam_count, column_count))
    weight_imag = lax.dynamic_slice(beam_weights[1], (0, column_first), (beam_count, column_count))
    upper = jnp.concatenate([weight_real, -weight_imag], axis=1)
    lower = jnp.concatenate([weight_imag, weight_real], axis=1)
    return jnp.concatenate([upper, lower], axis=0)


def integrate(power, starts, int_lengths, form):
    samples = power.shape[-1]
    sample_index = jnp.arange(samples, dtype=jnp.int32)[None, :]
    in_window = (
        (sample_index >= starts[:, None]) & (sample_index < (starts + int_lengths)[:, None])
    ).astype(jnp.float32)
    summed = jnp.einsum(form, power, in_window, precision=lax.Precision.HIGHEST)
    return summed / int_lengths.astype(jnp.float32)[:, None, None]


def local(voltages, phase_index, int_lengths, beam_weights):
    channel = jnp.arange(voltages.shape[0], dtype=jnp.int32)
    rotated = rotate(voltages, phase_index, channel)
    turned = lax.all_to_all(rotated, "chan", split_axis=0, concat_axis=2, tiled=True)
    station = lax.axis_index("stn")
    stations = lax.axis_size("stn")
    halfway = stations // 2
    share = BEAMS // stations
    ch_local, _, block_rows, samples = turned.shape
    own = turned.reshape(ch_local, 2 * block_rows, samples)
    starts = jnp.cumsum(int_lengths) - int_lengths
    own_parts = windows(own, starts, int_lengths)
    slots = [correlate(own_parts, own, starts, int_lengths)]
    for offset in range(1, halfway + 1):
        other = shifted(turned, "stn", -offset)
        slots.append(
            correlate(
                own_parts, other.reshape(ch_local, 2 * block_rows, samples), starts, int_lengths
            )
        )
    vis_total = jnp.stack(slots)
    stacked = stack_weights(
        beam_weights, lax.axis_size("stn") * share, station * block_rows, block_rows
    )
    partial_beam = jnp.einsum("rk,ckt->crt", stacked, own, preferred_element_type=jnp.float32)
    beam_total = lax.psum_scatter(
        partial_beam.reshape(ch_local, 2, lax.axis_size("stn") * share, samples)
        .transpose(2, 0, 1, 3)
        .astype(jnp.bfloat16),
        "stn",
        scatter_dimension=0,
        tiled=True,
    ).astype(jnp.float32)
    power = beam_total[:, :, 0] ** 2 + beam_total[:, :, 1] ** 2
    beam_power = integrate(power, starts, int_lengths, "bct,jt->jcb")
    return (vis_total[None], beam_power)


def solution(mesh):
    return jax.shard_map(
        local,
        mesh=mesh,
        in_specs=(P(None, None, ("stn", "chan"), None), P(("stn", "chan")), P(), P()),
        out_specs=(P("stn", None, None, "chan", None, None, None), P(None, "chan", "stn")),
        check_vma=False,
    )
```

profile of v0, /device:TPU:0, one launch (start us, length us, event | category | flops | bytes accessed | tf_op | source)
XLA Modules:
  0.0 59.0 jit_solution(5483759724921158643)
XLA Ops:
  7.2 0.7 %fusion.96 = (f32[16,8]{1,0:T(8,128)S(1)}, f32[16,8]{1,0:T(8,128)S(1)}) fusion(s32[8]{0:T(128)} %param.5), kind=kLoop, calls=%fused_computation.149 | loop fusion | flops 1792 | bytes 1056 | tf_op jit(solution)/shard_map/cos | solution.py:25
  7.9 1.1 %fusion.1 = (bf16[16,1,8,512]{3,2,1,0:T(8,128)(2,1)S(1)}, bf16[16,1,8,512]{3,2,1,0:T(8,128)(2,1)S(1)}) fusion(f32[16,8]{1,0:T(8,128)S(1)} %get-tuple-element.43, f32[16,8]{1,0:T(8,128)S(1)} %get-tuple-element.42, bf16[16,2,8,512]{3,2,1,0:T(8,128)(2,1)} %param.4), kind=kLoop, calls=%fused_computation.24 | loop fusion | flops 655360 | bytes 525312 | tf_op jit(solution)/shard_map/convert
  9.0 0.7 %pad_maximum_fusion = bf16[16,2,8,512]{3,2,1,0:T(8,128)(2,1)} fusion(bf16[16,1,8,512]{3,2,1,0:T(8,128)(2,1)S(1)} %get-tuple-element.11, bf16[16,1,8,512]{3,2,1,0:T(8,128)(2,1)S(1)} %get-tuple-element.10), kind=kLoop, calls=%fused_computation.31 | loop fusion | flops 131072 | bytes 524288 | tf_op jit(solution)/shard_map/stack | solution.py:29
  9.7 0.0 copy-start.1
  9.7 0.0 copy-start
  9.8 7.5 %all-to-all-start = ((bf16[16,2,8,512]{3,2,1,0:T(8,128)(2,1)}), bf16[16,2,8,512]{3,2,1,0:T(8,128)(2,1)S(1)}, u32[]{:S(2)}, u32[]{:S(2)}) async-start(bf16[16,2,8,512]{3,2,1,0:T(8,128)(2,1)} %pad_maximum_fusion), calls=%async_computation | async-start | bytes 524288 | tf_op jit(solution)/shard_map/all_to_all | solution.py:82
  17.2 0.0 reduce-scatter.2.cloned.1.call-start
  17.3 0.0 copy-done.1
  17.3 0.7 %fusion.118 = (s32[1]{0:T(128)}, s32[1]{0:T(128)}, s32[1]{0:T(128)}, s32[1]{0:T(128)}) fusion(s32[4]{0:T(128)S(1)} %copy-done.1), kind=kLoop, calls=%fused_computation.177 | loop fusion | bytes 32 | tf_op jit(solution)/shard_map/slice | solution.py:40
  18.0 0.2 reduce-window.8
  18.2 0.6 %fusion.119 = (s32[1]{0:T(128)}, s32[1]{0:T(128)}, s32[1]{0:T(128)}, s32[1]{0:T(128)}) fusion(s32[4]{0:T(128)S(1)} %get-tuple-element.33), kind=kLoop, calls=%fused_computation.178 | loop fusion | bytes 32 | tf_op jit(solution)/shard_map/slice | solution.py:39
  18.8 0.7 %iota_compare_fusion.5 = pred[192]{0:T(512)(128)(4,1)S(1)} fusion(s32[]{:T(128)} %bitcast.13), kind=kLoop, calls=%fused_computation.160 | loop fusion | flops 192 | bytes 196 | tf_op jit(solution)/shard_map/lt | solution.py:40
  19.5 0.6 %iota_compare_fusion.4 = pred[192]{0:T(512)(128)(4,1)S(1)} fusion(s32[]{:T(128)} %bitcast.22), kind=kLoop, calls=%fused_computation.159 | loop fusion | flops 192 | bytes 196 | tf_op jit(solution)/shard_map/lt | solution.py:40
  20.1 0.6 iota_compare_fusion.3
  20.7 0.6 %iota_compare_fusion.6 = pred[192]{0:T(512)(128)(4,1)S(1)} fusion(s32[]{:T(128)} %bitcast), kind=kLoop, calls=%fused_computation.161 | loop fusion | flops 192 | bytes 196 | tf_op jit(solution)/shard_map/lt | solution.py:40
  31.4 0.0 copy-done
  31.5 0.0 all-to-all-done
  31.5 1.6 %collective-permute-start = (bf16[1,2,128,512]{3,2,1,0:T(8,128)(2,1)S(1)}, bf16[1,2,128,512]{3,2,1,0:T(8,128)(2,1)S(1)}, u32[]{:S(2)}, u32[]{:S(2)}) collective-permute-start(bf16[1,2,128,512]{3,2,1,0:T(8,128)(2,1)S(1)} %bitcast.162), channel_id=1, source_target_pairs={{0,1},{1,0},{2,3},{3,2},{4,5},{5,4},{6,7},{7,6},{8,9},{9,8},{10,11... | collective-permute-start | bytes 786440 | tf_op jit(solution)/shard_map/ppermute | solution.py:19
  33.1 0.3 convolution_bitcast_fusion.6
  33.4 0.3 convolution_bitcast_fusion.5
  33.8 0.3 convolution_bitcast_fusion.7
  34.1 1.1 %convolution_convert_fusion = bf16[512,512]{0,1:T(8,128)(2,1)} fusion(bf16[256,512]{1,0:T(8,128)(2,1)S(1)} %bitcast.166, bf16[256,128]{1,0:T(8,128)(2,1)S(1)} %dynamic-slice_bitcast_fusion.1, bf16[256,128]{1,0:T(8,128)(2,1)S(1)} %get-tuple-element.9, bf16[256,128]{1,0:T(8,128)(2,1)S(1)} %get-tuple-element.8), kind=kOutput, calls=%fused_computation | convolution fusion | flops 135528448 | bytes 983040 | tf_op jit(solution)/shard_map/rk,ckt->crt/dot_general | solution.py:103
  35.2 0.0 reduce-scatter.2.cloned.1.call-update
  35.2 0.3 convolution_bitcast_fusion.4
  35.6 4.6 %collective-permute-done = bf16[1,2,128,512]{3,2,1,0:T(8,128)(2,1)S(1)} collective-permute-done((bf16[1,2,128,512]{3,2,1,0:T(8,128)(2,1)S(1)}, bf16[1,2,128,512]{3,2,1,0:T(8,128)(2,1)S(1)}, u32[]{:S(2)}, u32[]{:S(2)}) %collective-permute-start) | collective-permute-done | bytes 262176 | tf_op jit(solution)/shard_map/ppermute | solution.py:19
  40.2 0.3 convolution_bitcast_fusion.2
  40.5 0.3 convolution_bitcast_fusion.1
  40.9 0.3 convolution_bitcast_fusion.3
  41.3 0.3 convolution_bitcast_fusion
  41.8 0.8 %maximum_bitcast_fusion = bf16[1,2,4,1,2,128,128]{6,5,4,3,2,1,0:T(8,128)(2,1)} fusion(bf16[1,4,1,2,128,128]{5,4,3,1,2,0:T(8,128)(2,1)S(1)} %maximum_bitcast_fusion.2, bf16[1,4,1,2,128,128]{5,4,3,1,2,0:T(8,128)(2,1)S(1)} %maximum_bitcast_fusion.1), kind=kLoop, calls=%fused_computation.10 | loop fusion | flops 262144 | bytes 1048576
  42.6 7.7 %reduce-scatter.2.cloned.1.call-done = bf16[128,1,2,512]{3,0,2,1:T(8,128)(2,1)} async-done(((bf16[256,1,2,512]{3,0,2,1:T(8,128)(2,1)}), bf16[128,1,2,512]{3,0,2,1:T(8,128)(2,1)}) %reduce-scatter.2.cloned.1.call-update) | async-done | bytes 262160 | tf_op jit(solution)/shard_map/reduce_scatter | solution.py:104
  50.3 1.0 %convert_element_type.179 = f32[128,1,2,512]{3,0,2,1:T(8,128)S(1)} convert(bf16[128,1,2,512]{3,0,2,1:T(8,128)(2,1)} %reduce-scatter.2.cloned.1.call-done) | non-fusion elementwise | flops 131072 | bytes 786432 | tf_op jit(solution)/shard_map/convert_element_type | solution.py:111
  51.3 0.9 %convolution_divide_fusion = f32[4,128]{1,0:T(4,128)} fusion(f32[128,1,2,512]{3,0,2,1:T(8,128)S(1)} %convert_element_type.179, s32[4]{0:T(128)S(1)} %bitcast.178, s32[4]{0:T(128)S(1)} %get-tuple-element.33, f32[4]{0:T(128)S(1)} %get-tuple-element.32), kind=kOutput, calls=%fused_computation.9 | convolution fusion | flops 3348992 | bytes 526384 | tf_op jit(solution)/shard_map/bct,jt->jcb/dot_general | solution.py:75
  (20 shorter events, 0.4 us)
Async XLA Ops:
  9.7 7.6 %copy-start.1 = (s32[4]{0:T(128)S(1)}, s32[4]{0:T(128)}, u32[]{:S(2)}) copy-start(s32[4]{0:T(128)} %param.6) | copy-start | bytes 52
  9.7 21.6 %copy-start = (bf16[2,256,256]{2,1,0:T(8,128)(2,1)S(1)}, bf16[2,256,256]{2,1,0:T(8,128)(2,1)}, u32[]{:S(2)}) copy-start(bf16[2,256,256]{2,1,0:T(8,128)(2,1)} %param.7) | copy-start | bytes 786436
  9.8 21.7 %all-to-all-start = ((bf16[16,2,8,512]{3,2,1,0:T(8,128)(2,1)}), bf16[16,2,8,512]{3,2,1,0:T(8,128)(2,1)S(1)}, u32[]{:S(2)}, u32[]{:S(2)}) async-start(bf16[16,2,8,512]{3,2,1,0:T(8,128)(2,1)} %pad_maximum_fusion), calls=%async_computation | async-start | bytes 524288 | tf_op jit(solution)/shard_map/all_to_all | solution.py:82
  17.2 33.1 %reduce-scatter.2.cloned.1.call-start = ((), (), s32[]{:S(2)}) async-start(), calls=%async_computation.2 | async-start | bytes 786432 | tf_op jit(solution)/shard_map/reduce_scatter | solution.py:104
  31.5 8.7 %collective-permute-start = (bf16[1,2,128,512]{3,2,1,0:T(8,128)(2,1)S(1)}, bf16[1,2,128,512]{3,2,1,0:T(8,128)(2,1)S(1)}, u32[]{:S(2)}, u32[]{:S(2)}) collective-permute-start(bf16[1,2,128,512]{3,2,1,0:T(8,128)(2,1)S(1)} %bitcast.162), channel_id=1, source_target_pairs={{0,1},{1,0},{2,3},{3,2},{4,5},{5,4},{6,7},{7,6},{8,9},{9,8},{10,11... | collective-permute-start | bytes 786440 | tf_op jit(solution)/shard_map/ppermute | solution.py:19
Sparse Core Ops, SparseCore 0:
  35.4 14.9 reduce-scatter.1
where the time goes:
time: 59.5 us; the launch traced here: 59 us
  between operations  24.4 us (41%)
  waiting for transfers between devices  12.3 us (21%)
  starting transfers between devices  9.11 us (15%)
  other arithmetic  7.46 us (13%)
  matrix products  4.41 us (7%)
  local copies, waits for them, and re-layouts  1.36 us (2%)
    reduce_scatter x1, waiting for transfers between devices, local(): lax.psum_scatter(partial_beam.reshape(ch_local, 2, lax.axis_size('stn') *...  7.69 us
    all_to_all x1, starting transfers between devices, local(): lax.all_to_all(rotated, 'chan', split_axis=0, concat_axis=2, tiled=True)  7.49 us
    ppermute x1, waiting for transfers between devices, shifted(): lax.ppermute(value, axis, [(i, (i + by) % length) for i in range(length)])  4.62 us
    lt x4, other arithmetic, windows(): keep_mask = (in_range < int_lengths[period])[None, None, :]  2.52 us
    dot_general x8, matrix products, correlate(): jnp.einsum('cal,cbl->cab', own_parts[period], segment, preferred_element_...  2.47 us
    ppermute x1, starting transfers between devices, shifted(): lax.ppermute(value, axis, [(i, (i + by) % length) for i in range(length)])  1.58 us
    another operation x2, other arithmetic  1.3 us
  transfers between devices with their start and end apart: 3, of which 2 were waited for; matrix products, arithmetic and copies ran while one was open for 15% of the time, Pallas kernels for 0%

commit v1 on v0

v1 whole, which is shorter than its diff:
```python
import functools
import math

import jax
import jax.numpy as jnp
from jax import lax
from jax.experimental import pallas as pl
from jax.experimental.pallas import tpu as pltpu
from jax.sharding import PartitionSpec as P

PHASES = 1024
VMEM_BYTES = 32 * 1024 * 1024


def phasors(turns):
    quarter = PHASES // 4
    quadrant = (turns + quarter // 2) // quarter
    x = (turns - quadrant * quarter).astype(jnp.float32) * (2.0 * math.pi / PHASES)
    xx = x * x
    sine = x * (1.0 + xx * (-1.0 / 6 + xx * (1.0 / 120 + xx * (-1.0 / 5040 + xx * (1.0 / 362880)))))
    cosine = 1.0 + xx * (-0.5 + xx * (1.0 / 24 + xx * (-1.0 / 720 + xx * (1.0 / 40320))))
    odd = (quadrant % 2) == 1
    cos_out = jnp.where(odd, sine, cosine)
    sin_out = jnp.where(odd, cosine, sine)
    cos_out = jnp.where((quadrant == 1) | (quadrant == 2), -cos_out, cos_out)
    sin_out = jnp.where((quadrant == 2) | (quadrant == 3), -sin_out, sin_out)
    return cos_out, sin_out


def rotate_kernel(phase_ref, volt_ref, out_ref):
    channels, _, rows, samples = volt_ref.shape
    row = lax.broadcasted_iota(jnp.int32, (rows, 128), 0)
    channel = lax.broadcasted_iota(jnp.int32, (rows, 128), 1)
    step = jnp.zeros((rows, 128), jnp.int32)
    for r in range(rows):
        step = jnp.where(row == r, phase_ref[r], step)
    cosine, sine = phasors((step * channel) % PHASES)
    for c in range(channels):
        cos_c = cosine[:, c : c + 1]
        sin_c = sine[:, c : c + 1]
        real_in = volt_ref[c, 0].astype(jnp.float32)
        imag_in = volt_ref[c, 1].astype(jnp.float32)
        real_out = (real_in * cos_c + imag_in * sin_c).astype(jnp.bfloat16)
        imag_out = (imag_in * cos_c - real_in * sin_c).astype(jnp.bfloat16)
        for s in range(out_ref.shape[0]):
            out_ref[s, c, 0] = real_out
            out_ref[s, c, 1] = imag_out


def rotate(voltages, phase_index, copies):
    return pl.pallas_call(
        rotate_kernel,
        out_shape=jax.ShapeDtypeStruct((copies, *voltages.shape), jnp.bfloat16),
        in_specs=[
            pl.BlockSpec(memory_space=pltpu.SMEM),
            pl.BlockSpec(memory_space=pltpu.VMEM),
        ],
        out_specs=pl.BlockSpec(memory_space=pltpu.VMEM),
        compiler_params=pltpu.CompilerParams(vmem_limit_bytes=VMEM_BYTES),
    )(phase_index, voltages)


def dot_nt(a, b):
    return lax.dot_general(a, b, (((1,), (1,)), ((), ())), preferred_element_type=jnp.float32)


def finish_kernel(length_ref, weight_ref, blocks_ref, vis_ref, power_ref):
    stations, twice, samples = blocks_ref.shape
    half = twice // 2
    integs = length_ref.shape[0]
    slots = vis_ref.shape[1]
    share = power_ref.shape[2]
    station = lax.axis_index("stn")

    sample = lax.broadcasted_iota(jnp.int32, (1, samples), 1)
    masks = []
    start = jnp.int32(0)
    for j in range(integs):
        end = start + length_ref[j]
        masks.append(jnp.where((sample >= start) & (sample < end), 1.0, 0.0))
        start = end

    own = blocks_ref[station]
    for j in range(integs):
        part = own * masks[j].astype(jnp.bfloat16)
        inverse = 1.0 / jnp.full((1, half), length_ref[j], jnp.int32).astype(jnp.float32)
        for k in range(slots):
            other = own if k == 0 else blocks_ref[lax.rem(station + k, stations)]
            prod = dot_nt(part, other)
            real = prod[:half, :half] + prod[half:, half:]
            imag = prod[half:, :half] - prod[:half, half:]
            vis_ref[0, k, j, 0, 0] = (real * inverse).astype(jnp.bfloat16)
            vis_ref[0, k, j, 0, 1] = (imag * inverse).astype(jnp.bfloat16)

    rows = pl.ds(pl.multiple_of(station * share, share), share)
    beam = jnp.zeros((2 * share, samples), jnp.float32)
    for b in range(stations):
        w_real = weight_ref[0, rows, b * half : (b + 1) * half]
        w_imag = weight_ref[1, rows, b * half : (b + 1) * half]
        stacked = jnp.concatenate(
            [
                jnp.concatenate([w_real, -w_imag], axis=1),
                jnp.concatenate([w_imag, w_real], axis=1),
            ],
            axis=0,
        )
        beam = beam + jnp.dot(stacked, blocks_ref[b], preferred_element_type=jnp.float32)
    power = beam[:share] * beam[:share] + beam[share:] * beam[share:]
    high = power.astype(jnp.bfloat16)
    low = (power - high.astype(jnp.float32)).astype(jnp.bfloat16)
    window = jnp.concatenate(
        masks + [jnp.zeros((16 - integs, samples), jnp.float32)], axis=0
    ).astype(jnp.bfloat16)
    summed = dot_nt(window, high) + dot_nt(window, low)
    for j in range(integs):
        count = jnp.full((1, share), length_ref[j], jnp.int32).astype(jnp.float32)
        power_ref[j] = summed[j : j + 1] / count


def finish(int_lengths, beam_weights, blocks, slots):
    stations, twice, samples = blocks.shape
    integs = int_lengths.shape[0]
    half = twice // 2
    return pl.pallas_call(
        finish_kernel,
        out_shape=(
            jax.ShapeDtypeStruct((1, slots, integs, 1, 2, half, half), jnp.bfloat16),
            jax.ShapeDtypeStruct((integs, 1, beam_weights.shape[1] // stations), jnp.float32),
        ),
        in_specs=[
            pl.BlockSpec(memory_space=pltpu.SMEM),
            pl.BlockSpec(memory_space=pltpu.VMEM),
            pl.BlockSpec(memory_space=pltpu.VMEM),
        ],
        out_specs=(
            pl.BlockSpec(memory_space=pltpu.VMEM),
            pl.BlockSpec(memory_space=pltpu.VMEM),
        ),
        compiler_params=pltpu.CompilerParams(vmem_limit_bytes=VMEM_BYTES),
    )(int_lengths, beam_weights, blocks)


def local(voltages, phase_index, int_lengths, beam_weights):
    stations = lax.axis_size("stn")
    channels, parts, rows, samples = voltages.shape
    sent = rotate(voltages, phase_index, stations)
    got = lax.all_to_all(
        sent.reshape(stations * channels, parts, rows, samples),
        ("stn", "chan"),
        split_axis=0,
        concat_axis=0,
        tiled=True,
    )
    blocks = (
        got.reshape(stations, channels, parts, rows, samples)
        .transpose(0, 2, 1, 3, 4)
        .reshape(stations, parts * channels * rows, samples)
    )
    return finish(int_lengths, beam_weights, blocks, stations // 2 + 1)


def solution(mesh):
    return jax.shard_map(
        local,
        mesh=mesh,
        in_specs=(P(None, None, ("stn", "chan"), None), P(("stn", "chan")), P(), P()),
        out_specs=(P("stn", None, None, "chan", None, None, None), P(None, "chan", "stn")),
        check_vma=False,
    )
```

time: 59.5 us -> 29.5 us (0.50)
  between operations: 24.4 us -> 0.66 us
  blocking collectives: 0 us -> 23 us
  waiting for transfers between devices: 12.3 us -> 0 us
  starting transfers between devices: 9.11 us -> 0 us
  other arithmetic: 7.46 us -> 0 us
  matrix products: 4.41 us -> 0 us
  Pallas kernels: 0 us -> 3.04 us
  local copies, waits for them, and re-layouts: 1.36 us -> 2.53 us
    all_to_all x0 -> x1, blocking collectives: none -> 23 us  [local(): lax.all_to_all(sent.reshape(stations * channels, parts, rows, samples), (...]
    reduce_scatter x1 -> x0, waiting for transfers between devices: 7.69 us -> none  [local(): lax.psum_scatter(partial_beam.reshape(ch_local, 2, lax.axis_size('stn') *...]
    all_to_all x1 -> x0, starting transfers between devices: 7.49 us -> none  [local(): lax.all_to_all(rotated, 'chan', split_axis=0, concat_axis=2, tiled=True)]
    ppermute x1 -> x0, waiting for transfers between devices: 4.62 us -> none  [shifted(): lax.ppermute(value, axis, [(i, (i + by) % length) for i in range(length)])]
    dot_general x10 -> x0, matrix products: 4.41 us -> none  [the longest x8 2.47 us: correlate(): jnp.einsum('cal,cbl->cab', own_parts[period], segment, preferred_element_...]
    pallas_call x0 -> x2, Pallas kernels: none -> 3.04 us  [the longest x1 2.3 us: finish(): pl.pallas_call(finish_kernel, out_shape=(jax.ShapeDtypeStruct((1, slots,...]
    lt x4 -> x0, other arithmetic: 2.52 us -> none  [windows(): keep_mask = (in_range < int_lengths[period])[None, None, :]]
    unnamed x4 -> x8, local copies, waits for them, and re-layouts: 0.01 us -> 2.5 us
  transfers between devices with their start and end apart: 3 -> 0, of which waited for: 2 -> 0; matrix products, arithmetic and copies ran while one was open for 15% -> 0% of each run, Pallas kernels for 0% -> 0%
where the time goes in v1:
time: 29.5 us; the launch traced here: 29.3 us
  blocking collectives  23 us (78%)
  Pallas kernels  3.04 us (10%)
  local copies, waits for them, and re-layouts  2.53 us (9%)
  between operations  0.66 us (2%)
    all_to_all x1, blocking collectives, local(): lax.all_to_all(sent.reshape(stations * channels, parts, rows, samples), (...  23 us
    unnamed x8, local copies, waits for them, and re-layouts  2.5 us
    pallas_call x1, Pallas kernels, finish(): pl.pallas_call(finish_kernel, out_shape=(jax.ShapeDtypeStruct((1, slots,...  2.3 us
    pallas_call x1, Pallas kernels, rotate(): pl.pallas_call(rotate_kernel, out_shape=jax.ShapeDtypeStruct((copies, *vo...  0.74 us

profile of v1, /device:TPU:0, one launch (start us, length us, event | category | flops | bytes accessed | tf_op | source)
XLA Modules:
  0.0 29.3 jit_solution(14696796440567655956)
XLA Ops:
  0.6 0.0 copy-start
  0.6 0.9 %copy-done = bf16[16,2,8,512]{3,2,1,0:T(8,128)(2,1)S(1)} copy-done((bf16[16,2,8,512]{3,2,1,0:T(8,128)(2,1)S(1)}, bf16[16,2,8,512]{3,2,1,0:T(8,128)(2,1)}, u32[]{:S(2)}) %copy-start) | copy-done | bytes 262168
  1.6 0.0 copy-start.2
  1.6 0.7 %copy-done.2 = s32[8]{0:T(128)S(1)} copy-done((s32[8]{0:T(128)S(1)}, s32[8]{0:T(128)}, u32[]{:S(2)}) %copy-start.2) | copy-done | bytes 56
  2.2 0.7 %shard_map.59 = bf16[2,16,2,8,512]{4,3,2,1,0:T(8,128)(2,1)S(1)} custom-call(s32[8]{0:T(128)S(1)} %copy-done.2, bf16[16,2,8,512]{3,2,1,0:T(8,128)(2,1)S(1)} %copy-done), custom_call_target="tpu_custom_call" | custom-call | tf_op jit(solution)/shard_map/pallas_call | solution.py:51
  3.0 23.0 %all_to_all.5 = bf16[32,2,8,512]{3,2,1,0:T(8,128)(2,1)S(1)} all-to-all(bf16[32,2,8,512]{3,2,1,0:T(8,128)(2,1)S(1)} %bitcast.6), channel_id=1, replica_groups=mesh['chan'=16,'stn'=2] {'stn','chan'}, dimensions={0} | all-to-all | bytes 1048576 | tf_op jit(solution)/shard_map/all_to_all | solution.py:147
  26.0 0.0 copy-start.1
  26.0 0.0 copy-start.3
  26.1 0.9 %copy-done.1 = bf16[2,256,256]{2,1,0:T(8,128)(2,1)S(1)} copy-done((bf16[2,256,256]{2,1,0:T(8,128)(2,1)S(1)}, bf16[2,256,256]{2,1,0:T(8,128)(2,1)}, u32[]{:S(2)}) %copy-start.1) | copy-done | bytes 262168
  27.0 0.0 copy-done.3
  27.0 2.3 %shard_map.60 = (bf16[1,2,4,1,2,128,128]{6,5,4,3,2,1,0:T(8,128)(2,1)}, f32[4,1,128]{2,1,0:T(1,128)}) custom-call(s32[4]{0:T(128)S(1)} %copy-done.3, bf16[2,256,256]{2,1,0:T(8,128)(2,1)S(1)} %copy-done.1, bf16[2,256,512]{2,1,0:T(8,128)(2,1)S(1)} %bitcast.5), custom_call_target="tpu_custom_call" | custom-call | tf_op jit(solution)/shard_map/pallas_call | solution.py:124
  (1 shorter events, 0.0 us)
Async XLA Ops:
  0.6 1.0 %copy-start = (bf16[16,2,8,512]{3,2,1,0:T(8,128)(2,1)S(1)}, bf16[16,2,8,512]{3,2,1,0:T(8,128)(2,1)}, u32[]{:S(2)}) copy-start(bf16[16,2,8,512]{3,2,1,0:T(8,128)(2,1)} %volt_ref.1) | copy-start | bytes 786436
  1.6 0.7 %copy-start.2 = (s32[8]{0:T(128)S(1)}, s32[8]{0:T(128)}, u32[]{:S(2)}) copy-start(s32[8]{0:T(128)} %phase_ref.1) | copy-start | bytes 100
  26.0 1.0 %copy-start.1 = (bf16[2,256,256]{2,1,0:T(8,128)(2,1)S(1)}, bf16[2,256,256]{2,1,0:T(8,128)(2,1)}, u32[]{:S(2)}) copy-start(bf16[2,256,256]{2,1,0:T(8,128)(2,1)} %weight_ref.1) | copy-start | bytes 786436
  26.0 0.9 %copy-start.3 = (s32[4]{0:T(128)S(1)}, s32[4]{0:T(128)}, u32[]{:S(2)}) copy-start(s32[4]{0:T(128)} %length_ref.1) | copy-start | bytes 52

commit v2 on v1

v2 whole, which is shorter than its diff:
```python
import functools
import math

import jax
import jax.numpy as jnp
from jax import lax
from jax.experimental import pallas as pl
from jax.experimental.pallas import tpu as pltpu
from jax.sharding import PartitionSpec as P

PHASES = 1024
VMEM_BYTES = 32 * 1024 * 1024
IN_VMEM = pl.BlockSpec(memory_space=pltpu.VMEM)
IN_SMEM = pl.BlockSpec(memory_space=pltpu.SMEM)


def params():
    return pltpu.CompilerParams(vmem_limit_bytes=VMEM_BYTES)


def phasors(turns):
    quarter = PHASES // 4
    quadrant = (turns + quarter // 2) // quarter
    x = (turns - quadrant * quarter).astype(jnp.float32) * (2.0 * math.pi / PHASES)
    xx = x * x
    sine = x * (1.0 + xx * (-1.0 / 6 + xx * (1.0 / 120 + xx * (-1.0 / 5040 + xx * (1.0 / 362880)))))
    cosine = 1.0 + xx * (-0.5 + xx * (1.0 / 24 + xx * (-1.0 / 720 + xx * (1.0 / 40320))))
    odd = (quadrant % 2) == 1
    cos_out = jnp.where(odd, sine, cosine)
    sin_out = jnp.where(odd, cosine, sine)
    cos_out = jnp.where((quadrant == 1) | (quadrant == 2), -cos_out, cos_out)
    sin_out = jnp.where((quadrant == 2) | (quadrant == 3), -sin_out, sin_out)
    return cos_out, sin_out


def rotate_kernel(step_ref, volt_ref, kept_ref, given_ref):
    channels, _, rows, samples = volt_ref.shape
    me = lax.axis_index("chan")
    slot = lax.broadcasted_iota(jnp.int32, step_ref.shape, 1)
    cosine, sine = phasors((step_ref[...] * jnp.bitwise_xor(slot, me)) % PHASES)
    for k in range(channels):
        c = jnp.bitwise_xor(me, k)
        cos_c = cosine[:, k : k + 1]
        sin_c = sine[:, k : k + 1]
        real_in = volt_ref[c, 0].astype(jnp.float32)
        imag_in = volt_ref[c, 1].astype(jnp.float32)
        out_ref = given_ref if k % 2 else kept_ref
        out_ref[k // 2, 0] = (real_in * cos_c + imag_in * sin_c).astype(jnp.bfloat16)
        out_ref[k // 2, 1] = (imag_in * cos_c - real_in * sin_c).astype(jnp.bfloat16)


def rotate(voltages, phase_index):
    channels, parts, rows, samples = voltages.shape
    step = jnp.broadcast_to(phase_index[:, None], (rows, 128 * pl.cdiv(channels, 128)))
    half = jax.ShapeDtypeStruct((channels // 2, parts, rows, samples), jnp.bfloat16)
    return pl.pallas_call(
        rotate_kernel,
        out_shape=(half, half),
        in_specs=[IN_VMEM, IN_VMEM],
        out_specs=(IN_VMEM, IN_VMEM),
        compiler_params=params(),
    )(step, voltages)


def prepare_kernel(length_ref, weight_ref, window_ref, inverse_ref, stacked_ref):
    integs = length_ref.shape[0]
    stations, twice, width = stacked_ref.shape
    share, half = twice // 2, width // 2
    sample = lax.broadcasted_iota(jnp.int32, (1, window_ref.shape[1]), 1)
    window_ref[...] = jnp.zeros(window_ref.shape, jnp.float32)
    start = jnp.int32(0)
    for j in range(integs):
        end = start + length_ref[j]
        window_ref[j : j + 1] = jnp.where((sample >= start) & (sample < end), 1.0, 0.0)
        inverse_ref[j : j + 1] = 1.0 / jnp.full((1, inverse_ref.shape[1]), length_ref[j]).astype(
            jnp.float32
        )
        start = end
    rows = pl.ds(pl.multiple_of(lax.axis_index("stn") * share, share), share)
    for b in range(stations):
        w_real = weight_ref[0, rows, b * half : (b + 1) * half]
        w_imag = weight_ref[1, rows, b * half : (b + 1) * half]
        stacked_ref[b, :share, :half] = w_real
        stacked_ref[b, :share, half:] = -w_imag
        stacked_ref[b, share:, :half] = w_imag
        stacked_ref[b, share:, half:] = w_real


def prepare(int_lengths, beam_weights, stations, block, samples):
    share = beam_weights.shape[1] // stations
    return pl.pallas_call(
        prepare_kernel,
        out_shape=(
            jax.ShapeDtypeStruct((16, samples), jnp.float32),
            jax.ShapeDtypeStruct((int_lengths.shape[0], 128), jnp.float32),
            jax.ShapeDtypeStruct((stations, 2 * share, 2 * block), jnp.bfloat16),
        ),
        in_specs=[IN_SMEM, IN_VMEM],
        out_specs=(IN_VMEM, IN_VMEM, IN_VMEM),
        compiler_params=params(),
    )(int_lengths, beam_weights)


def dot_nt(a, b):
    return lax.dot_general(a, b, (((1,), (1,)), ((), ())), preferred_element_type=jnp.float32)


def finish_kernel(layout, window_ref, inverse_ref, stacked_ref, *refs):
    pieces, (vis_ref, power_ref, blocks_ref) = refs[:-3], refs[-3:]
    stations, parts, channels, rows, samples = blocks_ref.shape
    twice = parts * channels * rows
    half = twice // 2
    _, slots, integs = vis_ref.shape[:3]
    share = power_ref.shape[2]
    me = lax.axis_index("chan")
    station = lax.axis_index("stn")

    for piece_ref, (dy, offsets) in zip(pieces, layout):
        b = lax.rem(station + dy, stations)
        for i, offset in enumerate(offsets):
            source = jnp.bitwise_xor(me, offset)
            for part in range(parts):
                blocks_ref[b, part, source] = piece_ref[i, part]

    def block(b):
        return blocks_ref[b].astype(jnp.float32).reshape(twice, samples).astype(jnp.bfloat16)

    window = window_ref[...].astype(jnp.bfloat16)
    own = block(station)
    masked = jnp.concatenate([own * window[j : j + 1] for j in range(integs)], axis=0)
    for k in range(slots):
        other = own if k == 0 else block(lax.rem(station + k, stations))
        products = dot_nt(masked, other)
        for j in range(integs):
            prod = products[j * twice : (j + 1) * twice]
            inverse = inverse_ref[j : j + 1]
            real = prod[:half, :half] + prod[half:, half:]
            imag = prod[half:, :half] - prod[:half, half:]
            vis_ref[0, k, j, 0, 0] = (real * inverse).astype(jnp.bfloat16)
            vis_ref[0, k, j, 0, 1] = (imag * inverse).astype(jnp.bfloat16)

    beam = jnp.zeros((2 * share, samples), jnp.float32)
    for b in range(stations):
        beam = beam + jnp.dot(stacked_ref[b], block(b), preferred_element_type=jnp.float32)
    power = beam[:share] * beam[:share] + beam[share:] * beam[share:]
    high = power.astype(jnp.bfloat16)
    low = (power - high.astype(jnp.float32)).astype(jnp.bfloat16)
    summed = dot_nt(window, high) + dot_nt(window, low)
    for j in range(integs):
        power_ref[j] = summed[j : j + 1] * inverse_ref[j : j + 1, :share]


def finish(prepared, pieces, layout, slots, integs, share, block_shape):
    stations, parts, channels, rows, samples = block_shape
    half = channels * rows
    return pl.pallas_call(
        functools.partial(finish_kernel, layout),
        out_shape=(
            jax.ShapeDtypeStruct((1, slots, integs, 1, 2, half, half), jnp.bfloat16),
            jax.ShapeDtypeStruct((integs, 1, share), jnp.float32),
        ),
        in_specs=[IN_VMEM] * (len(prepared) + len(pieces)),
        out_specs=(IN_VMEM, IN_VMEM),
        scratch_shapes=[pltpu.VMEM(block_shape, jnp.bfloat16)],
        compiler_params=params(),
    )(*prepared, *pieces)


def exchanged(value, offset, dy):
    channels, stations = lax.axis_size("chan"), lax.axis_size("stn")
    if dy == 0:
        return lax.ppermute(value, "chan", [(c, c ^ offset) for c in range(channels)])
    pairs = [
        ((c ^ offset) * stations + (s + dy) % stations, c * stations + s)
        for c in range(channels)
        for s in range(stations)
    ]
    return lax.ppermute(value, ("chan", "stn"), pairs)


def local(voltages, phase_index, int_lengths, beam_weights):
    stations = lax.axis_size("stn")
    channels, parts, rows, samples = voltages.shape
    far = channels // 4
    kept, given = rotate(voltages, phase_index)
    prepared = prepare(int_lengths, beam_weights, stations, channels * rows, samples)

    both = jnp.stack([kept, exchanged(given, 1, 0)], axis=1)
    both = both.reshape(far, 2, 2, parts, rows, samples)
    arrived = [both[0]] + [exchanged(both[k], 4 * k, 0) for k in range(1, far)]

    def held(dx, ks):
        slabs = [arrived[k][dx] for k in ks]
        return slabs[0] if len(slabs) == 1 else jnp.concatenate(slabs, axis=0)

    every = tuple(range(far))
    pieces, layout = [], []
    for dy in range(1, stations):
        pieces.append(exchanged(held(1, (0,)), 2, dy))
        layout.append((1, dy, (0,)))
    pieces, arrived = lax.optimization_barrier((pieces, arrived))
    for dy in range(stations):
        for dx in range(2):
            ks = every[1:] if dx and dy else every
            piece = held(dx, ks)
            pieces.append(exchanged(piece, 2 * dx, dy) if dx or dy else piece)
            layout.append((dx, dy, ks))
    layout = [
        (dy, tuple(4 * k + 2 * dx + pair for k in ks for pair in range(2)))
        for dx, dy, ks in layout
    ]
    return finish(
        prepared,
        pieces,
        layout,
        stations // 2 + 1,
        int_lengths.shape[0],
        beam_weights.shape[1] // stations,
        (stations, parts, channels, rows, samples),
    )


def solution(mesh):
    return jax.shard_map(
        local,
        mesh=mesh,
        in_specs=(P(None, None, ("stn", "chan"), None), P(("stn", "chan")), P(), P()),
        out_specs=(P("stn", None, None, "chan", None, None, None), P(None, "chan", "stn")),
        check_vma=False,
    )
```

time: 29.5 us -> 25.7 us (0.87)
  blocking collectives: 23 us -> 0 us
  starting transfers between devices: 0 us -> 12.5 us
  waiting for transfers between devices: 0 us -> 8.06 us
  local copies, waits for them, and re-layouts: 2.53 us -> 1.71 us
  Pallas kernels: 3.04 us -> 2.55 us
    all_to_all x1 -> x0, blocking collectives: 23 us -> none  [local(): lax.all_to_all(sent.reshape(stations * channels, parts, rows, samples), (...]
    ppermute x0 -> x8, starting transfers between devices: none -> 12.5 us  [the longest x5 7.74 us: exchanged(): lax.ppermute(value, 'chan', [(c, c ^ offset) for c in range(channels)])]
    ppermute x0 -> x8, waiting for transfers between devices: none -> 8.06 us  [the longest x3 6.66 us: exchanged(): return lax.ppermute(value, ('chan', 'stn'), pairs)]
    unnamed x8 -> x6, local copies, waits for them, and re-layouts: 2.5 us -> 0.96 us
    broadcast_in_dim x0 -> x1, local copies, waits for them, and re-layouts: none -> 0.72 us  [rotate(): jnp.broadcast_to(phase_index[:, None], (rows, 128 * pl.cdiv(channels, 128)))]
    pallas_call x2 -> x3, Pallas kernels: 3.04 us -> 2.55 us  [the longest x1 1.76 us: finish(): pl.pallas_call(functools.partial(finish_kernel, layout), out_shape=(jax.S...]
  transfers between devices with their start and end apart: 0 -> 8, of which waited for: 0 -> 4; matrix products, arithmetic and copies ran while one was open for 0% -> 0% of each run, Pallas kernels for 0% -> 2%
where the time goes in v2:
time: 25.7 us; the launch traced here: 25.6 us
  starting transfers between devices  12.5 us (49%)
  waiting for transfers between devices  8.06 us (31%)
  Pallas kernels  2.55 us (10%)
  local copies, waits for them, and re-layouts  1.71 us (7%)
  between operations  0.7 us (3%)
    ppermute x5, starting transfers between devices, exchanged(): lax.ppermute(value, 'chan', [(c, c ^ offset) for c in range(channels)])  7.74 us
    ppermute x3, waiting for transfers between devices, exchanged(): return lax.ppermute(value, ('chan', 'stn'), pairs)  6.66 us
    ppermute x3, starting transfers between devices, exchanged(): return lax.ppermute(value, ('chan', 'stn'), pairs)  4.72 us
    pallas_call x1, Pallas kernels, finish(): pl.pallas_call(functools.partial(finish_kernel, layout), out_shape=(jax.S...  1.76 us
    ppermute x5, waiting for transfers between devices, exchanged(): lax.ppermute(value, 'chan', [(c, c ^ offset) for c in range(channels)])  1.4 us
    unnamed x6, local copies, waits for them, and re-layouts  0.96 us
    broadcast_in_dim x1, local copies, waits for them, and re-layouts, rotate(): jnp.broadcast_to(phase_index[:, None], (rows, 128 * pl.cdiv(channels, 128)))  0.72 us
    pallas_call x1, Pallas kernels, prepare(): pl.pallas_call(prepare_kernel, out_shape=(jax.ShapeDtypeStruct((16, sampl...  0.59 us
  transfers between devices with their start and end apart: 8, of which 4 were waited for; matrix products, arithmetic and copies ran while one was open for 0% of the time, Pallas kernels for 2%

profile of v2, /device:TPU:0, one launch (start us, length us, event | category | flops | bytes accessed | tf_op | source)
XLA Modules:
  0.0 25.6 jit_solution(9468239985033264461)
XLA Ops:
  0.6 0.7 %broadcast_in_dim.2.step_ref = s32[8,128]{1,0:T(8,128)S(1)} broadcast(s32[8]{0:T(128)} %param.5), dimensions={0} | broadcast | bytes 4128 | tf_op jit(solution)/shard_map/broadcast_in_dim | solution.py:54
  1.4 0.0 copy-start
  1.4 0.9 %copy-done = bf16[16,2,8,512]{3,2,1,0:T(8,128)(2,1)S(1)} copy-done((bf16[16,2,8,512]{3,2,1,0:T(8,128)(2,1)S(1)}, bf16[16,2,8,512]{3,2,1,0:T(8,128)(2,1)}, u32[]{:S(2)}) %copy-start) | copy-done | bytes 262168
  2.3 0.2 shard_map.60
  2.5 0.5 %collective-permute-start = (bf16[8,2,8,512]{3,2,1,0:T(8,128)(2,1)S(1)}, bf16[8,2,8,512]{3,2,1,0:T(8,128)(2,1)S(1)}, u32[]{:S(2)}, u32[]{:S(2)}) collective-permute-start(bf16[8,2,8,512]{3,2,1,0:T(8,128)(2,1)S(1)} %get-tuple-element.16), channel_id=1, source_target_pairs={{0,2},{2,0},{4,6},{6,4},{8,10},{10,8},{12,14},{14,12},{16,18},{18,... | collective-permute-start | bytes 393224 | tf_op jit(solution)/shard_map/ppermute | solution.py:172
  3.0 1.0 %collective-permute-done = bf16[8,2,8,512]{3,2,1,0:T(8,128)(2,1)S(1)} collective-permute-done((bf16[8,2,8,512]{3,2,1,0:T(8,128)(2,1)S(1)}, bf16[8,2,8,512]{3,2,1,0:T(8,128)(2,1)S(1)}, u32[]{:S(2)}, u32[]{:S(2)}) %collective-permute-start) | collective-permute-done | bytes 131104 | tf_op jit(solution)/shard_map/ppermute | solution.py:172
  4.0 5.0 %collective-permute-start.4 = (bf16[2,2,2,8,512]{4,3,2,1,0:T(8,128)(2,1)S(1)}, bf16[2,2,2,8,512]{4,3,2,1,0:T(8,128)(2,1)S(1)}, u32[]{:S(2)}, u32[]{:S(2)}) collective-permute-start(bf16[2,2,2,8,512]{4,3,2,1,0:T(8,128)(2,1)S(1)} %get-tuple-element.22), channel_id=1, source_target_pairs={{0,24},{2,26},{4,28},{6,30},{8,16},{10,18},{12,20},{14,22},{16,8},... | collective-permute-start | bytes 196616 | tf_op jit(solution)/shard_map/ppermute | solution.py:172
  9.1 0.0 collective-permute-start.2
  9.1 0.6 %collective-permute-start.3 = (bf16[2,2,2,8,512]{4,3,2,1,0:T(8,128)(2,1)S(1)}, bf16[2,2,2,8,512]{4,3,2,1,0:T(8,128)(2,1)S(1)}, u32[]{:S(2)}, u32[]{:S(2)}) collective-permute-start(bf16[2,2,2,8,512]{4,3,2,1,0:T(8,128)(2,1)S(1)} %get-tuple-element.25), channel_id=1, source_target_pairs={{0,16},{2,18},{4,20},{6,22},{8,24},{10,26},{12,28},{14,30},{16,0},... | collective-permute-start | bytes 196616 | tf_op jit(solution)/shard_map/ppermute | solution.py:172
  9.7 2.6 %collective-permute-start.1 = (bf16[2,2,8,512]{3,2,1,0:T(8,128)(2,1)S(1)}, bf16[2,2,8,512]{3,2,1,0:T(8,128)(2,1)S(1)}, u32[]{:S(2)}, u32[]{:S(2)}) collective-permute-start(bf16[2,2,8,512]{3,2,1,0:T(8,128)(2,1)S(1)} %maximum_bitcast_fusion), channel_id=1, source_target_pairs={{5,0},{4,1},{7,2},{6,3},{1,4},{0,5},{3,6},{2,7},{13,8},{12,9},{15,... | collective-permute-start | bytes 98312 | tf_op jit(solution)/shard_map/ppermute | solution.py:178
  12.3 2.2 %collective-permute-done.1.refs_0_ = bf16[2,2,8,512]{3,2,1,0:T(8,128)(2,1)S(1)} collective-permute-done((bf16[2,2,8,512]{3,2,1,0:T(8,128)(2,1)S(1)}, bf16[2,2,8,512]{3,2,1,0:T(8,128)(2,1)S(1)}, u32[]{:S(2)}, u32[]{:S(2)}) %collective-permute-start.1) | collective-permute-done | bytes 32800 | tf_op jit(solution)/shard_map/ppermute | solution.py:178
  14.5 0.0 collective-permute-done.4
  14.5 0.0 collective-permute-done.2
  14.5 0.4 %collective-permute-done.3 = bf16[2,2,2,8,512]{4,3,2,1,0:T(8,128)(2,1)S(1)} collective-permute-done((bf16[2,2,2,8,512]{4,3,2,1,0:T(8,128)(2,1)S(1)}, bf16[2,2,2,8,512]{4,3,2,1,0:T(8,128)(2,1)S(1)}, u32[]{:S(2)}, u32[]{:S(2)}) %collective-permute-start.3) | collective-permute-done | bytes 65568 | tf_op jit(solution)/shard_map/ppermute | solution.py:172
  15.0 0.0 copy-start.1
  15.0 1.6 %collective-permute-start.5 = (bf16[8,2,8,512]{3,2,1,0:T(8,128)(2,1)S(1)}, bf16[8,2,8,512]{3,2,1,0:T(8,128)(2,1)S(1)}, u32[]{:S(2)}, u32[]{:S(2)}) collective-permute-start(bf16[8,2,8,512]{3,2,1,0:T(8,128)(2,1)S(1)} %pad_maximum_fusion.1), channel_id=1, source_target_pairs={{0,4},{2,6},{4,0},{6,2},{8,12},{10,14},{12,8},{14,10},{16,20},{18,... | collective-permute-start | bytes 393224 | tf_op jit(solution)/shard_map/ppermute | solution.py:172
  16.6 0.0 copy-start.2
  16.6 1.6 %collective-permute-start.6 = (bf16[8,2,8,512]{3,2,1,0:T(8,128)(2,1)S(1)}, bf16[8,2,8,512]{3,2,1,0:T(8,128)(2,1)S(1)}, u32[]{:S(2)}, u32[]{:S(2)}) collective-permute-start(bf16[8,2,8,512]{3,2,1,0:T(8,128)(2,1)S(1)} %pad_maximum_fusion.refs_1_), channel_id=1, source_target_pairs={{1,0},{0,1},{3,2},{2,3},{5,4},{4,5},{7,6},{6,7},{9,8},{8,9},{11,10... | collective-permute-start | bytes 393224 | tf_op jit(solution)/shard_map/ppermute | solution.py:178
  18.2 0.5 %collective-permute-start.7 = (bf16[6,2,8,512]{3,2,1,0:T(8,128)(2,1)S(1)}, bf16[6,2,8,512]{3,2,1,0:T(8,128)(2,1)S(1)}, u32[]{:S(2)}, u32[]{:S(2)}) collective-permute-start(bf16[6,2,8,512]{3,2,1,0:T(8,128)(2,1)S(1)} %pad_maximum_fusion.2), channel_id=1, source_target_pairs={{5,0},{4,1},{7,2},{6,3},{1,4},{0,5},{3,6},{2,7},{13,8},{12,9},{15,... | collective-permute-start | bytes 294920 | tf_op jit(solution)/shard_map/ppermute | solution.py:178
  18.7 0.0 copy-done.1
  18.7 0.0 copy-done.2
  18.7 0.6 %shard_map.59 = (f32[16,512]{1,0:T(8,128)S(1)}, f32[4,128]{1,0:T(4,128)S(1)}, bf16[2,256,256]{2,1,0:T(8,128)(2,1)S(1)}) custom-call(s32[4]{0:T(128)S(1)} %copy-done.2, bf16[2,256,256]{2,1,0:T(8,128)(2,1)S(1)} %copy-done.1), custom_call_target="tpu_custom_call" | custom-call | tf_op jit(solution)/shard_map/pallas_call | solution.py:91
  19.3 4.4 %collective-permute-done.7.refs_4_ = bf16[6,2,8,512]{3,2,1,0:T(8,128)(2,1)S(1)} collective-permute-done((bf16[6,2,8,512]{3,2,1,0:T(8,128)(2,1)S(1)}, bf16[6,2,8,512]{3,2,1,0:T(8,128)(2,1)S(1)}, u32[]{:S(2)}, u32[]{:S(2)}) %collective-permute-start.7) | collective-permute-done | bytes 98336 | tf_op jit(solution)/shard_map/ppermute | solution.py:178
  23.8 0.0 collective-permute-done.5.refs_2_
  23.8 0.0 collective-permute-done.6.refs_3_
  23.8 1.8 %shard_map.61 = (bf16[1,2,4,1,2,128,128]{6,5,4,3,2,1,0:T(8,128)(2,1)}, f32[4,1,128]{2,1,0:T(1,128)}) custom-call(f32[16,512]{1,0:T(8,128)S(1)} %get-tuple-element.12.window_ref, f32[4,128]{1,0:T(4,128)S(1)} %get-tuple-element.13.inverse_ref, bf16[2,256,256]{2,1,0:T(8,128)(2,1)S(1)} %get-tuple-element.14.stacked_ref, ...), custom_call_target="tpu_custom_call" | custom-call | tf_op jit(solution)/shard_map/pallas_call | solution.py:156
  (7 shorter events, 0.1 us)
Async XLA Ops:
  1.4 0.9 %copy-start = (bf16[16,2,8,512]{3,2,1,0:T(8,128)(2,1)S(1)}, bf16[16,2,8,512]{3,2,1,0:T(8,128)(2,1)}, u32[]{:S(2)}) copy-start(bf16[16,2,8,512]{3,2,1,0:T(8,128)(2,1)} %volt_ref.1) | copy-start | bytes 786436
  2.5 1.5 %collective-permute-start = (bf16[8,2,8,512]{3,2,1,0:T(8,128)(2,1)S(1)}, bf16[8,2,8,512]{3,2,1,0:T(8,128)(2,1)S(1)}, u32[]{:S(2)}, u32[]{:S(2)}) collective-permute-start(bf16[8,2,8,512]{3,2,1,0:T(8,128)(2,1)S(1)} %get-tuple-element.16), channel_id=1, source_target_pairs={{0,2},{2,0},{4,6},{6,4},{8,10},{10,8},{12,14},{14,12},{16,18},{18,... | collective-permute-start | bytes 393224 | tf_op jit(solution)/shard_map/ppermute | solution.py:172
  4.0 10.5 %collective-permute-start.4 = (bf16[2,2,2,8,512]{4,3,2,1,0:T(8,128)(2,1)S(1)}, bf16[2,2,2,8,512]{4,3,2,1,0:T(8,128)(2,1)S(1)}, u32[]{:S(2)}, u32[]{:S(2)}) collective-permute-start(bf16[2,2,2,8,512]{4,3,2,1,0:T(8,128)(2,1)S(1)} %get-tuple-element.22), channel_id=1, source_target_pairs={{0,24},{2,26},{4,28},{6,30},{8,16},{10,18},{12,20},{14,22},{16,8},... | collective-permute-start | bytes 196616 | tf_op jit(solution)/shard_map/ppermute | solution.py:172
  9.1 5.5 %collective-permute-start.2 = (bf16[2,2,2,8,512]{4,3,2,1,0:T(8,128)(2,1)S(1)}, bf16[2,2,2,8,512]{4,3,2,1,0:T(8,128)(2,1)S(1)}, u32[]{:S(2)}, u32[]{:S(2)}) collective-permute-start(bf16[2,2,2,8,512]{4,3,2,1,0:T(8,128)(2,1)S(1)} %get-tuple-element.24), channel_id=1, source_target_pairs={{0,8},{2,10},{4,12},{6,14},{8,0},{10,2},{12,4},{14,6},{16,24},{18,... | collective-permute-start | bytes 196616 | tf_op jit(solution)/shard_map/ppermute | solution.py:172
  9.1 5.9 %collective-permute-start.3 = (bf16[2,2,2,8,512]{4,3,2,1,0:T(8,128)(2,1)S(1)}, bf16[2,2,2,8,512]{4,3,2,1,0:T(8,128)(2,1)S(1)}, u32[]{:S(2)}, u32[]{:S(2)}) collective-permute-start(bf16[2,2,2,8,512]{4,3,2,1,0:T(8,128)(2,1)S(1)} %get-tuple-element.25), channel_id=1, source_target_pairs={{0,16},{2,18},{4,20},{6,22},{8,24},{10,26},{12,28},{14,30},{16,0},... | collective-permute-start | bytes 196616 | tf_op jit(solution)/shard_map/ppermute | solution.py:172
  9.7 4.8 %collective-permute-start.1 = (bf16[2,2,8,512]{3,2,1,0:T(8,128)(2,1)S(1)}, bf16[2,2,8,512]{3,2,1,0:T(8,128)(2,1)S(1)}, u32[]{:S(2)}, u32[]{:S(2)}) collective-permute-start(bf16[2,2,8,512]{3,2,1,0:T(8,128)(2,1)S(1)} %maximum_bitcast_fusion), channel_id=1, source_target_pairs={{5,0},{4,1},{7,2},{6,3},{1,4},{0,5},{3,6},{2,7},{13,8},{12,9},{15,... | collective-permute-start | bytes 98312 | tf_op jit(solution)/shard_map/ppermute | solution.py:178
  15.0 3.7 %copy-start.1 = (bf16[2,256,256]{2,1,0:T(8,128)(2,1)S(1)}, bf16[2,256,256]{2,1,0:T(8,128)(2,1)}, u32[]{:S(2)}) copy-start(bf16[2,256,256]{2,1,0:T(8,128)(2,1)} %weight_ref.1) | copy-start | bytes 786436
  15.0 8.8 %collective-permute-start.5 = (bf16[8,2,8,512]{3,2,1,0:T(8,128)(2,1)S(1)}, bf16[8,2,8,512]{3,2,1,0:T(8,128)(2,1)S(1)}, u32[]{:S(2)}, u32[]{:S(2)}) collective-permute-start(bf16[8,2,8,512]{3,2,1,0:T(8,128)(2,1)S(1)} %pad_maximum_fusion.1), channel_id=1, source_target_pairs={{0,4},{2,6},{4,0},{6,2},{8,12},{10,14},{12,8},{14,10},{16,20},{18,... | collective-permute-start | bytes 393224 | tf_op jit(solution)/shard_map/ppermute | solution.py:172
  16.6 2.2 %copy-start.2 = (s32[4]{0:T(128)S(1)}, s32[4]{0:T(128)}, u32[]{:S(2)}) copy-start(s32[4]{0:T(128)} %length_ref.1) | copy-start | bytes 52
  16.6 7.2 %collective-permute-start.6 = (bf16[8,2,8,512]{3,2,1,0:T(8,128)(2,1)S(1)}, bf16[8,2,8,512]{3,2,1,0:T(8,128)(2,1)S(1)}, u32[]{:S(2)}, u32[]{:S(2)}) collective-permute-start(bf16[8,2,8,512]{3,2,1,0:T(8,128)(2,1)S(1)} %pad_maximum_fusion.refs_1_), channel_id=1, source_target_pairs={{1,0},{0,1},{3,2},{2,3},{5,4},{4,5},{7,6},{6,7},{9,8},{8,9},{11,10... | collective-permute-start | bytes 393224 | tf_op jit(solution)/shard_map/ppermute | solution.py:178
  18.2 5.6 %collective-permute-start.7 = (bf16[6,2,8,512]{3,2,1,0:T(8,128)(2,1)S(1)}, bf16[6,2,8,512]{3,2,1,0:T(8,128)(2,1)S(1)}, u32[]{:S(2)}, u32[]{:S(2)}) collective-permute-start(bf16[6,2,8,512]{3,2,1,0:T(8,128)(2,1)S(1)} %pad_maximum_fusion.2), channel_id=1, source_target_pairs={{5,0},{4,1},{7,2},{6,3},{1,4},{0,5},{3,6},{2,7},{13,8},{12,9},{15,... | collective-permute-start | bytes 294920 | tf_op jit(solution)/shard_map/ppermute | solution.py:178

commit v3 on v2

--- a/solution.py
+++ b/solution.py
@@ -42,8 +42,8 @@
         c = jnp.bitwise_xor(me, k)
         cos_c = cosine[:, k : k + 1]
         sin_c = sine[:, k : k + 1]
-        real_in = volt_ref[c, 0].astype(jnp.float32)
-        imag_in = volt_ref[c, 1].astype(jnp.float32)
+        real_in = volt_ref[c, 0]
+        imag_in = volt_ref[c, 1]
         out_ref = given_ref if k % 2 else kept_ref
         out_ref[k // 2, 0] = (real_in * cos_c + imag_in * sin_c).astype(jnp.bfloat16)
         out_ref[k // 2, 1] = (imag_in * cos_c - real_in * sin_c).astype(jnp.bfloat16)
@@ -59,7 +59,7 @@
         in_specs=[IN_VMEM, IN_VMEM],
         out_specs=(IN_VMEM, IN_VMEM),
         compiler_params=params(),
-    )(step, voltages)
+    )(step, voltages.astype(jnp.float32))
 
 
 def prepare_kernel(length_ref, weight_ref, window_ref, inverse_ref, stacked_ref):
@@ -105,65 +105,118 @@
     return lax.dot_general(a, b, (((1,), (1,)), ((), ())), preferred_element_type=jnp.float32)
 
 
-def finish_kernel(layout, window_ref, inverse_ref, stacked_ref, *refs):
-    pieces, (vis_ref, power_ref, blocks_ref) = refs[:-3], refs[-3:]
-    stations, parts, channels, rows, samples = blocks_ref.shape
-    twice = parts * channels * rows
-    half = twice // 2
-    _, slots, integs = vis_ref.shape[:3]
-    share = power_ref.shape[2]
+def assemble(pieces, layout, blocks_ref):
     me = lax.axis_index("chan")
-    station = lax.axis_index("stn")
-
-    for piece_ref, (dy, offsets) in zip(pieces, layout):
-        b = lax.rem(station + dy, stations)
+    for piece_ref, (block, offsets) in zip(pieces, layout):
         for i, offset in enumerate(offsets):
             source = jnp.bitwise_xor(me, offset)
-            for part in range(parts):
-                blocks_ref[b, part, source] = piece_ref[i, part]
-
-    def block(b):
-        return blocks_ref[b].astype(jnp.float32).reshape(twice, samples).astype(jnp.bfloat16)
-
+            for part in range(piece_ref.shape[1]):
+                blocks_ref[block, part, source] = piece_ref[i, part]
+
+
+def assembled(blocks_ref, block):
+    _, parts, channels, rows, samples = blocks_ref.shape
+    values = blocks_ref[block].astype(jnp.float32)
+    return values.reshape(parts * channels * rows, samples).astype(jnp.bfloat16)
+
+
+def correlate(own, other, window_ref, inverse_ref, vis_ref):
+    integs = vis_ref.shape[2]
+    twice = own.shape[0]
+    half = twice // 2
     window = window_ref[...].astype(jnp.bfloat16)
-    own = block(station)
     masked = jnp.concatenate([own * window[j : j + 1] for j in range(integs)], axis=0)
-    for k in range(slots):
-        other = own if k == 0 else block(lax.rem(station + k, stations))
-        products = dot_nt(masked, other)
+    products = dot_nt(masked, other)
+    for j in range(integs):
+        prod = products[j * twice : (j + 1) * twice]
+        inverse = inverse_ref[j : j + 1]
+        real = prod[:half, :half] + prod[half:, half:]
+        imag = prod[half:, :half] - prod[:half, half:]
+        vis_ref[0, 0, j, 0, 0] = (real * inverse).astype(jnp.bfloat16)
+        vis_ref[0, 0, j, 0, 1] = (imag * inverse).astype(jnp.bfloat16)
+
+
+def own_kernel(layout, window_ref, inverse_ref, stacked_ref, *refs):
+    pieces, (vis_ref, own_ref, beam_ref, blocks_ref) = refs[:-4], refs[-4:]
+    assemble(pieces, layout, blocks_ref)
+    own = assembled(blocks_ref, 0)
+    own_ref[...] = own
+    correlate(own, own, window_ref, inverse_ref, vis_ref)
+    beam_ref[...] = jnp.dot(
+        stacked_ref[lax.axis_index("stn")], own, preferred_element_type=jnp.float32
+    )
+
+
+def other_kernel(layout, window_ref, inverse_ref, stacked_ref, own_ref, beam_ref, *refs):
+    pieces, (vis_ref, power_ref, blocks_ref) = refs[:-4], refs[-3:]
+    others = blocks_ref.shape[0]
+    integs, _, share = power_ref.shape
+    station = lax.axis_index("stn")
+    slot = pl.program_id(0)
+
+    @pl.when(slot == 0)
+    def _():
+        assemble(pieces, layout, blocks_ref)
+
+    correlate(own_ref[...], assembled(blocks_ref, slot), window_ref, inverse_ref, vis_ref)
+
+    @pl.when(slot == pl.num_programs(0) - 1)
+    def _():
+        beam = beam_ref[...]
+        for b in range(others):
+            weights = stacked_ref[lax.rem(station + b + 1, others + 1)]
+            beam = beam + jnp.dot(
+                weights, assembled(blocks_ref, b), preferred_element_type=jnp.float32
+            )
+        power = beam[:share] * beam[:share] + beam[share:] * beam[share:]
+        high = power.astype(jnp.bfloat16)
+        low = (power - high.astype(jnp.float32)).astype(jnp.bfloat16)
+        window = window_ref[...].astype(jnp.bfloat16)
+        summed = dot_nt(window, high) + dot_nt(window, low)
         for j in range(integs):
-            prod = products[j * twice : (j + 1) * twice]
-            inverse = inverse_ref[j : j + 1]
-            real = prod[:half, :half] + prod[half:, half:]
-            imag = prod[half:, :half] - prod[:half, half:]
-            vis_ref[0, k, j, 0, 0] = (real * inverse).astype(jnp.bfloat16)
-            vis_ref[0, k, j, 0, 1] = (imag * inverse).astype(jnp.bfloat16)
-
-    beam = jnp.zeros((2 * share, samples), jnp.float32)
-    for b in range(stations):
-        beam = beam + jnp.dot(stacked_ref[b], block(b), preferred_element_type=jnp.float32)
-    power = beam[:share] * beam[:share] + beam[share:] * beam[share:]
-    high = power.astype(jnp.bfloat16)
-    low = (power - high.astype(jnp.float32)).astype(jnp.bfloat16)
-    summed = dot_nt(window, high) + dot_nt(window, low)
-    for j in range(integs):
-        power_ref[j] = summed[j : j + 1] * inverse_ref[j : j + 1, :share]
+            power_ref[j] = summed[j : j + 1] * inverse_ref[j : j + 1, :share]
 
 
 def finish(prepared, pieces, layout, slots, integs, share, block_shape):
     stations, parts, channels, rows, samples = block_shape
     half = channels * rows
+    vis = jax.ShapeDtypeStruct((1, slots, integs, 1, 2, half, half), jnp.bfloat16)
+    vis_block = (1, 1, integs, 1, 2, half, half)
+
+    near = [(p, (0, o)) for p, (dy, o) in zip(pieces, layout) if dy == 0]
+    vis, own, beam = pl.pallas_call(
+        functools.partial(own_kernel, [place for _, place in near]),
+        grid=(1,),
+        out_shape=(
+            vis,
+            jax.ShapeDtypeStruct((2 * half, samples), jnp.bfloat16),
+            jax.ShapeDtypeStruct((2 * share, samples), jnp.float32),
+        ),
+        in_specs=[IN_VMEM] * (len(prepared) + len(near)),
+        out_specs=(
+            pl.BlockSpec(vis_block, lambda k: (0, 0, 0, 0, 0, 0, 0)),
+            IN_VMEM,
+            IN_VMEM,
+        ),
+        scratch_shapes=[pltpu.VMEM((1, *block_shape[1:]), jnp.bfloat16)],
+        compiler_params=params(),
+    )(*prepared, *[p for p, _ in near])
+
+    away = [(p, (dy - 1, o)) for p, (dy, o) in zip(pieces, layout) if dy]
+    operands = (*prepared, own, beam, *[p for p, _ in away], vis)
     return pl.pallas_call(
-        functools.partial(finish_kernel, layout),
-        out_shape=(
-            jax.ShapeDtypeStruct((1, slots, integs, 1, 2, half, half), jnp.bfloat16),
-            jax.ShapeDtypeStruct((integs, 1, share), jnp.float32),
-        ),
-        in_specs=[IN_VMEM] * (len(prepared) + len(pieces)),
-        out_specs=(IN_VMEM, IN_VMEM),
-        scratch_shapes=[pltpu.VMEM(block_shape, jnp.bfloat16)],
-        compiler_params=params(),
-    )(*prepared, *pieces)
+        functools.partial(other_kernel, [place for _, place in away]),
+        grid=(slots - 1,),
+        out_shape=(vis, jax.ShapeDtypeStruct((integs, 1, share), jnp.float32)),
+        in_specs=[IN_VMEM] * (len(operands) - 1) + [pl.BlockSpec(memory_space=pl.ANY)],
+        out_specs=(
+            pl.BlockSpec(vis_block, lambda k: (0, k + 1, 0, 0, 0, 0, 0)),
+            IN_VMEM,
+        ),
+        scratch_shapes=[pltpu.VMEM((stations - 1, *block_shape[1:]), jnp.bfloat16)],
+        input_output_aliases={len(operands) - 1: 0},
+        compiler_params=params(),
+    )(*operands)
 
 
 def exchanged(value, offset, dy):
@@ -198,7 +251,9 @@
     for dy in range(1, stations):
         pieces.append(exchanged(held(1, (0,)), 2, dy))
         layout.append((1, dy, (0,)))
-    pieces, arrived = lax.optimization_barrier((pieces, arrived))
+    order = (0, far - 1, *range(1, far - 1))
+    pieces, waited = lax.optimization_barrier((pieces, [arrived[k] for k in order]))
+    arrived = [waited[order.index(k)] for k in every]
     for dy in range(stations):
         for dx in range(2):
             ks = every[1:] if dx and dy else every

time: 25.7 us -> 24.5 us (0.953)
  local copies, waits for them, and re-layouts: 1.71 us -> 0.11 us
  waiting for transfers between devices: 8.06 us -> 6.86 us
  other arithmetic: 0.08 us -> 1.09 us
  Pallas kernels: 2.55 us -> 3.37 us
  starting transfers between devices: 12.5 us -> 12.2 us
    ppermute x3, waiting for transfers between devices: 6.66 us -> 4.39 us  [exchanged(): return lax.ppermute(value, ('chan', 'stn'), pairs)]
    ppermute x5, waiting for transfers between devices: 1.4 us -> 2.47 us  [exchanged(): lax.ppermute(value, 'chan', [(c, c ^ offset) for c in range(channels)])]
    convert_element_type x0 -> x1, other arithmetic: none -> 1.01 us  [rotate(): voltages.astype(jnp.float32)]
    unnamed x6, local copies, waits for them, and re-layouts: 0.96 us -> 0.02 us
    pallas_call x1 -> x2, Pallas kernels: 1.76 us -> 2.61 us  [the longest x1 1.34 us: finish(): pl.pallas_call(functools.partial(other_kernel, [place for _, place in awa...]
    broadcast_in_dim x1, local copies, waits for them, and re-layouts: 0.72 us -> 0.07 us  [rotate(): jnp.broadcast_to(phase_index[:, None], (rows, 128 * pl.cdiv(channels, 128)))]
    ppermute x3, starting transfers between devices: 4.72 us -> 4.4 us  [exchanged(): return lax.ppermute(value, ('chan', 'stn'), pairs)]
  transfers between devices with their start and end apart: 8 -> 8, of which waited for: 4 -> 5; matrix products, arithmetic and copies ran while one was open for 0% -> 0% of each run, Pallas kernels for 2% -> 8%
where the time goes in v3:
time: 24.5 us; the launch traced here: 24.4 us
  starting transfers between devices  12.2 us (50%)
  waiting for transfers between devices  6.86 us (28%)
  Pallas kernels  3.37 us (14%)
  other arithmetic  1.09 us (4%)
  between operations  0.72 us (3%)
    ppermute x5, starting transfers between devices, exchanged(): lax.ppermute(value, 'chan', [(c, c ^ offset) for c in range(channels)])  7.83 us
    ppermute x3, starting transfers between devices, exchanged(): return lax.ppermute(value, ('chan', 'stn'), pairs)  4.4 us
    ppermute x3, waiting for transfers between devices, exchanged(): return lax.ppermute(value, ('chan', 'stn'), pairs)  4.39 us
    ppermute x5, waiting for transfers between devices, exchanged(): lax.ppermute(value, 'chan', [(c, c ^ offset) for c in range(channels)])  2.47 us
    pallas_call x1, Pallas kernels, finish(): pl.pallas_call(functools.partial(other_kernel, [place for _, place in awa...  1.34 us
    pallas_call x1, Pallas kernels, finish(): pl.pallas_call(functools.partial(own_kernel, [place for _, place in near]...  1.28 us
    convert_element_type x1, other arithmetic, rotate(): voltages.astype(jnp.float32)  1.01 us
    pallas_call x1, Pallas kernels, prepare(): pl.pallas_call(prepare_kernel, out_shape=(jax.ShapeDtypeStruct((16, sampl...  0.59 us
  transfers between devices with their start and end apart: 8, of which 5 were waited for; matrix products, arithmetic and copies ran while one was open for 0% of the time, Pallas kernels for 8%

profile of v3, /device:TPU:0, one launch (start us, length us, event | category | flops | bytes accessed | tf_op | source)
XLA Modules:
  0.0 24.4 jit_solution(2611326142829076057)
XLA Ops:
  0.6 0.0 copy-start.2
  0.6 1.0 %convert_element_type.3.volt_ref = f32[16,2,8,512]{3,2,1,0:T(8,128)S(1)} convert(bf16[16,2,8,512]{3,2,1,0:T(8,128)(2,1)} %param.4) | non-fusion elementwise | flops 131072 | bytes 786432 | tf_op jit(solution)/shard_map/convert_element_type | solution.py:62
  1.7 0.0 copy-done.2
  1.7 0.1 broadcast_in_dim.2.step_ref
  1.7 0.2 shard_map.60
  1.9 0.5 %collective-permute-start = (bf16[8,2,8,512]{3,2,1,0:T(8,128)(2,1)S(1)}, bf16[8,2,8,512]{3,2,1,0:T(8,128)(2,1)S(1)}, u32[]{:S(2)}, u32[]{:S(2)}) collective-permute-start(bf16[8,2,8,512]{3,2,1,0:T(8,128)(2,1)S(1)} %get-tuple-element.19), channel_id=1, source_target_pairs={{0,2},{2,0},{4,6},{6,4},{8,10},{10,8},{12,14},{14,12},{16,18},{18,... | collective-permute-start | bytes 393224 | tf_op jit(solution)/shard_map/ppermute | solution.py:225
  2.4 1.0 %collective-permute-done = bf16[8,2,8,512]{3,2,1,0:T(8,128)(2,1)S(1)} collective-permute-done((bf16[8,2,8,512]{3,2,1,0:T(8,128)(2,1)S(1)}, bf16[8,2,8,512]{3,2,1,0:T(8,128)(2,1)S(1)}, u32[]{:S(2)}, u32[]{:S(2)}) %collective-permute-start) | collective-permute-done | bytes 131104 | tf_op jit(solution)/shard_map/ppermute | solution.py:225
  3.4 4.0 %collective-permute-start.4 = (bf16[2,2,2,8,512]{4,3,2,1,0:T(8,128)(2,1)S(1)}, bf16[2,2,2,8,512]{4,3,2,1,0:T(8,128)(2,1)S(1)}, u32[]{:S(2)}, u32[]{:S(2)}) collective-permute-start(bf16[2,2,2,8,512]{4,3,2,1,0:T(8,128)(2,1)S(1)} %get-tuple-element.28), channel_id=1, source_target_pairs={{0,16},{2,18},{4,20},{6,22},{8,24},{10,26},{12,28},{14,30},{16,0},... | collective-permute-start | bytes 196616 | tf_op jit(solution)/shard_map/ppermute | solution.py:225
  7.5 1.3 %collective-permute-start.2 = (bf16[2,2,2,8,512]{4,3,2,1,0:T(8,128)(2,1)S(1)}, bf16[2,2,2,8,512]{4,3,2,1,0:T(8,128)(2,1)S(1)}, u32[]{:S(2)}, u32[]{:S(2)}) collective-permute-start(bf16[2,2,2,8,512]{4,3,2,1,0:T(8,128)(2,1)S(1)} %get-tuple-element.30), channel_id=1, source_target_pairs={{0,24},{2,26},{4,28},{6,30},{8,16},{10,18},{12,20},{14,22},{16,8},... | collective-permute-start | bytes 196616 | tf_op jit(solution)/shard_map/ppermute | solution.py:225
  8.8 0.2 collective-permute-start.3
  9.0 2.4 %collective-permute-start.1 = (bf16[2,2,8,512]{3,2,1,0:T(8,128)(2,1)S(1)}, bf16[2,2,8,512]{3,2,1,0:T(8,128)(2,1)S(1)}, u32[]{:S(2)}, u32[]{:S(2)}) collective-permute-start(bf16[2,2,8,512]{3,2,1,0:T(8,128)(2,1)S(1)} %maximum_bitcast_fusion), channel_id=1, source_target_pairs={{5,0},{4,1},{7,2},{6,3},{1,4},{0,5},{3,6},{2,7},{13,8},{12,9},{15,... | collective-permute-start | bytes 98312 | tf_op jit(solution)/shard_map/ppermute | solution.py:231
  11.5 2.4 %collective-permute-done.1.refs_0_ = bf16[2,2,8,512]{3,2,1,0:T(8,128)(2,1)S(1)} collective-permute-done((bf16[2,2,8,512]{3,2,1,0:T(8,128)(2,1)S(1)}, bf16[2,2,8,512]{3,2,1,0:T(8,128)(2,1)S(1)}, u32[]{:S(2)}, u32[]{:S(2)}) %collective-permute-start.1) | collective-permute-done | bytes 32800 | tf_op jit(solution)/shard_map/ppermute | solution.py:231
  13.8 0.0 collective-permute-done.4
  13.9 0.0 collective-permute-done.2
  13.9 0.2 collective-permute-done.3
  14.1 0.0 copy-start
  14.1 1.7 %collective-permute-start.5 = (bf16[8,2,8,512]{3,2,1,0:T(8,128)(2,1)S(1)}, bf16[8,2,8,512]{3,2,1,0:T(8,128)(2,1)S(1)}, u32[]{:S(2)}, u32[]{:S(2)}) collective-permute-start(bf16[8,2,8,512]{3,2,1,0:T(8,128)(2,1)S(1)} %pad_maximum_fusion.1), channel_id=1, source_target_pairs={{0,4},{2,6},{4,0},{6,2},{8,12},{10,14},{12,8},{14,10},{16,20},{18,... | collective-permute-start | bytes 393224 | tf_op jit(solution)/shard_map/ppermute | solution.py:225
  15.9 0.0 copy-start.1
  15.9 1.6 %collective-permute-start.6 = (bf16[8,2,8,512]{3,2,1,0:T(8,128)(2,1)S(1)}, bf16[8,2,8,512]{3,2,1,0:T(8,128)(2,1)S(1)}, u32[]{:S(2)}, u32[]{:S(2)}) collective-permute-start(bf16[8,2,8,512]{3,2,1,0:T(8,128)(2,1)S(1)} %pad_maximum_fusion.refs_0_), channel_id=1, source_target_pairs={{1,0},{0,1},{3,2},{2,3},{5,4},{4,5},{7,6},{6,7},{9,8},{8,9},{11,10... | collective-permute-start | bytes 393224 | tf_op jit(solution)/shard_map/ppermute | solution.py:231
  17.5 0.4 %collective-permute-start.7 = (bf16[6,2,8,512]{3,2,1,0:T(8,128)(2,1)S(1)}, bf16[6,2,8,512]{3,2,1,0:T(8,128)(2,1)S(1)}, u32[]{:S(2)}, u32[]{:S(2)}) collective-permute-start(bf16[6,2,8,512]{3,2,1,0:T(8,128)(2,1)S(1)} %pad_maximum_fusion.2), channel_id=1, source_target_pairs={{5,0},{4,1},{7,2},{6,3},{1,4},{0,5},{3,6},{2,7},{13,8},{12,9},{15,... | collective-permute-start | bytes 294920 | tf_op jit(solution)/shard_map/ppermute | solution.py:231
  17.8 0.0 copy-done
  17.8 0.0 copy-done.1
  17.8 0.6 %shard_map.59 = (f32[16,512]{1,0:T(8,128)S(1)}, f32[4,128]{1,0:T(4,128)S(1)}, bf16[2,256,256]{2,1,0:T(8,128)(2,1)S(1)}) custom-call(s32[4]{0:T(128)S(1)} %copy-done.1, bf16[2,256,256]{2,1,0:T(8,128)(2,1)S(1)} %copy-done), custom_call_target="tpu_custom_call" | custom-call | tf_op jit(solution)/shard_map/pallas_call | solution.py:91
  18.4 1.3 %collective-permute-done.5.refs_1_ = bf16[8,2,8,512]{3,2,1,0:T(8,128)(2,1)S(1)} collective-permute-done((bf16[8,2,8,512]{3,2,1,0:T(8,128)(2,1)S(1)}, bf16[8,2,8,512]{3,2,1,0:T(8,128)(2,1)S(1)}, u32[]{:S(2)}, u32[]{:S(2)}) %collective-permute-start.5) | collective-permute-done | bytes 131104 | tf_op jit(solution)/shard_map/ppermute | solution.py:225
  19.7 1.3 %shard_map.61 = (bf16[1,2,4,1,2,128,128]{6,5,4,3,2,1,0:T(8,128)(2,1)}, bf16[256,512]{1,0:T(8,128)(2,1)S(1)}, f32[256,512]{1,0:T(8,128)S(1)}) custom-call(f32[16,512]{1,0:T(8,128)S(1)} %get-tuple-element.15.window_ref, f32[4,128]{1,0:T(4,128)S(1)} %get-tuple-element.16.inverse_ref, bf16[2,256,256]{2,1,0:T(8,128)(2,1)S(1)} %get-tuple-element.17.stacked_ref, ...), custom_call_target="tpu_custom_call" | custom-call | tf_op jit(solution)/shard_map/pallas_call | solution.py:187
  21.0 2.0 %collective-permute-done.7.refs_2_ = bf16[6,2,8,512]{3,2,1,0:T(8,128)(2,1)S(1)} collective-permute-done((bf16[6,2,8,512]{3,2,1,0:T(8,128)(2,1)S(1)}, bf16[6,2,8,512]{3,2,1,0:T(8,128)(2,1)S(1)}, u32[]{:S(2)}, u32[]{:S(2)}) %collective-permute-start.7) | collective-permute-done | bytes 98336 | tf_op jit(solution)/shard_map/ppermute | solution.py:231
  23.0 0.0 collective-permute-done.6.refs_1_
  23.1 1.3 %shard_map.62 = (bf16[1,2,4,1,2,128,128]{6,5,4,3,2,1,0:T(8,128)(2,1)}, f32[4,1,128]{2,1,0:T(1,128)}) custom-call(f32[16,512]{1,0:T(8,128)S(1)} %get-tuple-element.15.window_ref, f32[4,128]{1,0:T(4,128)S(1)} %get-tuple-element.16.inverse_ref, bf16[2,256,256]{2,1,0:T(8,128)(2,1)S(1)} %get-tuple-element.17.stacked_ref, ...), custom_call_target="tpu_custom_call", output_to_operand_aliasing={{0}: (8, {})} | custom-call | tf_op jit(solution)/shard_map/pallas_call | solution.py:207
  (7 shorter events, 0.1 us)
Async XLA Ops:
  0.6 1.0 %copy-start.2 = (s32[8]{0:T(128)S(1)}, s32[8]{0:T(128)}, u32[]{:S(2)}) copy-start(s32[8]{0:T(128)} %param.5) | copy-start | bytes 100
  1.9 1.5 %collective-permute-start = (bf16[8,2,8,512]{3,2,1,0:T(8,128)(2,1)S(1)}, bf16[8,2,8,512]{3,2,1,0:T(8,128)(2,1)S(1)}, u32[]{:S(2)}, u32[]{:S(2)}) collective-permute-start(bf16[8,2,8,512]{3,2,1,0:T(8,128)(2,1)S(1)} %get-tuple-element.19), channel_id=1, source_target_pairs={{0,2},{2,0},{4,6},{6,4},{8,10},{10,8},{12,14},{14,12},{16,18},{18,... | collective-permute-start | bytes 393224 | tf_op jit(solution)/shard_map/ppermute | solution.py:225
  3.4 10.4 %collective-permute-start.4 = (bf16[2,2,2,8,512]{4,3,2,1,0:T(8,128)(2,1)S(1)}, bf16[2,2,2,8,512]{4,3,2,1,0:T(8,128)(2,1)S(1)}, u32[]{:S(2)}, u32[]{:S(2)}) collective-permute-start(bf16[2,2,2,8,512]{4,3,2,1,0:T(8,128)(2,1)S(1)} %get-tuple-element.28), channel_id=1, source_target_pairs={{0,16},{2,18},{4,20},{6,22},{8,24},{10,26},{12,28},{14,30},{16,0},... | collective-permute-start | bytes 196616 | tf_op jit(solution)/shard_map/ppermute | solution.py:225
  7.5 6.4 %collective-permute-start.2 = (bf16[2,2,2,8,512]{4,3,2,1,0:T(8,128)(2,1)S(1)}, bf16[2,2,2,8,512]{4,3,2,1,0:T(8,128)(2,1)S(1)}, u32[]{:S(2)}, u32[]{:S(2)}) collective-permute-start(bf16[2,2,2,8,512]{4,3,2,1,0:T(8,128)(2,1)S(1)} %get-tuple-element.30), channel_id=1, source_target_pairs={{0,24},{2,26},{4,28},{6,30},{8,16},{10,18},{12,20},{14,22},{16,8},... | collective-permute-start | bytes 196616 | tf_op jit(solution)/shard_map/ppermute | solution.py:225
  8.8 5.2 %collective-permute-start.3 = (bf16[2,2,2,8,512]{4,3,2,1,0:T(8,128)(2,1)S(1)}, bf16[2,2,2,8,512]{4,3,2,1,0:T(8,128)(2,1)S(1)}, u32[]{:S(2)}, u32[]{:S(2)}) collective-permute-start(bf16[2,2,2,8,512]{4,3,2,1,0:T(8,128)(2,1)S(1)} %get-tuple-element.31), channel_id=1, source_target_pairs={{0,8},{2,10},{4,12},{6,14},{8,0},{10,2},{12,4},{14,6},{16,24},{18,... | collective-permute-start | bytes 196616 | tf_op jit(solution)/shard_map/ppermute | solution.py:225
  9.0 4.8 %collective-permute-start.1 = (bf16[2,2,8,512]{3,2,1,0:T(8,128)(2,1)S(1)}, bf16[2,2,8,512]{3,2,1,0:T(8,128)(2,1)S(1)}, u32[]{:S(2)}, u32[]{:S(2)}) collective-permute-start(bf16[2,2,8,512]{3,2,1,0:T(8,128)(2,1)S(1)} %maximum_bitcast_fusion), channel_id=1, source_target_pairs={{5,0},{4,1},{7,2},{6,3},{1,4},{0,5},{3,6},{2,7},{13,8},{12,9},{15,... | collective-permute-start | bytes 98312 | tf_op jit(solution)/shard_map/ppermute | solution.py:231
  14.1 3.7 %copy-start = (bf16[2,256,256]{2,1,0:T(8,128)(2,1)S(1)}, bf16[2,256,256]{2,1,0:T(8,128)(2,1)}, u32[]{:S(2)}) copy-start(bf16[2,256,256]{2,1,0:T(8,128)(2,1)} %weight_ref.1) | copy-start | bytes 786436
  14.1 5.6 %collective-permute-start.5 = (bf16[8,2,8,512]{3,2,1,0:T(8,128)(2,1)S(1)}, bf16[8,2,8,512]{3,2,1,0:T(8,128)(2,1)S(1)}, u32[]{:S(2)}, u32[]{:S(2)}) collective-permute-start(bf16[8,2,8,512]{3,2,1,0:T(8,128)(2,1)S(1)} %pad_maximum_fusion.1), channel_id=1, source_target_pairs={{0,4},{2,6},{4,0},{6,2},{8,12},{10,14},{12,8},{14,10},{16,20},{18,... | collective-permute-start | bytes 393224 | tf_op jit(solution)/shard_map/ppermute | solution.py:225
  15.9 2.0 %copy-start.1 = (s32[4]{0:T(128)S(1)}, s32[4]{0:T(128)}, u32[]{:S(2)}) copy-start(s32[4]{0:T(128)} %length_ref.1) | copy-start | bytes 52
  15.9 7.2 %collective-permute-start.6 = (bf16[8,2,8,512]{3,2,1,0:T(8,128)(2,1)S(1)}, bf16[8,2,8,512]{3,2,1,0:T(8,128)(2,1)S(1)}, u32[]{:S(2)}, u32[]{:S(2)}) collective-permute-start(bf16[8,2,8,512]{3,2,1,0:T(8,128)(2,1)S(1)} %pad_maximum_fusion.refs_0_), channel_id=1, source_target_pairs={{1,0},{0,1},{3,2},{2,3},{5,4},{4,5},{7,6},{6,7},{9,8},{8,9},{11,10... | collective-permute-start | bytes 393224 | tf_op jit(solution)/shard_map/ppermute | solution.py:231
  17.5 5.6 %collective-permute-start.7 = (bf16[6,2,8,512]{3,2,1,0:T(8,128)(2,1)S(1)}, bf16[6,2,8,512]{3,2,1,0:T(8,128)(2,1)S(1)}, u32[]{:S(2)}, u32[]{:S(2)}) collective-permute-start(bf16[6,2,8,512]{3,2,1,0:T(8,128)(2,1)S(1)} %pad_maximum_fusion.2), channel_id=1, source_target_pairs={{5,0},{4,1},{7,2},{6,3},{1,4},{0,5},{3,6},{2,7},{13,8},{12,9},{15,... | collective-permute-start | bytes 294920 | tf_op jit(solution)/shard_map/ppermute | solution.py:231

commit v4 on v3

--- a/solution.py
+++ b/solution.py
@@ -33,33 +33,31 @@
     return cos_out, sin_out
 
 
-def rotate_kernel(step_ref, volt_ref, kept_ref, given_ref):
-    channels, _, rows, samples = volt_ref.shape
+def rotate_kernel(step_ref, volt_ref, out_ref):
+    slots = out_ref.shape[0]
     me = lax.axis_index("chan")
-    slot = lax.broadcasted_iota(jnp.int32, step_ref.shape, 1)
+    slot = 2 * lax.broadcasted_iota(jnp.int32, step_ref.shape, 1)
     cosine, sine = phasors((step_ref[...] * jnp.bitwise_xor(slot, me)) % PHASES)
-    for k in range(channels):
-        c = jnp.bitwise_xor(me, k)
-        cos_c = cosine[:, k : k + 1]
-        sin_c = sine[:, k : k + 1]
-        real_in = volt_ref[c, 0]
-        imag_in = volt_ref[c, 1]
-        out_ref = given_ref if k % 2 else kept_ref
-        out_ref[k // 2, 0] = (real_in * cos_c + imag_in * sin_c).astype(jnp.bfloat16)
-        out_ref[k // 2, 1] = (imag_in * cos_c - real_in * sin_c).astype(jnp.bfloat16)
+    for i in range(slots):
+        c = jnp.bitwise_xor(me, 2 * i)
+        cos_c = cosine[:, i : i + 1]
+        sin_c = sine[:, i : i + 1]
+        real_in = volt_ref[c, 0].astype(jnp.float32)
+        imag_in = volt_ref[c, 1].astype(jnp.float32)
+        out_ref[i, 0] = (real_in * cos_c + imag_in * sin_c).astype(jnp.bfloat16)
+        out_ref[i, 1] = (imag_in * cos_c - real_in * sin_c).astype(jnp.bfloat16)
 
 
 def rotate(voltages, phase_index):
     channels, parts, rows, samples = voltages.shape
     step = jnp.broadcast_to(phase_index[:, None], (rows, 128 * pl.cdiv(channels, 128)))
-    half = jax.ShapeDtypeStruct((channels // 2, parts, rows, samples), jnp.bfloat16)
     return pl.pallas_call(
         rotate_kernel,
-        out_shape=(half, half),
+        out_shape=jax.ShapeDtypeStruct((channels // 2, parts, rows, samples), jnp.bfloat16),
         in_specs=[IN_VMEM, IN_VMEM],
-        out_specs=(IN_VMEM, IN_VMEM),
-        compiler_params=params(),
-    )(step, voltages.astype(jnp.float32))
+        out_specs=IN_VMEM,
+        compiler_params=params(),
+    )(step, voltages)
 
 
 def prepare_kernel(length_ref, weight_ref, window_ref, inverse_ref, stacked_ref):
@@ -235,10 +233,12 @@
     stations = lax.axis_size("stn")
     channels, parts, rows, samples = voltages.shape
     far = channels // 4
-    kept, given = rotate(voltages, phase_index)
+    pair_phase, pair_voltages = exchanged(phase_index, 1, 0), exchanged(voltages, 1, 0)
+    kept = rotate(voltages.astype(jnp.float32), phase_index)
+    swapped = rotate(pair_voltages, pair_phase)
     prepared = prepare(int_lengths, beam_weights, stations, channels * rows, samples)
 
-    both = jnp.stack([kept, exchanged(given, 1, 0)], axis=1)
+    both = jnp.stack([kept, swapped], axis=1)
     both = both.reshape(far, 2, 2, parts, rows, samples)
     arrived = [both[0]] + [exchanged(both[k], 4 * k, 0) for k in range(1, far)]
 

time: 24.5 us -> 23.9 us (0.976)
  waiting for transfers between devices: 6.86 us -> 5.92 us
    ppermute x5 -> x6, waiting for transfers between devices: 2.47 us -> 1.56 us  [exchanged(): lax.ppermute(value, 'chan', [(c, c ^ offset) for c in range(channels)])]
    ppermute x5 -> x6, starting transfers between devices: 7.83 us -> 7.96 us  [exchanged(): lax.ppermute(value, 'chan', [(c, c ^ offset) for c in range(channels)])]
  transfers between devices with their start and end apart: 8 -> 9, of which waited for: 5 -> 5; matrix products, arithmetic and copies ran while one was open for 0% -> 5% of each run, Pallas kernels for 8% -> 8%
where the time goes in v4:
time: 23.9 us; the launch traced here: 23.8 us
  starting transfers between devices  12.3 us (51%)
  waiting for transfers between devices  5.92 us (25%)
  Pallas kernels  3.5 us (15%)
  other arithmetic  1.08 us (5%)
  between operations  0.74 us (3%)
    ppermute x6, starting transfers between devices, exchanged(): lax.ppermute(value, 'chan', [(c, c ^ offset) for c in range(channels)])  7.96 us
    ppermute x3, starting transfers between devices, exchanged(): return lax.ppermute(value, ('chan', 'stn'), pairs)  4.38 us
    ppermute x3, waiting for transfers between devices, exchanged(): return lax.ppermute(value, ('chan', 'stn'), pairs)  4.36 us
    ppermute x6, waiting for transfers between devices, exchanged(): lax.ppermute(value, 'chan', [(c, c ^ offset) for c in range(channels)])  1.56 us
    pallas_call x1, Pallas kernels, finish(): pl.pallas_call(functools.partial(other_kernel, [place for _, place in awa...  1.34 us
    pallas_call x1, Pallas kernels, finish(): pl.pallas_call(functools.partial(own_kernel, [place for _, place in near]...  1.28 us
    convert_element_type x1, other arithmetic, local(): kept = rotate(voltages.astype(jnp.float32), phase_index)  1 us
    pallas_call x1, Pallas kernels, prepare(): pl.pallas_call(prepare_kernel, out_shape=(jax.ShapeDtypeStruct((16, sampl...  0.59 us
  transfers between devices with their start and end apart: 9, of which 5 were waited for; matrix products, arithmetic and copies ran while one was open for 5% of the time, Pallas kernels for 8%

profile of v4, /device:TPU:0, one launch (start us, length us, event | category | flops | bytes accessed | tf_op | source)
XLA Modules:
  0.0 23.8 jit_solution(10268114380738276096)
XLA Ops:
  0.6 0.0 copy-start.2
  0.6 0.5 %collective-permute-start.1 = (bf16[16,2,8,512]{3,2,1,0:T(8,128)(2,1)}, bf16[16,2,8,512]{3,2,1,0:T(8,128)(2,1)S(1)}, u32[]{:S(2)}, u32[]{:S(2)}) collective-permute-start(bf16[16,2,8,512]{3,2,1,0:T(8,128)(2,1)} %param.4), channel_id=1, source_target_pairs={{0,2},{2,0},{4,6},{6,4},{8,10},{10,8},{12,14},{14,12},{16,18},{18,... | collective-permute-start | bytes 786440 | tf_op jit(solution)/shard_map/ppermute | solution.py:223
  1.2 0.1 collective-permute-start
  1.2 1.0 %convert_element_type.3.volt_ref = f32[16,2,8,512]{3,2,1,0:T(8,128)S(1)} convert(bf16[16,2,8,512]{3,2,1,0:T(8,128)(2,1)} %param.4) | non-fusion elementwise | flops 131072 | bytes 786432 | tf_op jit(solution)/shard_map/convert_element_type | solution.py:237
  2.2 0.0 copy-done.2
  2.3 0.1 broadcast_in_dim.4.step_ref
  2.3 0.1 shard_map.60
  2.5 0.1 collective-permute-done
  2.5 0.0 collective-permute-done.1.volt_ref
  2.5 0.1 broadcast_in_dim.5.step_ref
  2.6 0.1 shard_map.61
  2.8 4.0 %collective-permute-start.5 = (bf16[2,2,2,8,512]{4,3,2,1,0:T(8,128)(2,1)S(1)}, bf16[2,2,2,8,512]{4,3,2,1,0:T(8,128)(2,1)S(1)}, u32[]{:S(2)}, u32[]{:S(2)}) collective-permute-start(bf16[2,2,2,8,512]{4,3,2,1,0:T(8,128)(2,1)S(1)} %get-tuple-element.24), channel_id=1, source_target_pairs={{0,16},{2,18},{4,20},{6,22},{8,24},{10,26},{12,28},{14,30},{16,0},... | collective-permute-start | bytes 196616 | tf_op jit(solution)/shard_map/ppermute | solution.py:223
  6.8 1.3 %collective-permute-start.3 = (bf16[2,2,2,8,512]{4,3,2,1,0:T(8,128)(2,1)S(1)}, bf16[2,2,2,8,512]{4,3,2,1,0:T(8,128)(2,1)S(1)}, u32[]{:S(2)}, u32[]{:S(2)}) collective-permute-start(bf16[2,2,2,8,512]{4,3,2,1,0:T(8,128)(2,1)S(1)} %get-tuple-element.26), channel_id=1, source_target_pairs={{0,24},{2,26},{4,28},{6,30},{8,16},{10,18},{12,20},{14,22},{16,8},... | collective-permute-start | bytes 196616 | tf_op jit(solution)/shard_map/ppermute | solution.py:223
  8.2 0.2 collective-permute-start.4
  8.4 2.4 %collective-permute-start.2 = (bf16[2,2,8,512]{3,2,1,0:T(8,128)(2,1)S(1)}, bf16[2,2,8,512]{3,2,1,0:T(8,128)(2,1)S(1)}, u32[]{:S(2)}, u32[]{:S(2)}) collective-permute-start(bf16[2,2,8,512]{3,2,1,0:T(8,128)(2,1)S(1)} %maximum_bitcast_fusion), channel_id=1, source_target_pairs={{5,0},{4,1},{7,2},{6,3},{1,4},{0,5},{3,6},{2,7},{13,8},{12,9},{15,... | collective-permute-start | bytes 98312 | tf_op jit(solution)/shard_map/ppermute | solution.py:229
  10.9 2.4 %collective-permute-done.2.refs_0_ = bf16[2,2,8,512]{3,2,1,0:T(8,128)(2,1)S(1)} collective-permute-done((bf16[2,2,8,512]{3,2,1,0:T(8,128)(2,1)S(1)}, bf16[2,2,8,512]{3,2,1,0:T(8,128)(2,1)S(1)}, u32[]{:S(2)}, u32[]{:S(2)}) %collective-permute-start.2) | collective-permute-done | bytes 32800 | tf_op jit(solution)/shard_map/ppermute | solution.py:229
  13.2 0.0 collective-permute-done.5
  13.2 0.0 collective-permute-done.3
  13.2 0.1 collective-permute-done.4
  13.4 0.0 copy-start
  13.4 1.7 %collective-permute-start.6 = (bf16[8,2,8,512]{3,2,1,0:T(8,128)(2,1)S(1)}, bf16[8,2,8,512]{3,2,1,0:T(8,128)(2,1)S(1)}, u32[]{:S(2)}, u32[]{:S(2)}) collective-permute-start(bf16[8,2,8,512]{3,2,1,0:T(8,128)(2,1)S(1)} %pad_maximum_fusion.1), channel_id=1, source_target_pairs={{0,4},{2,6},{4,0},{6,2},{8,12},{10,14},{12,8},{14,10},{16,20},{18,... | collective-permute-start | bytes 393224 | tf_op jit(solution)/shard_map/ppermute | solution.py:223
  15.2 0.0 copy-start.1
  15.2 1.6 %collective-permute-start.7 = (bf16[8,2,8,512]{3,2,1,0:T(8,128)(2,1)S(1)}, bf16[8,2,8,512]{3,2,1,0:T(8,128)(2,1)S(1)}, u32[]{:S(2)}, u32[]{:S(2)}) collective-permute-start(bf16[8,2,8,512]{3,2,1,0:T(8,128)(2,1)S(1)} %pad_maximum_fusion.refs_0_), channel_id=1, source_target_pairs={{1,0},{0,1},{3,2},{2,3},{5,4},{4,5},{7,6},{6,7},{9,8},{8,9},{11,10... | collective-permute-start | bytes 393224 | tf_op jit(solution)/shard_map/ppermute | solution.py:229
  16.8 0.4 %collective-permute-start.8 = (bf16[6,2,8,512]{3,2,1,0:T(8,128)(2,1)S(1)}, bf16[6,2,8,512]{3,2,1,0:T(8,128)(2,1)S(1)}, u32[]{:S(2)}, u32[]{:S(2)}) collective-permute-start(bf16[6,2,8,512]{3,2,1,0:T(8,128)(2,1)S(1)} %pad_maximum_fusion.2), channel_id=1, source_target_pairs={{5,0},{4,1},{7,2},{6,3},{1,4},{0,5},{3,6},{2,7},{13,8},{12,9},{15,... | collective-permute-start | bytes 294920 | tf_op jit(solution)/shard_map/ppermute | solution.py:229
  17.2 0.0 copy-done
  17.2 0.0 copy-done.1
  17.2 0.6 %shard_map.59 = (f32[16,512]{1,0:T(8,128)S(1)}, f32[4,128]{1,0:T(4,128)S(1)}, bf16[2,256,256]{2,1,0:T(8,128)(2,1)S(1)}) custom-call(s32[4]{0:T(128)S(1)} %copy-done.1, bf16[2,256,256]{2,1,0:T(8,128)(2,1)S(1)} %copy-done), custom_call_target="tpu_custom_call" | custom-call | tf_op jit(solution)/shard_map/pallas_call | solution.py:89
  17.8 1.4 %collective-permute-done.6.refs_1_ = bf16[8,2,8,512]{3,2,1,0:T(8,128)(2,1)S(1)} collective-permute-done((bf16[8,2,8,512]{3,2,1,0:T(8,128)(2,1)S(1)}, bf16[8,2,8,512]{3,2,1,0:T(8,128)(2,1)S(1)}, u32[]{:S(2)}, u32[]{:S(2)}) %collective-permute-start.6) | collective-permute-done | bytes 131104 | tf_op jit(solution)/shard_map/ppermute | solution.py:223
  19.1 1.3 %shard_map.62 = (bf16[1,2,4,1,2,128,128]{6,5,4,3,2,1,0:T(8,128)(2,1)}, bf16[256,512]{1,0:T(8,128)(2,1)S(1)}, f32[256,512]{1,0:T(8,128)S(1)}) custom-call(f32[16,512]{1,0:T(8,128)S(1)} %get-tuple-element.13.window_ref, f32[4,128]{1,0:T(4,128)S(1)} %get-tuple-element.14.inverse_ref, bf16[2,256,256]{2,1,0:T(8,128)(2,1)S(1)} %get-tuple-element.15.stacked_ref, ...), custom_call_target="tpu_custom_call" | custom-call | tf_op jit(solution)/shard_map/pallas_call | solution.py:185
  20.4 2.0 %collective-permute-done.8.refs_2_ = bf16[6,2,8,512]{3,2,1,0:T(8,128)(2,1)S(1)} collective-permute-done((bf16[6,2,8,512]{3,2,1,0:T(8,128)(2,1)S(1)}, bf16[6,2,8,512]{3,2,1,0:T(8,128)(2,1)S(1)}, u32[]{:S(2)}, u32[]{:S(2)}) %collective-permute-start.8) | collective-permute-done | bytes 98336 | tf_op jit(solution)/shard_map/ppermute | solution.py:229
  22.4 0.0 collective-permute-done.7.refs_1_
  22.4 1.3 %shard_map.63 = (bf16[1,2,4,1,2,128,128]{6,5,4,3,2,1,0:T(8,128)(2,1)}, f32[4,1,128]{2,1,0:T(1,128)}) custom-call(f32[16,512]{1,0:T(8,128)S(1)} %get-tuple-element.13.window_ref, f32[4,128]{1,0:T(4,128)S(1)} %get-tuple-element.14.inverse_ref, bf16[2,256,256]{2,1,0:T(8,128)(2,1)S(1)} %get-tuple-element.15.stacked_ref, ...), custom_call_target="tpu_custom_call", output_to_operand_aliasing={{0}: (8, {})} | custom-call | tf_op jit(solution)/shard_map/pallas_call | solution.py:205
  (7 shorter events, 0.1 us)
Async XLA Ops:
  0.6 1.6 %copy-start.2 = (s32[8]{0:T(128)S(1)}, s32[8]{0:T(128)}, u32[]{:S(2)}) copy-start(s32[8]{0:T(128)} %param.5) | copy-start | bytes 100
  0.6 1.9 %collective-permute-start.1 = (bf16[16,2,8,512]{3,2,1,0:T(8,128)(2,1)}, bf16[16,2,8,512]{3,2,1,0:T(8,128)(2,1)S(1)}, u32[]{:S(2)}, u32[]{:S(2)}) collective-permute-start(bf16[16,2,8,512]{3,2,1,0:T(8,128)(2,1)} %param.4), channel_id=1, source_target_pairs={{0,2},{2,0},{4,6},{6,4},{8,10},{10,8},{12,14},{14,12},{16,18},{18,... | collective-permute-start | bytes 786440 | tf_op jit(solution)/shard_map/ppermute | solution.py:223
  1.2 1.4 %collective-permute-start = (s32[8]{0:T(128)}, s32[8]{0:T(128)S(1)}, u32[]{:S(2)}, u32[]{:S(2)}) collective-permute-start(s32[8]{0:T(128)} %param.5), channel_id=1, source_target_pairs={{0,2},{2,0},{4,6},{6,4},{8,10},{10,8},{12,14},{14,12},{16,18},{18,... | collective-permute-start | bytes 104 | tf_op jit(solution)/shard_map/ppermute | solution.py:223
  2.8 10.4 %collective-permute-start.5 = (bf16[2,2,2,8,512]{4,3,2,1,0:T(8,128)(2,1)S(1)}, bf16[2,2,2,8,512]{4,3,2,1,0:T(8,128)(2,1)S(1)}, u32[]{:S(2)}, u32[]{:S(2)}) collective-permute-start(bf16[2,2,2,8,512]{4,3,2,1,0:T(8,128)(2,1)S(1)} %get-tuple-element.24), channel_id=1, source_target_pairs={{0,16},{2,18},{4,20},{6,22},{8,24},{10,26},{12,28},{14,30},{16,0},... | collective-permute-start | bytes 196616 | tf_op jit(solution)/shard_map/ppermute | solution.py:223
  6.8 6.4 %collective-permute-start.3 = (bf16[2,2,2,8,512]{4,3,2,1,0:T(8,128)(2,1)S(1)}, bf16[2,2,2,8,512]{4,3,2,1,0:T(8,128)(2,1)S(1)}, u32[]{:S(2)}, u32[]{:S(2)}) collective-permute-start(bf16[2,2,2,8,512]{4,3,2,1,0:T(8,128)(2,1)S(1)} %get-tuple-element.26), channel_id=1, source_target_pairs={{0,24},{2,26},{4,28},{6,30},{8,16},{10,18},{12,20},{14,22},{16,8},... | collective-permute-start | bytes 196616 | tf_op jit(solution)/shard_map/ppermute | solution.py:223
  8.2 5.2 %collective-permute-start.4 = (bf16[2,2,2,8,512]{4,3,2,1,0:T(8,128)(2,1)S(1)}, bf16[2,2,2,8,512]{4,3,2,1,0:T(8,128)(2,1)S(1)}, u32[]{:S(2)}, u32[]{:S(2)}) collective-permute-start(bf16[2,2,2,8,512]{4,3,2,1,0:T(8,128)(2,1)S(1)} %get-tuple-element.27), channel_id=1, source_target_pairs={{0,8},{2,10},{4,12},{6,14},{8,0},{10,2},{12,4},{14,6},{16,24},{18,... | collective-permute-start | bytes 196616 | tf_op jit(solution)/shard_map/ppermute | solution.py:223
  8.4 4.8 %collective-permute-start.2 = (bf16[2,2,8,512]{3,2,1,0:T(8,128)(2,1)S(1)}, bf16[2,2,8,512]{3,2,1,0:T(8,128)(2,1)S(1)}, u32[]{:S(2)}, u32[]{:S(2)}) collective-permute-start(bf16[2,2,8,512]{3,2,1,0:T(8,128)(2,1)S(1)} %maximum_bitcast_fusion), channel_id=1, source_target_pairs={{5,0},{4,1},{7,2},{6,3},{1,4},{0,5},{3,6},{2,7},{13,8},{12,9},{15,... | collective-permute-start | bytes 98312 | tf_op jit(solution)/shard_map/ppermute | solution.py:229
  13.4 3.7 %copy-start = (bf16[2,256,256]{2,1,0:T(8,128)(2,1)S(1)}, bf16[2,256,256]{2,1,0:T(8,128)(2,1)}, u32[]{:S(2)}) copy-start(bf16[2,256,256]{2,1,0:T(8,128)(2,1)} %weight_ref.1) | copy-start | bytes 786436
  13.4 5.7 %collective-permute-start.6 = (bf16[8,2,8,512]{3,2,1,0:T(8,128)(2,1)S(1)}, bf16[8,2,8,512]{3,2,1,0:T(8,128)(2,1)S(1)}, u32[]{:S(2)}, u32[]{:S(2)}) collective-permute-start(bf16[8,2,8,512]{3,2,1,0:T(8,128)(2,1)S(1)} %pad_maximum_fusion.1), channel_id=1, source_target_pairs={{0,4},{2,6},{4,0},{6,2},{8,12},{10,14},{12,8},{14,10},{16,20},{18,... | collective-permute-start | bytes 393224 | tf_op jit(solution)/shard_map/ppermute | solution.py:223
  15.2 2.0 %copy-start.1 = (s32[4]{0:T(128)S(1)}, s32[4]{0:T(128)}, u32[]{:S(2)}) copy-start(s32[4]{0:T(128)} %length_ref.1) | copy-start | bytes 52
  15.2 7.2 %collective-permute-start.7 = (bf16[8,2,8,512]{3,2,1,0:T(8,128)(2,1)S(1)}, bf16[8,2,8,512]{3,2,1,0:T(8,128)(2,1)S(1)}, u32[]{:S(2)}, u32[]{:S(2)}) collective-permute-start(bf16[8,2,8,512]{3,2,1,0:T(8,128)(2,1)S(1)} %pad_maximum_fusion.refs_0_), channel_id=1, source_target_pairs={{1,0},{0,1},{3,2},{2,3},{5,4},{4,5},{7,6},{6,7},{9,8},{8,9},{11,10... | collective-permute-start | bytes 393224 | tf_op jit(solution)/shard_map/ppermute | solution.py:229
  16.8 5.6 %collective-permute-start.8 = (bf16[6,2,8,512]{3,2,1,0:T(8,128)(2,1)S(1)}, bf16[6,2,8,512]{3,2,1,0:T(8,128)(2,1)S(1)}, u32[]{:S(2)}, u32[]{:S(2)}) collective-permute-start(bf16[6,2,8,512]{3,2,1,0:T(8,128)(2,1)S(1)} %pad_maximum_fusion.2), channel_id=1, source_target_pairs={{5,0},{4,1},{7,2},{6,3},{1,4},{0,5},{3,6},{2,7},{13,8},{12,9},{15,... | collective-permute-start | bytes 294920 | tf_op jit(solution)/shard_map/ppermute | solution.py:229

commit v5 on v2

--- a/solution.py
+++ b/solution.py
@@ -10,6 +10,7 @@
 
 PHASES = 1024
 VMEM_BYTES = 32 * 1024 * 1024
+PREPARE_FLOPS = 3_000_000_000
 IN_VMEM = pl.BlockSpec(memory_space=pltpu.VMEM)
 IN_SMEM = pl.BlockSpec(memory_space=pltpu.SMEM)
 
@@ -33,31 +34,29 @@
     return cos_out, sin_out
 
 
-def rotate_kernel(step_ref, volt_ref, kept_ref, given_ref):
-    channels, _, rows, samples = volt_ref.shape
+def rotate_kernel(step_ref, volt_ref, out_ref):
+    slots = out_ref.shape[0]
     me = lax.axis_index("chan")
-    slot = lax.broadcasted_iota(jnp.int32, step_ref.shape, 1)
+    slot = 2 * lax.broadcasted_iota(jnp.int32, step_ref.shape, 1)
     cosine, sine = phasors((step_ref[...] * jnp.bitwise_xor(slot, me)) % PHASES)
-    for k in range(channels):
-        c = jnp.bitwise_xor(me, k)
-        cos_c = cosine[:, k : k + 1]
-        sin_c = sine[:, k : k + 1]
+    for i in range(slots):
+        c = jnp.bitwise_xor(me, 2 * i)
+        cos_c = cosine[:, i : i + 1]
+        sin_c = sine[:, i : i + 1]
         real_in = volt_ref[c, 0].astype(jnp.float32)
         imag_in = volt_ref[c, 1].astype(jnp.float32)
-        out_ref = given_ref if k % 2 else kept_ref
-        out_ref[k // 2, 0] = (real_in * cos_c + imag_in * sin_c).astype(jnp.bfloat16)
-        out_ref[k // 2, 1] = (imag_in * cos_c - real_in * sin_c).astype(jnp.bfloat16)
+        out_ref[i, 0] = (real_in * cos_c + imag_in * sin_c).astype(jnp.bfloat16)
+        out_ref[i, 1] = (imag_in * cos_c - real_in * sin_c).astype(jnp.bfloat16)
 
 
 def rotate(voltages, phase_index):
     channels, parts, rows, samples = voltages.shape
     step = jnp.broadcast_to(phase_index[:, None], (rows, 128 * pl.cdiv(channels, 128)))
-    half = jax.ShapeDtypeStruct((channels // 2, parts, rows, samples), jnp.bfloat16)
     return pl.pallas_call(
         rotate_kernel,
-        out_shape=(half, half),
+        out_shape=jax.ShapeDtypeStruct((channels // 2, parts, rows, samples), jnp.bfloat16),
         in_specs=[IN_VMEM, IN_VMEM],
-        out_specs=(IN_VMEM, IN_VMEM),
+        out_specs=IN_VMEM,
         compiler_params=params(),
     )(step, voltages)
 
@@ -97,6 +96,7 @@
         ),
         in_specs=[IN_SMEM, IN_VMEM],
         out_specs=(IN_VMEM, IN_VMEM, IN_VMEM),
+        cost_estimate=pl.CostEstimate(flops=PREPARE_FLOPS, transcendentals=0, bytes_accessed=0),
         compiler_params=params(),
     )(int_lengths, beam_weights)
 
@@ -105,43 +105,55 @@
     return lax.dot_general(a, b, (((1,), (1,)), ((), ())), preferred_element_type=jnp.float32)
 
 
+def assemble(pieces, layout, blocks_ref):
+    me = lax.axis_index("chan")
+    for piece_ref, (block, offsets) in zip(pieces, layout):
+        for i, offset in enumerate(offsets):
+            source = jnp.bitwise_xor(me, offset)
+            for part in range(piece_ref.shape[1]):
+                blocks_ref[block, part, source] = piece_ref[i, part]
+
+
+def assembled(blocks_ref, block):
+    _, parts, channels, rows, samples = blocks_ref.shape
+    values = blocks_ref[block].astype(jnp.float32)
+    return values.reshape(parts * channels * rows, samples).astype(jnp.bfloat16)
+
+
+def correlate(masked, other, inverse_ref, vis_ref, slot):
+    twice = other.shape[0]
+    half = twice // 2
+    products = dot_nt(masked, other)
+    for j in range(vis_ref.shape[2]):
+        prod = products[j * twice : (j + 1) * twice]
+        inverse = inverse_ref[j : j + 1]
+        real = prod[:half, :half] + prod[half:, half:]
+        imag = prod[half:, :half] - prod[:half, half:]
+        vis_ref[0, slot, j, 0, 0] = (real * inverse).astype(jnp.bfloat16)
+        vis_ref[0, slot, j, 0, 1] = (imag * inverse).astype(jnp.bfloat16)
+
+
 def finish_kernel(layout, window_ref, inverse_ref, stacked_ref, *refs):
     pieces, (vis_ref, power_ref, blocks_ref) = refs[:-3], refs[-3:]
-    stations, parts, channels, rows, samples = blocks_ref.shape
-    twice = parts * channels * rows
-    half = twice // 2
+    stations = blocks_ref.shape[0]
     _, slots, integs = vis_ref.shape[:3]
     share = power_ref.shape[2]
-    me = lax.axis_index("chan")
     station = lax.axis_index("stn")
-
-    for piece_ref, (dy, offsets) in zip(pieces, layout):
-        b = lax.rem(station + dy, stations)
-        for i, offset in enumerate(offsets):
-            source = jnp.bitwise_xor(me, offset)
-            for part in range(parts):
-                blocks_ref[b, part, source] = piece_ref[i, part]
-
-    def block(b):
-        return blocks_ref[b].astype(jnp.float32).reshape(twice, samples).astype(jnp.bfloat16)
-
+    assemble(pieces, layout, blocks_ref)
+
+    own = assembled(blocks_ref, 0)
     window = window_ref[...].astype(jnp.bfloat16)
-    own = block(station)
     masked = jnp.concatenate([own * window[j : j + 1] for j in range(integs)], axis=0)
     for k in range(slots):
-        other = own if k == 0 else block(lax.rem(station + k, stations))
-        products = dot_nt(masked, other)
-        for j in range(integs):
-            prod = products[j * twice : (j + 1) * twice]
-            inverse = inverse_ref[j : j + 1]
-            real = prod[:half, :half] + prod[half:, half:]
-            imag = prod[half:, :half] - prod[:half, half:]
-            vis_ref[0, k, j, 0, 0] = (real * inverse).astype(jnp.bfloat16)
-            vis_ref[0, k, j, 0, 1] = (imag * inverse).astype(jnp.bfloat16)
-
-    beam = jnp.zeros((2 * share, samples), jnp.float32)
+        other = assembled(blocks_ref, k) if k else own
+        correlate(masked, other, inverse_ref, vis_ref, k)
+
+    beam = jnp.zeros((2 * share, own.shape[1]), jnp.float32)
     for b in range(stations):
-        beam = beam + jnp.dot(stacked_ref[b], block(b), preferred_element_type=jnp.float32)
+        weights = stacked_ref[lax.rem(station + b, stations)]
+        beam = beam + jnp.dot(
+            weights, assembled(blocks_ref, b), preferred_element_type=jnp.float32
+        )
     power = beam[:share] * beam[:share] + beam[share:] * beam[share:]
     high = power.astype(jnp.bfloat16)
     low = (power - high.astype(jnp.float32)).astype(jnp.bfloat16)
@@ -182,10 +194,11 @@
     stations = lax.axis_size("stn")
     channels, parts, rows, samples = voltages.shape
     far = channels // 4
-    kept, given = rotate(voltages, phase_index)
-    prepared = prepare(int_lengths, beam_weights, stations, channels * rows, samples)
-
-    both = jnp.stack([kept, exchanged(given, 1, 0)], axis=1)
+    pair_phase, pair_voltages = exchanged(phase_index, 1, 0), exchanged(voltages, 1, 0)
+    kept = rotate(voltages.astype(jnp.float32), phase_index)
+    swapped = rotate(pair_voltages, pair_phase)
+
+    both = jnp.stack([kept, swapped], axis=1)
     both = both.reshape(far, 2, 2, parts, rows, samples)
     arrived = [both[0]] + [exchanged(both[k], 4 * k, 0) for k in range(1, far)]
 
@@ -198,13 +211,21 @@
     for dy in range(1, stations):
         pieces.append(exchanged(held(1, (0,)), 2, dy))
         layout.append((1, dy, (0,)))
-    pieces, arrived = lax.optimization_barrier((pieces, arrived))
+    order = (0, far - 1, *range(1, far - 1))
+    pieces, waited = lax.optimization_barrier((pieces, [arrived[k] for k in order]))
+    arrived = [waited[order.index(k)] for k in every]
+    for dy in range(1, stations):
+        pieces.append(exchanged(held(1, every[1:]), 2, dy))
+        layout.append((1, dy, every[1:]))
+    pieces, int_lengths, beam_weights = lax.optimization_barrier(
+        (pieces, int_lengths, beam_weights)
+    )
+    prepared = prepare(int_lengths, beam_weights, stations, channels * rows, samples)
     for dy in range(stations):
-        for dx in range(2):
-            ks = every[1:] if dx and dy else every
-            piece = held(dx, ks)
+        for dx in range(1 if dy else 2):
+            piece = held(dx, every)
             pieces.append(exchanged(piece, 2 * dx, dy) if dx or dy else piece)
-            layout.append((dx, dy, ks))
+            layout.append((dx, dy, every))
     layout = [
         (dy, tuple(4 * k + 2 * dx + pair for k in ks for pair in range(2)))
         for dx, dy, ks in layout

time: 25.7 us -> 23.7 us (0.922)
  local copies, waits for them, and re-layouts: 1.71 us -> 0.17 us
  waiting for transfers between devices: 8.06 us -> 6.62 us
  other arithmetic: 0.08 us -> 1.08 us
    ppermute x3, waiting for transfers between devices: 6.66 us -> 5.58 us  [exchanged(): return lax.ppermute(value, ('chan', 'stn'), pairs)]
    convert_element_type x0 -> x1, other arithmetic: none -> 1 us  [local(): kept = rotate(voltages.astype(jnp.float32), phase_index)]
    ppermute x5 -> x6, starting transfers between devices: 7.74 us -> 6.75 us  [exchanged(): lax.ppermute(value, 'chan', [(c, c ^ offset) for c in range(channels)])]
    unnamed x6, local copies, waits for them, and re-layouts: 0.96 us -> 0.01 us
    ppermute x3, starting transfers between devices: 4.72 us -> 5.53 us  [exchanged(): return lax.ppermute(value, ('chan', 'stn'), pairs)]
    broadcast_in_dim x1 -> x2, local copies, waits for them, and re-layouts: 0.72 us -> 0.14 us  [rotate(): jnp.broadcast_to(phase_index[:, None], (rows, 128 * pl.cdiv(channels, 128)))]
    ppermute x5 -> x6, waiting for transfers between devices: 1.4 us -> 1.04 us  [exchanged(): lax.ppermute(value, 'chan', [(c, c ^ offset) for c in range(channels)])]
  transfers between devices with their start and end apart: 8 -> 9, of which waited for: 4 -> 6; matrix products, arithmetic and copies ran while one was open for 0% -> 5% of each run, Pallas kernels for 2% -> 3%
where the time goes in v5:
time: 23.7 us; the launch traced here: 23.5 us
  starting transfers between devices  12.3 us (52%)
  waiting for transfers between devices  6.62 us (28%)
  Pallas kernels  2.63 us (11%)
  other arithmetic  1.08 us (5%)
  between operations  0.74 us (3%)
    ppermute x6, starting transfers between devices, exchanged(): lax.ppermute(value, 'chan', [(c, c ^ offset) for c in range(channels)])  6.75 us
    ppermute x3, waiting for transfers between devices, exchanged(): return lax.ppermute(value, ('chan', 'stn'), pairs)  5.58 us
    ppermute x3, starting transfers between devices, exchanged(): return lax.ppermute(value, ('chan', 'stn'), pairs)  5.53 us
    pallas_call x1, Pallas kernels, finish(): pl.pallas_call(functools.partial(finish_kernel, layout), out_shape=(jax.S...  1.76 us
    ppermute x6, waiting for transfers between devices, exchanged(): lax.ppermute(value, 'chan', [(c, c ^ offset) for c in range(channels)])  1.04 us
    convert_element_type x1, other arithmetic, local(): kept = rotate(voltages.astype(jnp.float32), phase_index)  1 us
    pallas_call x1, Pallas kernels, prepare(): pl.pallas_call(prepare_kernel, out_shape=(jax.ShapeDtypeStruct((16, sampl...  0.59 us
  transfers between devices with their start and end apart: 9, of which 6 were waited for; matrix products, arithmetic and copies ran while one was open for 5% of the time, Pallas kernels for 3%

profile of v5, /device:TPU:0, one launch (start us, length us, event | category | flops | bytes accessed | tf_op | source)
XLA Modules:
  0.0 23.5 jit_solution(10655355402666915385)
XLA Ops:
  0.6 0.0 copy-start.2
  0.6 0.5 %collective-permute-start.1 = (bf16[16,2,8,512]{3,2,1,0:T(8,128)(2,1)}, bf16[16,2,8,512]{3,2,1,0:T(8,128)(2,1)S(1)}, u32[]{:S(2)}, u32[]{:S(2)}) collective-permute-start(bf16[16,2,8,512]{3,2,1,0:T(8,128)(2,1)} %param.4), channel_id=1, source_target_pairs={{0,2},{2,0},{4,6},{6,4},{8,10},{10,8},{12,14},{14,12},{16,18},{18,... | collective-permute-start | bytes 786440 | tf_op jit(solution)/shard_map/ppermute | solution.py:184
  1.2 0.1 collective-permute-start
  1.2 1.0 %convert_element_type.3.volt_ref = f32[16,2,8,512]{3,2,1,0:T(8,128)S(1)} convert(bf16[16,2,8,512]{3,2,1,0:T(8,128)(2,1)} %param.4) | non-fusion elementwise | flops 131072 | bytes 786432 | tf_op jit(solution)/shard_map/convert_element_type | solution.py:198
  2.2 0.0 copy-done.2
  2.3 0.1 broadcast_in_dim.4.step_ref
  2.3 0.1 shard_map.59
  2.5 0.1 collective-permute-done
  2.5 0.0 collective-permute-done.1.volt_ref
  2.5 0.1 broadcast_in_dim.5.step_ref
  2.6 0.1 shard_map.60
  2.8 4.0 %collective-permute-start.5 = (bf16[2,2,2,8,512]{4,3,2,1,0:T(8,128)(2,1)S(1)}, bf16[2,2,2,8,512]{4,3,2,1,0:T(8,128)(2,1)S(1)}, u32[]{:S(2)}, u32[]{:S(2)}) collective-permute-start(bf16[2,2,2,8,512]{4,3,2,1,0:T(8,128)(2,1)S(1)} %get-tuple-element.26), channel_id=1, source_target_pairs={{0,16},{2,18},{4,20},{6,22},{8,24},{10,26},{12,28},{14,30},{16,0},... | collective-permute-start | bytes 196616 | tf_op jit(solution)/shard_map/ppermute | solution.py:184
  6.8 1.3 %collective-permute-start.3 = (bf16[2,2,2,8,512]{4,3,2,1,0:T(8,128)(2,1)S(1)}, bf16[2,2,2,8,512]{4,3,2,1,0:T(8,128)(2,1)S(1)}, u32[]{:S(2)}, u32[]{:S(2)}) collective-permute-start(bf16[2,2,2,8,512]{4,3,2,1,0:T(8,128)(2,1)S(1)} %get-tuple-element.28), channel_id=1, source_target_pairs={{0,24},{2,26},{4,28},{6,30},{8,16},{10,18},{12,20},{14,22},{16,8},... | collective-permute-start | bytes 196616 | tf_op jit(solution)/shard_map/ppermute | solution.py:184
  8.2 0.2 collective-permute-start.4
  8.4 2.4 %collective-permute-start.2 = (bf16[2,2,8,512]{3,2,1,0:T(8,128)(2,1)S(1)}, bf16[2,2,8,512]{3,2,1,0:T(8,128)(2,1)S(1)}, u32[]{:S(2)}, u32[]{:S(2)}) collective-permute-start(bf16[2,2,8,512]{3,2,1,0:T(8,128)(2,1)S(1)} %maximum_bitcast_fusion), channel_id=1, source_target_pairs={{5,0},{4,1},{7,2},{6,3},{1,4},{0,5},{3,6},{2,7},{13,8},{12,9},{15,... | collective-permute-start | bytes 98312 | tf_op jit(solution)/shard_map/ppermute | solution.py:190
  10.9 2.4 %collective-permute-done.2.refs_0_ = bf16[2,2,8,512]{3,2,1,0:T(8,128)(2,1)S(1)} collective-permute-done((bf16[2,2,8,512]{3,2,1,0:T(8,128)(2,1)S(1)}, bf16[2,2,8,512]{3,2,1,0:T(8,128)(2,1)S(1)}, u32[]{:S(2)}, u32[]{:S(2)}) %collective-permute-start.2) | collective-permute-done | bytes 32800 | tf_op jit(solution)/shard_map/ppermute | solution.py:190
  13.2 0.0 collective-permute-done.5
  13.2 0.0 collective-permute-done.3
  13.2 0.1 collective-permute-done.4
  13.4 0.0 copy-start
  13.5 2.7 %collective-permute-start.6 = (bf16[6,2,8,512]{3,2,1,0:T(8,128)(2,1)S(1)}, bf16[6,2,8,512]{3,2,1,0:T(8,128)(2,1)S(1)}, u32[]{:S(2)}, u32[]{:S(2)}) collective-permute-start(bf16[6,2,8,512]{3,2,1,0:T(8,128)(2,1)S(1)} %pad_maximum_fusion.2), channel_id=1, source_target_pairs={{5,0},{4,1},{7,2},{6,3},{1,4},{0,5},{3,6},{2,7},{13,8},{12,9},{15,... | collective-permute-start | bytes 294920 | tf_op jit(solution)/shard_map/ppermute | solution.py:190
  16.2 0.5 %collective-permute-start.7 = (bf16[8,2,8,512]{3,2,1,0:T(8,128)(2,1)S(1)}, bf16[8,2,8,512]{3,2,1,0:T(8,128)(2,1)S(1)}, u32[]{:S(2)}, u32[]{:S(2)}) collective-permute-start(bf16[8,2,8,512]{3,2,1,0:T(8,128)(2,1)S(1)} %pad_maximum_fusion.1), channel_id=1, source_target_pairs={{0,4},{2,6},{4,0},{6,2},{8,12},{10,14},{12,8},{14,10},{16,20},{18,... | collective-permute-start | bytes 393224 | tf_op jit(solution)/shard_map/ppermute | solution.py:184
  16.7 0.0 copy-start.1
  16.7 0.4 %collective-permute-start.8 = (bf16[8,2,8,512]{3,2,1,0:T(8,128)(2,1)S(1)}, bf16[8,2,8,512]{3,2,1,0:T(8,128)(2,1)S(1)}, u32[]{:S(2)}, u32[]{:S(2)}) collective-permute-start(bf16[8,2,8,512]{3,2,1,0:T(8,128)(2,1)S(1)} %pad_maximum_fusion.refs_2_), channel_id=1, source_target_pairs={{1,0},{0,1},{3,2},{2,3},{5,4},{4,5},{7,6},{6,7},{9,8},{8,9},{11,10... | collective-permute-start | bytes 393224 | tf_op jit(solution)/shard_map/ppermute | solution.py:190
  17.1 2.8 %collective-permute-done.6.refs_1_ = bf16[6,2,8,512]{3,2,1,0:T(8,128)(2,1)S(1)} collective-permute-done((bf16[6,2,8,512]{3,2,1,0:T(8,128)(2,1)S(1)}, bf16[6,2,8,512]{3,2,1,0:T(8,128)(2,1)S(1)}, u32[]{:S(2)}, u32[]{:S(2)}) %collective-permute-start.6) | collective-permute-done | bytes 98336 | tf_op jit(solution)/shard_map/ppermute | solution.py:190
  19.9 0.0 copy-done
  19.9 0.0 copy-done.1
  19.9 0.6 %shard_map.61 = (f32[16,512]{1,0:T(8,128)S(1)}, f32[4,128]{1,0:T(4,128)S(1)}, bf16[2,256,256]{2,1,0:T(8,128)(2,1)S(1)}) custom-call(s32[4]{0:T(128)S(1)} %copy-done.1, bf16[2,256,256]{2,1,0:T(8,128)(2,1)S(1)} %copy-done), custom_call_target="tpu_custom_call" | custom-call | flops 3000000000 | tf_op jit(solution)/shard_map/pallas_call | solution.py:90
  20.5 0.8 %collective-permute-done.7.refs_3_ = bf16[8,2,8,512]{3,2,1,0:T(8,128)(2,1)S(1)} collective-permute-done((bf16[8,2,8,512]{3,2,1,0:T(8,128)(2,1)S(1)}, bf16[8,2,8,512]{3,2,1,0:T(8,128)(2,1)S(1)}, u32[]{:S(2)}, u32[]{:S(2)}) %collective-permute-start.7) | collective-permute-done | bytes 131104 | tf_op jit(solution)/shard_map/ppermute | solution.py:184
  21.3 0.4 %collective-permute-done.8.refs_4_ = bf16[8,2,8,512]{3,2,1,0:T(8,128)(2,1)S(1)} collective-permute-done((bf16[8,2,8,512]{3,2,1,0:T(8,128)(2,1)S(1)}, bf16[8,2,8,512]{3,2,1,0:T(8,128)(2,1)S(1)}, u32[]{:S(2)}, u32[]{:S(2)}) %collective-permute-start.8) | collective-permute-done | bytes 131104 | tf_op jit(solution)/shard_map/ppermute | solution.py:190
  21.8 1.8 %shard_map.62 = (bf16[1,2,4,1,2,128,128]{6,5,4,3,2,1,0:T(8,128)(2,1)}, f32[4,1,128]{2,1,0:T(1,128)}) custom-call(f32[16,512]{1,0:T(8,128)S(1)} %get-tuple-element.20.window_ref, f32[4,128]{1,0:T(4,128)S(1)} %get-tuple-element.21.inverse_ref, bf16[2,256,256]{2,1,0:T(8,128)(2,1)S(1)} %get-tuple-element.22.stacked_ref, ...), custom_call_target="tpu_custom_call" | custom-call | tf_op jit(solution)/shard_map/pallas_call | solution.py:168
  (7 shorter events, 0.1 us)
Async XLA Ops:
  0.6 1.6 %copy-start.2 = (s32[8]{0:T(128)S(1)}, s32[8]{0:T(128)}, u32[]{:S(2)}) copy-start(s32[8]{0:T(128)} %param.5) | copy-start | bytes 100
  0.6 1.9 %collective-permute-start.1 = (bf16[16,2,8,512]{3,2,1,0:T(8,128)(2,1)}, bf16[16,2,8,512]{3,2,1,0:T(8,128)(2,1)S(1)}, u32[]{:S(2)}, u32[]{:S(2)}) collective-permute-start(bf16[16,2,8,512]{3,2,1,0:T(8,128)(2,1)} %param.4), channel_id=1, source_target_pairs={{0,2},{2,0},{4,6},{6,4},{8,10},{10,8},{12,14},{14,12},{16,18},{18,... | collective-permute-start | bytes 786440 | tf_op jit(solution)/shard_map/ppermute | solution.py:184
  1.2 1.4 %collective-permute-start = (s32[8]{0:T(128)}, s32[8]{0:T(128)S(1)}, u32[]{:S(2)}, u32[]{:S(2)}) collective-permute-start(s32[8]{0:T(128)} %param.5), channel_id=1, source_target_pairs={{0,2},{2,0},{4,6},{6,4},{8,10},{10,8},{12,14},{14,12},{16,18},{18,... | collective-permute-start | bytes 104 | tf_op jit(solution)/shard_map/ppermute | solution.py:184
  2.8 10.4 %collective-permute-start.5 = (bf16[2,2,2,8,512]{4,3,2,1,0:T(8,128)(2,1)S(1)}, bf16[2,2,2,8,512]{4,3,2,1,0:T(8,128)(2,1)S(1)}, u32[]{:S(2)}, u32[]{:S(2)}) collective-permute-start(bf16[2,2,2,8,512]{4,3,2,1,0:T(8,128)(2,1)S(1)} %get-tuple-element.26), channel_id=1, source_target_pairs={{0,16},{2,18},{4,20},{6,22},{8,24},{10,26},{12,28},{14,30},{16,0},... | collective-permute-start | bytes 196616 | tf_op jit(solution)/shard_map/ppermute | solution.py:184
  6.8 6.4 %collective-permute-start.3 = (bf16[2,2,2,8,512]{4,3,2,1,0:T(8,128)(2,1)S(1)}, bf16[2,2,2,8,512]{4,3,2,1,0:T(8,128)(2,1)S(1)}, u32[]{:S(2)}, u32[]{:S(2)}) collective-permute-start(bf16[2,2,2,8,512]{4,3,2,1,0:T(8,128)(2,1)S(1)} %get-tuple-element.28), channel_id=1, source_target_pairs={{0,24},{2,26},{4,28},{6,30},{8,16},{10,18},{12,20},{14,22},{16,8},... | collective-permute-start | bytes 196616 | tf_op jit(solution)/shard_map/ppermute | solution.py:184
  8.2 5.2 %collective-permute-start.4 = (bf16[2,2,2,8,512]{4,3,2,1,0:T(8,128)(2,1)S(1)}, bf16[2,2,2,8,512]{4,3,2,1,0:T(8,128)(2,1)S(1)}, u32[]{:S(2)}, u32[]{:S(2)}) collective-permute-start(bf16[2,2,2,8,512]{4,3,2,1,0:T(8,128)(2,1)S(1)} %get-tuple-element.29), channel_id=1, source_target_pairs={{0,8},{2,10},{4,12},{6,14},{8,0},{10,2},{12,4},{14,6},{16,24},{18,... | collective-permute-start | bytes 196616 | tf_op jit(solution)/shard_map/ppermute | solution.py:184
  8.4 4.8 %collective-permute-start.2 = (bf16[2,2,8,512]{3,2,1,0:T(8,128)(2,1)S(1)}, bf16[2,2,8,512]{3,2,1,0:T(8,128)(2,1)S(1)}, u32[]{:S(2)}, u32[]{:S(2)}) collective-permute-start(bf16[2,2,8,512]{3,2,1,0:T(8,128)(2,1)S(1)} %maximum_bitcast_fusion), channel_id=1, source_target_pairs={{5,0},{4,1},{7,2},{6,3},{1,4},{0,5},{3,6},{2,7},{13,8},{12,9},{15,... | collective-permute-start | bytes 98312 | tf_op jit(solution)/shard_map/ppermute | solution.py:190
  13.4 6.5 %copy-start = (bf16[2,256,256]{2,1,0:T(8,128)(2,1)S(1)}, bf16[2,256,256]{2,1,0:T(8,128)(2,1)}, u32[]{:S(2)}) copy-start(bf16[2,256,256]{2,1,0:T(8,128)(2,1)} %weight_ref) | copy-start | bytes 786436
  13.5 6.4 %collective-permute-start.6 = (bf16[6,2,8,512]{3,2,1,0:T(8,128)(2,1)S(1)}, bf16[6,2,8,512]{3,2,1,0:T(8,128)(2,1)S(1)}, u32[]{:S(2)}, u32[]{:S(2)}) collective-permute-start(bf16[6,2,8,512]{3,2,1,0:T(8,128)(2,1)S(1)} %pad_maximum_fusion.2), channel_id=1, source_target_pairs={{5,0},{4,1},{7,2},{6,3},{1,4},{0,5},{3,6},{2,7},{13,8},{12,9},{15,... | collective-permute-start | bytes 294920 | tf_op jit(solution)/shard_map/ppermute | solution.py:190
  16.2 5.2 %collective-permute-start.7 = (bf16[8,2,8,512]{3,2,1,0:T(8,128)(2,1)S(1)}, bf16[8,2,8,512]{3,2,1,0:T(8,128)(2,1)S(1)}, u32[]{:S(2)}, u32[]{:S(2)}) collective-permute-start(bf16[8,2,8,512]{3,2,1,0:T(8,128)(2,1)S(1)} %pad_maximum_fusion.1), channel_id=1, source_target_pairs={{0,4},{2,6},{4,0},{6,2},{8,12},{10,14},{12,8},{14,10},{16,20},{18,... | collective-permute-start | bytes 393224 | tf_op jit(solution)/shard_map/ppermute | solution.py:184
  16.7 3.2 %copy-start.1 = (s32[4]{0:T(128)S(1)}, s32[4]{0:T(128)}, u32[]{:S(2)}) copy-start(s32[4]{0:T(128)} %length_ref) | copy-start | bytes 52
  16.7 5.0 %collective-permute-start.8 = (bf16[8,2,8,512]{3,2,1,0:T(8,128)(2,1)S(1)}, bf16[8,2,8,512]{3,2,1,0:T(8,128)(2,1)S(1)}, u32[]{:S(2)}, u32[]{:S(2)}) collective-permute-start(bf16[8,2,8,512]{3,2,1,0:T(8,128)(2,1)S(1)} %pad_maximum_fusion.refs_2_), channel_id=1, source_target_pairs={{1,0},{0,1},{3,2},{2,3},{5,4},{4,5},{7,6},{6,7},{9,8},{8,9},{11,10... | collective-permute-start | bytes 393224 | tf_op jit(solution)/shard_map/ppermute | solution.py:190

commit v6 on v5

--- a/solution.py
+++ b/solution.py
@@ -209,10 +209,11 @@
     every = tuple(range(far))
     pieces, layout = [], []
     for dy in range(1, stations):
-        pieces.append(exchanged(held(1, (0,)), 2, dy))
-        layout.append((1, dy, (0,)))
+        for dx in (1, 0):
+            pieces.append(exchanged(held(dx, (0,)), 2 * dx, dy))
+            layout.append((dx, dy, (0,)))
     order = (0, far - 1, *range(1, far - 1))
-    pieces, waited = lax.optimization_barrier((pieces, [arrived[k] for k in order]))
+    waited = lax.optimization_barrier([arrived[k] for k in order])
     arrived = [waited[order.index(k)] for k in every]
     for dy in range(1, stations):
         pieces.append(exchanged(held(1, every[1:]), 2, dy))
@@ -223,9 +224,10 @@
     prepared = prepare(int_lengths, beam_weights, stations, channels * rows, samples)
     for dy in range(stations):
         for dx in range(1 if dy else 2):
-            piece = held(dx, every)
+            ks = every[1:] if dy else every
+            piece = held(dx, ks)
             pieces.append(exchanged(piece, 2 * dx, dy) if dx or dy else piece)
-            layout.append((dx, dy, every))
+            layout.append((dx, dy, ks))
     layout = [
         (dy, tuple(4 * k + 2 * dx + pair for k in ks for pair in range(2)))
         for dx, dy, ks in layout

time: 23.7 us -> 23.7 us (level)
  waiting for transfers between devices: 6.62 us -> 6.02 us
  starting transfers between devices: 12.3 us -> 12.8 us
    ppermute x3 -> x4, waiting for transfers between devices: 5.58 us -> 3.16 us  [exchanged(): return lax.ppermute(value, ('chan', 'stn'), pairs)]
    ppermute x6, waiting for transfers between devices: 1.04 us -> 2.86 us  [exchanged(): lax.ppermute(value, 'chan', [(c, c ^ offset) for c in range(channels)])]
    ppermute x3 -> x4, starting transfers between devices: 5.53 us -> 6.29 us  [exchanged(): return lax.ppermute(value, ('chan', 'stn'), pairs)]
  transfers between devices with their start and end apart: 9 -> 10, of which waited for: 6 -> 6; matrix products, arithmetic and copies ran while one was open for 5% -> 5% of each run, Pallas kernels for 3% -> 3%
where the time goes in v6:
time: 23.7 us; the launch traced here: 23.5 us
  starting transfers between devices  12.8 us (54%)
  waiting for transfers between devices  6.02 us (25%)
  Pallas kernels  2.64 us (11%)
  other arithmetic  1.1 us (5%)
  between operations  0.75 us (3%)
    ppermute x6, starting transfers between devices, exchanged(): lax.ppermute(value, 'chan', [(c, c ^ offset) for c in range(channels)])  6.55 us
    ppermute x4, starting transfers between devices, exchanged(): return lax.ppermute(value, ('chan', 'stn'), pairs)  6.29 us
    ppermute x4, waiting for transfers between devices, exchanged(): return lax.ppermute(value, ('chan', 'stn'), pairs)  3.16 us
    ppermute x6, waiting for transfers between devices, exchanged(): lax.ppermute(value, 'chan', [(c, c ^ offset) for c in range(channels)])  2.86 us
    pallas_call x1, Pallas kernels, finish(): pl.pallas_call(functools.partial(finish_kernel, layout), out_shape=(jax.S...  1.76 us
    convert_element_type x1, other arithmetic, local(): kept = rotate(voltages.astype(jnp.float32), phase_index)  1 us
    pallas_call x1, Pallas kernels, prepare(): pl.pallas_call(prepare_kernel, out_shape=(jax.ShapeDtypeStruct((16, sampl...  0.59 us
  transfers between devices with their start and end apart: 10, of which 6 were waited for; matrix products, arithmetic and copies ran while one was open for 5% of the time, Pallas kernels for 3%

profile of v6, /device:TPU:0, one launch (start us, length us, event | category | flops | bytes accessed | tf_op | source)
XLA Modules:
  0.0 23.5 jit_solution(15024418162460554946)
XLA Ops:
  0.6 0.0 copy-start.2
  0.6 0.5 %collective-permute-start.1 = (bf16[16,2,8,512]{3,2,1,0:T(8,128)(2,1)}, bf16[16,2,8,512]{3,2,1,0:T(8,128)(2,1)S(1)}, u32[]{:S(2)}, u32[]{:S(2)}) collective-permute-start(bf16[16,2,8,512]{3,2,1,0:T(8,128)(2,1)} %param.4), channel_id=1, source_target_pairs={{0,2},{2,0},{4,6},{6,4},{8,10},{10,8},{12,14},{14,12},{16,18},{18,... | collective-permute-start | bytes 786440 | tf_op jit(solution)/shard_map/ppermute | solution.py:184
  1.2 0.1 collective-permute-start
  1.2 1.0 %convert_element_type.3.volt_ref = f32[16,2,8,512]{3,2,1,0:T(8,128)S(1)} convert(bf16[16,2,8,512]{3,2,1,0:T(8,128)(2,1)} %param.4) | non-fusion elementwise | flops 131072 | bytes 786432 | tf_op jit(solution)/shard_map/convert_element_type | solution.py:198
  2.2 0.0 copy-done.2
  2.3 0.1 broadcast_in_dim.4.step_ref
  2.3 0.1 shard_map.59
  2.5 0.1 collective-permute-done
  2.5 0.0 collective-permute-done.1.volt_ref
  2.5 0.1 broadcast_in_dim.5.step_ref
  2.6 0.1 shard_map.60
  2.8 4.0 %collective-permute-start.6 = (bf16[2,2,2,8,512]{4,3,2,1,0:T(8,128)(2,1)S(1)}, bf16[2,2,2,8,512]{4,3,2,1,0:T(8,128)(2,1)S(1)}, u32[]{:S(2)}, u32[]{:S(2)}) collective-permute-start(bf16[2,2,2,8,512]{4,3,2,1,0:T(8,128)(2,1)S(1)} %get-tuple-element.26), channel_id=1, source_target_pairs={{0,16},{2,18},{4,20},{6,22},{8,24},{10,26},{12,28},{14,30},{16,0},... | collective-permute-start | bytes 196616 | tf_op jit(solution)/shard_map/ppermute | solution.py:184
  6.8 1.3 %collective-permute-start.4 = (bf16[2,2,2,8,512]{4,3,2,1,0:T(8,128)(2,1)S(1)}, bf16[2,2,2,8,512]{4,3,2,1,0:T(8,128)(2,1)S(1)}, u32[]{:S(2)}, u32[]{:S(2)}) collective-permute-start(bf16[2,2,2,8,512]{4,3,2,1,0:T(8,128)(2,1)S(1)} %get-tuple-element.28), channel_id=1, source_target_pairs={{0,24},{2,26},{4,28},{6,30},{8,16},{10,18},{12,20},{14,22},{16,8},... | collective-permute-start | bytes 196616 | tf_op jit(solution)/shard_map/ppermute | solution.py:184
  8.2 0.2 collective-permute-start.5
  8.4 1.6 %collective-permute-start.3 = (bf16[2,2,8,512]{3,2,1,0:T(8,128)(2,1)S(1)}, bf16[2,2,8,512]{3,2,1,0:T(8,128)(2,1)S(1)}, u32[]{:S(2)}, u32[]{:S(2)}) collective-permute-start(bf16[2,2,8,512]{3,2,1,0:T(8,128)(2,1)S(1)} %get-tuple-element.30), channel_id=1, source_target_pairs={{1,0},{0,1},{3,2},{2,3},{5,4},{4,5},{7,6},{6,7},{9,8},{8,9},{11,10... | collective-permute-start | bytes 98312 | tf_op jit(solution)/shard_map/ppermute | solution.py:190
  10.0 1.4 %collective-permute-start.2 = (bf16[2,2,8,512]{3,2,1,0:T(8,128)(2,1)S(1)}, bf16[2,2,8,512]{3,2,1,0:T(8,128)(2,1)S(1)}, u32[]{:S(2)}, u32[]{:S(2)}) collective-permute-start(bf16[2,2,8,512]{3,2,1,0:T(8,128)(2,1)S(1)} %get-tuple-element.31), channel_id=1, source_target_pairs={{5,0},{4,1},{7,2},{6,3},{1,4},{0,5},{3,6},{2,7},{13,8},{12,9},{15,... | collective-permute-start | bytes 98312 | tf_op jit(solution)/shard_map/ppermute | solution.py:190
  11.4 0.0 collective-permute-done.6
  11.4 1.8 %collective-permute-done.4 = bf16[2,2,2,8,512]{4,3,2,1,0:T(8,128)(2,1)S(1)} collective-permute-done((bf16[2,2,2,8,512]{4,3,2,1,0:T(8,128)(2,1)S(1)}, bf16[2,2,2,8,512]{4,3,2,1,0:T(8,128)(2,1)S(1)}, u32[]{:S(2)}, u32[]{:S(2)}) %collective-permute-start.4) | collective-permute-done | bytes 65568 | tf_op jit(solution)/shard_map/ppermute | solution.py:184
  13.2 0.1 collective-permute-done.5
  13.4 0.0 copy-start
  13.5 2.7 %collective-permute-start.7 = (bf16[6,2,8,512]{3,2,1,0:T(8,128)(2,1)S(1)}, bf16[6,2,8,512]{3,2,1,0:T(8,128)(2,1)S(1)}, u32[]{:S(2)}, u32[]{:S(2)}) collective-permute-start(bf16[6,2,8,512]{3,2,1,0:T(8,128)(2,1)S(1)} %pad_maximum_fusion.2), channel_id=1, source_target_pairs={{5,0},{4,1},{7,2},{6,3},{1,4},{0,5},{3,6},{2,7},{13,8},{12,9},{15,... | collective-permute-start | bytes 294920 | tf_op jit(solution)/shard_map/ppermute | solution.py:190
  16.2 0.0 copy-start.1
  16.2 0.6 %collective-permute-start.9 = (bf16[6,2,8,512]{3,2,1,0:T(8,128)(2,1)S(1)}, bf16[6,2,8,512]{3,2,1,0:T(8,128)(2,1)S(1)}, u32[]{:S(2)}, u32[]{:S(2)}) collective-permute-start(bf16[6,2,8,512]{3,2,1,0:T(8,128)(2,1)S(1)} %pad_maximum_fusion.3), channel_id=1, source_target_pairs={{1,0},{0,1},{3,2},{2,3},{5,4},{4,5},{7,6},{6,7},{9,8},{8,9},{11,10... | collective-permute-start | bytes 294920 | tf_op jit(solution)/shard_map/ppermute | solution.py:190
  16.8 0.3 %collective-permute-start.8 = (bf16[8,2,8,512]{3,2,1,0:T(8,128)(2,1)S(1)}, bf16[8,2,8,512]{3,2,1,0:T(8,128)(2,1)S(1)}, u32[]{:S(2)}, u32[]{:S(2)}) collective-permute-start(bf16[8,2,8,512]{3,2,1,0:T(8,128)(2,1)S(1)} %pad_maximum_fusion.1), channel_id=1, source_target_pairs={{0,4},{2,6},{4,0},{6,2},{8,12},{10,14},{12,8},{14,10},{16,20},{18,... | collective-permute-start | bytes 393224 | tf_op jit(solution)/shard_map/ppermute | solution.py:184
  17.1 0.0 collective-permute-done.3.refs_1_
  17.1 0.0 collective-permute-done.2.refs_0_
  17.1 2.2 %collective-permute-done.7.refs_2_ = bf16[6,2,8,512]{3,2,1,0:T(8,128)(2,1)S(1)} collective-permute-done((bf16[6,2,8,512]{3,2,1,0:T(8,128)(2,1)S(1)}, bf16[6,2,8,512]{3,2,1,0:T(8,128)(2,1)S(1)}, u32[]{:S(2)}, u32[]{:S(2)}) %collective-permute-start.7) | collective-permute-done | bytes 98336 | tf_op jit(solution)/shard_map/ppermute | solution.py:190
  19.4 0.0 copy-done
  19.4 0.0 copy-done.1
  19.4 0.6 %shard_map.61 = (f32[16,512]{1,0:T(8,128)S(1)}, f32[4,128]{1,0:T(4,128)S(1)}, bf16[2,256,256]{2,1,0:T(8,128)(2,1)S(1)}) custom-call(s32[4]{0:T(128)S(1)} %copy-done.1, bf16[2,256,256]{2,1,0:T(8,128)(2,1)S(1)} %copy-done), custom_call_target="tpu_custom_call" | custom-call | flops 3000000000 | tf_op jit(solution)/shard_map/pallas_call | solution.py:90
  20.0 0.9 %collective-permute-done.9.refs_5_ = bf16[6,2,8,512]{3,2,1,0:T(8,128)(2,1)S(1)} collective-permute-done((bf16[6,2,8,512]{3,2,1,0:T(8,128)(2,1)S(1)}, bf16[6,2,8,512]{3,2,1,0:T(8,128)(2,1)S(1)}, u32[]{:S(2)}, u32[]{:S(2)}) %collective-permute-start.9) | collective-permute-done | bytes 98336 | tf_op jit(solution)/shard_map/ppermute | solution.py:190
  20.9 0.9 %collective-permute-done.8.refs_4_ = bf16[8,2,8,512]{3,2,1,0:T(8,128)(2,1)S(1)} collective-permute-done((bf16[8,2,8,512]{3,2,1,0:T(8,128)(2,1)S(1)}, bf16[8,2,8,512]{3,2,1,0:T(8,128)(2,1)S(1)}, u32[]{:S(2)}, u32[]{:S(2)}) %collective-permute-start.8) | collective-permute-done | bytes 131104 | tf_op jit(solution)/shard_map/ppermute | solution.py:184
  21.8 1.8 %shard_map.62 = (bf16[1,2,4,1,2,128,128]{6,5,4,3,2,1,0:T(8,128)(2,1)}, f32[4,1,128]{2,1,0:T(1,128)}) custom-call(f32[16,512]{1,0:T(8,128)S(1)} %get-tuple-element.19.window_ref, f32[4,128]{1,0:T(4,128)S(1)} %get-tuple-element.20.inverse_ref, bf16[2,256,256]{2,1,0:T(8,128)(2,1)S(1)} %get-tuple-element.21.stacked_ref, ...), custom_call_target="tpu_custom_call" | custom-call | tf_op jit(solution)/shard_map/pallas_call | solution.py:168
  (8 shorter events, 0.1 us)
Async XLA Ops:
  0.6 1.6 %copy-start.2 = (s32[8]{0:T(128)S(1)}, s32[8]{0:T(128)}, u32[]{:S(2)}) copy-start(s32[8]{0:T(128)} %param.5) | copy-start | bytes 100
  0.6 1.9 %collective-permute-start.1 = (bf16[16,2,8,512]{3,2,1,0:T(8,128)(2,1)}, bf16[16,2,8,512]{3,2,1,0:T(8,128)(2,1)S(1)}, u32[]{:S(2)}, u32[]{:S(2)}) collective-permute-start(bf16[16,2,8,512]{3,2,1,0:T(8,128)(2,1)} %param.4), channel_id=1, source_target_pairs={{0,2},{2,0},{4,6},{6,4},{8,10},{10,8},{12,14},{14,12},{16,18},{18,... | collective-permute-start | bytes 786440 | tf_op jit(solution)/shard_map/ppermute | solution.py:184
  1.2 1.4 %collective-permute-start = (s32[8]{0:T(128)}, s32[8]{0:T(128)S(1)}, u32[]{:S(2)}, u32[]{:S(2)}) collective-permute-start(s32[8]{0:T(128)} %param.5), channel_id=1, source_target_pairs={{0,2},{2,0},{4,6},{6,4},{8,10},{10,8},{12,14},{14,12},{16,18},{18,... | collective-permute-start | bytes 104 | tf_op jit(solution)/shard_map/ppermute | solution.py:184
  2.8 8.6 %collective-permute-start.6 = (bf16[2,2,2,8,512]{4,3,2,1,0:T(8,128)(2,1)S(1)}, bf16[2,2,2,8,512]{4,3,2,1,0:T(8,128)(2,1)S(1)}, u32[]{:S(2)}, u32[]{:S(2)}) collective-permute-start(bf16[2,2,2,8,512]{4,3,2,1,0:T(8,128)(2,1)S(1)} %get-tuple-element.26), channel_id=1, source_target_pairs={{0,16},{2,18},{4,20},{6,22},{8,24},{10,26},{12,28},{14,30},{16,0},... | collective-permute-start | bytes 196616 | tf_op jit(solution)/shard_map/ppermute | solution.py:184
  6.8 6.4 %collective-permute-start.4 = (bf16[2,2,2,8,512]{4,3,2,1,0:T(8,128)(2,1)S(1)}, bf16[2,2,2,8,512]{4,3,2,1,0:T(8,128)(2,1)S(1)}, u32[]{:S(2)}, u32[]{:S(2)}) collective-permute-start(bf16[2,2,2,8,512]{4,3,2,1,0:T(8,128)(2,1)S(1)} %get-tuple-element.28), channel_id=1, source_target_pairs={{0,24},{2,26},{4,28},{6,30},{8,16},{10,18},{12,20},{14,22},{16,8},... | collective-permute-start | bytes 196616 | tf_op jit(solution)/shard_map/ppermute | solution.py:184
  8.2 5.2 %collective-permute-start.5 = (bf16[2,2,2,8,512]{4,3,2,1,0:T(8,128)(2,1)S(1)}, bf16[2,2,2,8,512]{4,3,2,1,0:T(8,128)(2,1)S(1)}, u32[]{:S(2)}, u32[]{:S(2)}) collective-permute-start(bf16[2,2,2,8,512]{4,3,2,1,0:T(8,128)(2,1)S(1)} %get-tuple-element.29), channel_id=1, source_target_pairs={{0,8},{2,10},{4,12},{6,14},{8,0},{10,2},{12,4},{14,6},{16,24},{18,... | collective-permute-start | bytes 196616 | tf_op jit(solution)/shard_map/ppermute | solution.py:184
  8.4 8.7 %collective-permute-start.3 = (bf16[2,2,8,512]{3,2,1,0:T(8,128)(2,1)S(1)}, bf16[2,2,8,512]{3,2,1,0:T(8,128)(2,1)S(1)}, u32[]{:S(2)}, u32[]{:S(2)}) collective-permute-start(bf16[2,2,8,512]{3,2,1,0:T(8,128)(2,1)S(1)} %get-tuple-element.30), channel_id=1, source_target_pairs={{1,0},{0,1},{3,2},{2,3},{5,4},{4,5},{7,6},{6,7},{9,8},{8,9},{11,10... | collective-permute-start | bytes 98312 | tf_op jit(solution)/shard_map/ppermute | solution.py:190
  10.0 7.1 %collective-permute-start.2 = (bf16[2,2,8,512]{3,2,1,0:T(8,128)(2,1)S(1)}, bf16[2,2,8,512]{3,2,1,0:T(8,128)(2,1)S(1)}, u32[]{:S(2)}, u32[]{:S(2)}) collective-permute-start(bf16[2,2,8,512]{3,2,1,0:T(8,128)(2,1)S(1)} %get-tuple-element.31), channel_id=1, source_target_pairs={{5,0},{4,1},{7,2},{6,3},{1,4},{0,5},{3,6},{2,7},{13,8},{12,9},{15,... | collective-permute-start | bytes 98312 | tf_op jit(solution)/shard_map/ppermute | solution.py:190
  13.4 5.9 %copy-start = (bf16[2,256,256]{2,1,0:T(8,128)(2,1)S(1)}, bf16[2,256,256]{2,1,0:T(8,128)(2,1)}, u32[]{:S(2)}) copy-start(bf16[2,256,256]{2,1,0:T(8,128)(2,1)} %weight_ref) | copy-start | bytes 786436
  13.5 5.9 %collective-permute-start.7 = (bf16[6,2,8,512]{3,2,1,0:T(8,128)(2,1)S(1)}, bf16[6,2,8,512]{3,2,1,0:T(8,128)(2,1)S(1)}, u32[]{:S(2)}, u32[]{:S(2)}) collective-permute-start(bf16[6,2,8,512]{3,2,1,0:T(8,128)(2,1)S(1)} %pad_maximum_fusion.2), channel_id=1, source_target_pairs={{5,0},{4,1},{7,2},{6,3},{1,4},{0,5},{3,6},{2,7},{13,8},{12,9},{15,... | collective-permute-start | bytes 294920 | tf_op jit(solution)/shard_map/ppermute | solution.py:190
  16.2 3.2 %copy-start.1 = (s32[4]{0:T(128)S(1)}, s32[4]{0:T(128)}, u32[]{:S(2)}) copy-start(s32[4]{0:T(128)} %length_ref) | copy-start | bytes 52
  16.2 4.7 %collective-permute-start.9 = (bf16[6,2,8,512]{3,2,1,0:T(8,128)(2,1)S(1)}, bf16[6,2,8,512]{3,2,1,0:T(8,128)(2,1)S(1)}, u32[]{:S(2)}, u32[]{:S(2)}) collective-permute-start(bf16[6,2,8,512]{3,2,1,0:T(8,128)(2,1)S(1)} %pad_maximum_fusion.3), channel_id=1, source_target_pairs={{1,0},{0,1},{3,2},{2,3},{5,4},{4,5},{7,6},{6,7},{9,8},{8,9},{11,10... | collective-permute-start | bytes 294920 | tf_op jit(solution)/shard_map/ppermute | solution.py:190
  16.8 5.0 %collective-permute-start.8 = (bf16[8,2,8,512]{3,2,1,0:T(8,128)(2,1)S(1)}, bf16[8,2,8,512]{3,2,1,0:T(8,128)(2,1)S(1)}, u32[]{:S(2)}, u32[]{:S(2)}) collective-permute-start(bf16[8,2,8,512]{3,2,1,0:T(8,128)(2,1)S(1)} %pad_maximum_fusion.1), channel_id=1, source_target_pairs={{0,4},{2,6},{4,0},{6,2},{8,12},{10,14},{12,8},{14,10},{16,20},{18,... | collective-permute-start | bytes 393224 | tf_op jit(solution)/shard_map/ppermute | solution.py:184

commit v7 on v5

--- a/solution.py
+++ b/solution.py
@@ -34,13 +34,13 @@
     return cos_out, sin_out
 
 
-def rotate_kernel(step_ref, volt_ref, out_ref):
+def rotate_kernel(stride, step_ref, volt_ref, out_ref):
     slots = out_ref.shape[0]
     me = lax.axis_index("chan")
     slot = 2 * lax.broadcasted_iota(jnp.int32, step_ref.shape, 1)
     cosine, sine = phasors((step_ref[...] * jnp.bitwise_xor(slot, me)) % PHASES)
     for i in range(slots):
-        c = jnp.bitwise_xor(me, 2 * i)
+        c = jnp.bitwise_xor(me, 2 * i) // stride
         cos_c = cosine[:, i : i + 1]
         sin_c = sine[:, i : i + 1]
         real_in = volt_ref[c, 0].astype(jnp.float32)
@@ -49,11 +49,11 @@
         out_ref[i, 1] = (imag_in * cos_c - real_in * sin_c).astype(jnp.bfloat16)
 
 
-def rotate(voltages, phase_index):
-    channels, parts, rows, samples = voltages.shape
+def rotate(voltages, phase_index, channels):
+    held, parts, rows, samples = voltages.shape
     step = jnp.broadcast_to(phase_index[:, None], (rows, 128 * pl.cdiv(channels, 128)))
     return pl.pallas_call(
-        rotate_kernel,
+        functools.partial(rotate_kernel, channels // held),
         out_shape=jax.ShapeDtypeStruct((channels // 2, parts, rows, samples), jnp.bfloat16),
         in_specs=[IN_VMEM, IN_VMEM],
         out_specs=IN_VMEM,
@@ -195,8 +195,11 @@
     channels, parts, rows, samples = voltages.shape
     far = channels // 4
     pair_phase, pair_voltages = exchanged(phase_index, 1, 0), exchanged(voltages, 1, 0)
-    kept = rotate(voltages.astype(jnp.float32), phase_index)
-    swapped = rotate(pair_voltages, pair_phase)
+    sides = voltages.reshape(channels // 2, 2, parts, rows, samples)
+    side = lax.axis_index("chan") % 2
+    mine = lax.dynamic_index_in_dim(sides, side, 1, keepdims=False)
+    kept = rotate(mine.astype(jnp.float32), phase_index, channels)
+    swapped = rotate(pair_voltages, pair_phase, channels)
 
     both = jnp.stack([kept, swapped], axis=1)
     both = both.reshape(far, 2, 2, parts, rows, samples)

time: 23.7 us -> 23.7 us (level)
  transfers between devices with their start and end apart: 9 -> 9, of which waited for: 6 -> 6; matrix products, arithmetic and copies ran while one was open for 5% -> 4% of each run, Pallas kernels for 3% -> 3%
where the time goes in v7:
time: 23.7 us; the launch traced here: 23.5 us
  starting transfers between devices  12.3 us (52%)
  waiting for transfers between devices  6.69 us (28%)
  Pallas kernels  2.64 us (11%)
  other arithmetic  1.02 us (4%)
  between operations  0.73 us (3%)
    ppermute x6, starting transfers between devices, exchanged(): lax.ppermute(value, 'chan', [(c, c ^ offset) for c in range(channels)])  6.73 us
    ppermute x3, waiting for transfers between devices, exchanged(): return lax.ppermute(value, ('chan', 'stn'), pairs)  5.56 us
    ppermute x3, starting transfers between devices, exchanged(): return lax.ppermute(value, ('chan', 'stn'), pairs)  5.53 us
    pallas_call x1, Pallas kernels, finish(): pl.pallas_call(functools.partial(finish_kernel, layout), out_shape=(jax.S...  1.76 us
    ppermute x6, waiting for transfers between devices, exchanged(): lax.ppermute(value, 'chan', [(c, c ^ offset) for c in range(channels)])  1.13 us
    convert_element_type x1, other arithmetic, local(): kept = rotate(mine.astype(jnp.float32), phase_index, channels)  0.94 us
    pallas_call x1, Pallas kernels, prepare(): pl.pallas_call(prepare_kernel, out_shape=(jax.ShapeDtypeStruct((16, sampl...  0.59 us
  transfers between devices with their start and end apart: 9, of which 6 were waited for; matrix products, arithmetic and copies ran while one was open for 4% of the time, Pallas kernels for 3%

profile of v7, /device:TPU:0, one launch (start us, length us, event | category | flops | bytes accessed | tf_op | source)
XLA Modules:
  0.0 23.5 jit_solution(1864383991040085383)
XLA Ops:
  0.6 0.5 %collective-permute-start.1 = (bf16[16,2,8,512]{3,2,1,0:T(8,128)(2,1)}, bf16[16,2,8,512]{3,2,1,0:T(8,128)(2,1)S(1)}, u32[]{:S(2)}, u32[]{:S(2)}) collective-permute-start(bf16[16,2,8,512]{3,2,1,0:T(8,128)(2,1)} %param.4), channel_id=1, source_target_pairs={{0,2},{2,0},{4,6},{6,4},{8,10},{10,8},{12,14},{14,12},{16,18},{18,... | collective-permute-start | bytes 786440 | tf_op jit(solution)/shard_map/ppermute | solution.py:184
  1.1 0.1 collective-permute-start
  1.2 0.0 copy-start.2
  1.2 0.9 %bitcast_convert_fusion.volt_ref = f32[8,2,8,512]{3,2,1,0:T(8,128)S(1)} fusion(bf16[8,2,2,8,512]{4,3,2,1,0:T(8,128)(2,1)} %bitcast.30, s32[]{:T(128)S(6)} %select_n.12), kind=kLoop, calls=%fused_computation.8 | loop fusion | flops 65536 | bytes 393220 | tf_op jit(solution)/shard_map/convert_element_type | solution.py:201
  2.2 0.0 copy-done.2
  2.2 0.1 broadcast_in_dim.4.step_ref
  2.3 0.1 shard_map.59
  2.4 0.1 collective-permute-done
  2.5 0.0 collective-permute-done.1.volt_ref
  2.5 0.1 broadcast_in_dim.5.step_ref
  2.6 0.1 shard_map.60
  2.8 4.0 %collective-permute-start.5 = (bf16[2,2,2,8,512]{4,3,2,1,0:T(8,128)(2,1)S(1)}, bf16[2,2,2,8,512]{4,3,2,1,0:T(8,128)(2,1)S(1)}, u32[]{:S(2)}, u32[]{:S(2)}) collective-permute-start(bf16[2,2,2,8,512]{4,3,2,1,0:T(8,128)(2,1)S(1)} %get-tuple-element.26), channel_id=1, source_target_pairs={{0,16},{2,18},{4,20},{6,22},{8,24},{10,26},{12,28},{14,30},{16,0},... | collective-permute-start | bytes 196616 | tf_op jit(solution)/shard_map/ppermute | solution.py:184
  6.8 1.3 %collective-permute-start.3 = (bf16[2,2,2,8,512]{4,3,2,1,0:T(8,128)(2,1)S(1)}, bf16[2,2,2,8,512]{4,3,2,1,0:T(8,128)(2,1)S(1)}, u32[]{:S(2)}, u32[]{:S(2)}) collective-permute-start(bf16[2,2,2,8,512]{4,3,2,1,0:T(8,128)(2,1)S(1)} %get-tuple-element.28), channel_id=1, source_target_pairs={{0,24},{2,26},{4,28},{6,30},{8,16},{10,18},{12,20},{14,22},{16,8},... | collective-permute-start | bytes 196616 | tf_op jit(solution)/shard_map/ppermute | solution.py:184
  8.2 0.2 collective-permute-start.4
  8.4 2.4 %collective-permute-start.2 = (bf16[2,2,8,512]{3,2,1,0:T(8,128)(2,1)S(1)}, bf16[2,2,8,512]{3,2,1,0:T(8,128)(2,1)S(1)}, u32[]{:S(2)}, u32[]{:S(2)}) collective-permute-start(bf16[2,2,8,512]{3,2,1,0:T(8,128)(2,1)S(1)} %maximum_bitcast_fusion), channel_id=1, source_target_pairs={{5,0},{4,1},{7,2},{6,3},{1,4},{0,5},{3,6},{2,7},{13,8},{12,9},{15,... | collective-permute-start | bytes 98312 | tf_op jit(solution)/shard_map/ppermute | solution.py:190
  10.8 2.4 %collective-permute-done.2.refs_0_ = bf16[2,2,8,512]{3,2,1,0:T(8,128)(2,1)S(1)} collective-permute-done((bf16[2,2,8,512]{3,2,1,0:T(8,128)(2,1)S(1)}, bf16[2,2,8,512]{3,2,1,0:T(8,128)(2,1)S(1)}, u32[]{:S(2)}, u32[]{:S(2)}) %collective-permute-start.2) | collective-permute-done | bytes 32800 | tf_op jit(solution)/shard_map/ppermute | solution.py:190
  13.2 0.0 collective-permute-done.5
  13.2 0.0 collective-permute-done.3
  13.2 0.2 collective-permute-done.4
  13.4 0.0 copy-start
  13.5 2.7 %collective-permute-start.6 = (bf16[6,2,8,512]{3,2,1,0:T(8,128)(2,1)S(1)}, bf16[6,2,8,512]{3,2,1,0:T(8,128)(2,1)S(1)}, u32[]{:S(2)}, u32[]{:S(2)}) collective-permute-start(bf16[6,2,8,512]{3,2,1,0:T(8,128)(2,1)S(1)} %pad_maximum_fusion.2), channel_id=1, source_target_pairs={{5,0},{4,1},{7,2},{6,3},{1,4},{0,5},{3,6},{2,7},{13,8},{12,9},{15,... | collective-permute-start | bytes 294920 | tf_op jit(solution)/shard_map/ppermute | solution.py:190
  16.2 0.5 %collective-permute-start.7 = (bf16[8,2,8,512]{3,2,1,0:T(8,128)(2,1)S(1)}, bf16[8,2,8,512]{3,2,1,0:T(8,128)(2,1)S(1)}, u32[]{:S(2)}, u32[]{:S(2)}) collective-permute-start(bf16[8,2,8,512]{3,2,1,0:T(8,128)(2,1)S(1)} %pad_maximum_fusion.1), channel_id=1, source_target_pairs={{0,4},{2,6},{4,0},{6,2},{8,12},{10,14},{12,8},{14,10},{16,20},{18,... | collective-permute-start | bytes 393224 | tf_op jit(solution)/shard_map/ppermute | solution.py:184
  16.7 0.0 copy-start.1
  16.7 0.4 %collective-permute-start.8 = (bf16[8,2,8,512]{3,2,1,0:T(8,128)(2,1)S(1)}, bf16[8,2,8,512]{3,2,1,0:T(8,128)(2,1)S(1)}, u32[]{:S(2)}, u32[]{:S(2)}) collective-permute-start(bf16[8,2,8,512]{3,2,1,0:T(8,128)(2,1)S(1)} %pad_maximum_fusion.refs_2_), channel_id=1, source_target_pairs={{1,0},{0,1},{3,2},{2,3},{5,4},{4,5},{7,6},{6,7},{9,8},{8,9},{11,10... | collective-permute-start | bytes 393224 | tf_op jit(solution)/shard_map/ppermute | solution.py:190
  17.1 2.8 %collective-permute-done.6.refs_1_ = bf16[6,2,8,512]{3,2,1,0:T(8,128)(2,1)S(1)} collective-permute-done((bf16[6,2,8,512]{3,2,1,0:T(8,128)(2,1)S(1)}, bf16[6,2,8,512]{3,2,1,0:T(8,128)(2,1)S(1)}, u32[]{:S(2)}, u32[]{:S(2)}) %collective-permute-start.6) | collective-permute-done | bytes 98336 | tf_op jit(solution)/shard_map/ppermute | solution.py:190
  19.9 0.0 copy-done
  19.9 0.0 copy-done.1
  19.9 0.6 %shard_map.61 = (f32[16,512]{1,0:T(8,128)S(1)}, f32[4,128]{1,0:T(4,128)S(1)}, bf16[2,256,256]{2,1,0:T(8,128)(2,1)S(1)}) custom-call(s32[4]{0:T(128)S(1)} %copy-done.1, bf16[2,256,256]{2,1,0:T(8,128)(2,1)S(1)} %copy-done), custom_call_target="tpu_custom_call" | custom-call | flops 3000000000 | tf_op jit(solution)/shard_map/pallas_call | solution.py:90
  20.5 0.8 %collective-permute-done.7.refs_3_ = bf16[8,2,8,512]{3,2,1,0:T(8,128)(2,1)S(1)} collective-permute-done((bf16[8,2,8,512]{3,2,1,0:T(8,128)(2,1)S(1)}, bf16[8,2,8,512]{3,2,1,0:T(8,128)(2,1)S(1)}, u32[]{:S(2)}, u32[]{:S(2)}) %collective-permute-start.7) | collective-permute-done | bytes 131104 | tf_op jit(solution)/shard_map/ppermute | solution.py:184
  21.4 0.4 %collective-permute-done.8.refs_4_ = bf16[8,2,8,512]{3,2,1,0:T(8,128)(2,1)S(1)} collective-permute-done((bf16[8,2,8,512]{3,2,1,0:T(8,128)(2,1)S(1)}, bf16[8,2,8,512]{3,2,1,0:T(8,128)(2,1)S(1)}, u32[]{:S(2)}, u32[]{:S(2)}) %collective-permute-start.8) | collective-permute-done | bytes 131104 | tf_op jit(solution)/shard_map/ppermute | solution.py:190
  21.8 1.8 %shard_map.62 = (bf16[1,2,4,1,2,128,128]{6,5,4,3,2,1,0:T(8,128)(2,1)}, f32[4,1,128]{2,1,0:T(1,128)}) custom-call(f32[16,512]{1,0:T(8,128)S(1)} %get-tuple-element.20.window_ref, f32[4,128]{1,0:T(4,128)S(1)} %get-tuple-element.21.inverse_ref, bf16[2,256,256]{2,1,0:T(8,128)(2,1)S(1)} %get-tuple-element.22.stacked_ref, ...), custom_call_target="tpu_custom_call" | custom-call | tf_op jit(solution)/shard_map/pallas_call | solution.py:168
  (7 shorter events, 0.1 us)
Async XLA Ops:
  0.6 1.9 %collective-permute-start.1 = (bf16[16,2,8,512]{3,2,1,0:T(8,128)(2,1)}, bf16[16,2,8,512]{3,2,1,0:T(8,128)(2,1)S(1)}, u32[]{:S(2)}, u32[]{:S(2)}) collective-permute-start(bf16[16,2,8,512]{3,2,1,0:T(8,128)(2,1)} %param.4), channel_id=1, source_target_pairs={{0,2},{2,0},{4,6},{6,4},{8,10},{10,8},{12,14},{14,12},{16,18},{18,... | collective-permute-start | bytes 786440 | tf_op jit(solution)/shard_map/ppermute | solution.py:184
  1.1 1.4 %collective-permute-start = (s32[8]{0:T(128)}, s32[8]{0:T(128)S(1)}, u32[]{:S(2)}, u32[]{:S(2)}) collective-permute-start(s32[8]{0:T(128)} %param.5), channel_id=1, source_target_pairs={{0,2},{2,0},{4,6},{6,4},{8,10},{10,8},{12,14},{14,12},{16,18},{18,... | collective-permute-start | bytes 104 | tf_op jit(solution)/shard_map/ppermute | solution.py:184
  1.2 0.9 %copy-start.2 = (s32[8]{0:T(128)S(1)}, s32[8]{0:T(128)}, u32[]{:S(2)}) copy-start(s32[8]{0:T(128)} %param.5) | copy-start | bytes 100
  2.8 10.4 %collective-permute-start.5 = (bf16[2,2,2,8,512]{4,3,2,1,0:T(8,128)(2,1)S(1)}, bf16[2,2,2,8,512]{4,3,2,1,0:T(8,128)(2,1)S(1)}, u32[]{:S(2)}, u32[]{:S(2)}) collective-permute-start(bf16[2,2,2,8,512]{4,3,2,1,0:T(8,128)(2,1)S(1)} %get-tuple-element.26), channel_id=1, source_target_pairs={{0,16},{2,18},{4,20},{6,22},{8,24},{10,26},{12,28},{14,30},{16,0},... | collective-permute-start | bytes 196616 | tf_op jit(solution)/shard_map/ppermute | solution.py:184
  6.8 6.4 %collective-permute-start.3 = (bf16[2,2,2,8,512]{4,3,2,1,0:T(8,128)(2,1)S(1)}, bf16[2,2,2,8,512]{4,3,2,1,0:T(8,128)(2,1)S(1)}, u32[]{:S(2)}, u32[]{:S(2)}) collective-permute-start(bf16[2,2,2,8,512]{4,3,2,1,0:T(8,128)(2,1)S(1)} %get-tuple-element.28), channel_id=1, source_target_pairs={{0,24},{2,26},{4,28},{6,30},{8,16},{10,18},{12,20},{14,22},{16,8},... | collective-permute-start | bytes 196616 | tf_op jit(solution)/shard_map/ppermute | solution.py:184
  8.2 5.2 %collective-permute-start.4 = (bf16[2,2,2,8,512]{4,3,2,1,0:T(8,128)(2,1)S(1)}, bf16[2,2,2,8,512]{4,3,2,1,0:T(8,128)(2,1)S(1)}, u32[]{:S(2)}, u32[]{:S(2)}) collective-permute-start(bf16[2,2,2,8,512]{4,3,2,1,0:T(8,128)(2,1)S(1)} %get-tuple-element.29), channel_id=1, source_target_pairs={{0,8},{2,10},{4,12},{6,14},{8,0},{10,2},{12,4},{14,6},{16,24},{18,... | collective-permute-start | bytes 196616 | tf_op jit(solution)/shard_map/ppermute | solution.py:184
  8.4 4.8 %collective-permute-start.2 = (bf16[2,2,8,512]{3,2,1,0:T(8,128)(2,1)S(1)}, bf16[2,2,8,512]{3,2,1,0:T(8,128)(2,1)S(1)}, u32[]{:S(2)}, u32[]{:S(2)}) collective-permute-start(bf16[2,2,8,512]{3,2,1,0:T(8,128)(2,1)S(1)} %maximum_bitcast_fusion), channel_id=1, source_target_pairs={{5,0},{4,1},{7,2},{6,3},{1,4},{0,5},{3,6},{2,7},{13,8},{12,9},{15,... | collective-permute-start | bytes 98312 | tf_op jit(solution)/shard_map/ppermute | solution.py:190
  13.4 6.5 %copy-start = (bf16[2,256,256]{2,1,0:T(8,128)(2,1)S(1)}, bf16[2,256,256]{2,1,0:T(8,128)(2,1)}, u32[]{:S(2)}) copy-start(bf16[2,256,256]{2,1,0:T(8,128)(2,1)} %weight_ref) | copy-start | bytes 786436
  13.5 6.4 %collective-permute-start.6 = (bf16[6,2,8,512]{3,2,1,0:T(8,128)(2,1)S(1)}, bf16[6,2,8,512]{3,2,1,0:T(8,128)(2,1)S(1)}, u32[]{:S(2)}, u32[]{:S(2)}) collective-permute-start(bf16[6,2,8,512]{3,2,1,0:T(8,128)(2,1)S(1)} %pad_maximum_fusion.2), channel_id=1, source_target_pairs={{5,0},{4,1},{7,2},{6,3},{1,4},{0,5},{3,6},{2,7},{13,8},{12,9},{15,... | collective-permute-start | bytes 294920 | tf_op jit(solution)/shard_map/ppermute | solution.py:190
  16.2 5.2 %collective-permute-start.7 = (bf16[8,2,8,512]{3,2,1,0:T(8,128)(2,1)S(1)}, bf16[8,2,8,512]{3,2,1,0:T(8,128)(2,1)S(1)}, u32[]{:S(2)}, u32[]{:S(2)}) collective-permute-start(bf16[8,2,8,512]{3,2,1,0:T(8,128)(2,1)S(1)} %pad_maximum_fusion.1), channel_id=1, source_target_pairs={{0,4},{2,6},{4,0},{6,2},{8,12},{10,14},{12,8},{14,10},{16,20},{18,... | collective-permute-start | bytes 393224 | tf_op jit(solution)/shard_map/ppermute | solution.py:184
  16.7 3.2 %copy-start.1 = (s32[4]{0:T(128)S(1)}, s32[4]{0:T(128)}, u32[]{:S(2)}) copy-start(s32[4]{0:T(128)} %length_ref) | copy-start | bytes 52
  16.7 5.0 %collective-permute-start.8 = (bf16[8,2,8,512]{3,2,1,0:T(8,128)(2,1)S(1)}, bf16[8,2,8,512]{3,2,1,0:T(8,128)(2,1)S(1)}, u32[]{:S(2)}, u32[]{:S(2)}) collective-permute-start(bf16[8,2,8,512]{3,2,1,0:T(8,128)(2,1)S(1)} %pad_maximum_fusion.refs_2_), channel_id=1, source_target_pairs={{1,0},{0,1},{3,2},{2,3},{5,4},{4,5},{7,6},{6,7},{9,8},{8,9},{11,10... | collective-permute-start | bytes 393224 | tf_op jit(solution)/shard_map/ppermute | solution.py:190

commit v8 on v5

--- a/solution.py
+++ b/solution.py
@@ -212,7 +212,7 @@
         pieces.append(exchanged(held(1, (0,)), 2, dy))
         layout.append((1, dy, (0,)))
     order = (0, far - 1, *range(1, far - 1))
-    pieces, waited = lax.optimization_barrier((pieces, [arrived[k] for k in order]))
+    waited = lax.optimization_barrier([arrived[k] for k in order])
     arrived = [waited[order.index(k)] for k in every]
     for dy in range(1, stations):
         pieces.append(exchanged(held(1, every[1:]), 2, dy))

time: 23.7 us -> 23.7 us (level)
    ppermute x6, waiting for transfers between devices: 1.04 us -> 3.41 us  [exchanged(): lax.ppermute(value, 'chan', [(c, c ^ offset) for c in range(channels)])]
    ppermute x3, waiting for transfers between devices: 5.58 us -> 3.21 us  [exchanged(): return lax.ppermute(value, ('chan', 'stn'), pairs)]
where the time goes in v8:
time: 23.7 us; the launch traced here: 23.5 us
  starting transfers between devices  12.3 us (52%)
  waiting for transfers between devices  6.62 us (28%)
  Pallas kernels  2.63 us (11%)
  other arithmetic  1.08 us (5%)
  between operations  0.74 us (3%)
    ppermute x6, starting transfers between devices, exchanged(): lax.ppermute(value, 'chan', [(c, c ^ offset) for c in range(channels)])  6.75 us
    ppermute x3, starting transfers between devices, exchanged(): return lax.ppermute(value, ('chan', 'stn'), pairs)  5.53 us
    ppermute x6, waiting for transfers between devices, exchanged(): lax.ppermute(value, 'chan', [(c, c ^ offset) for c in range(channels)])  3.41 us
    ppermute x3, waiting for transfers between devices, exchanged(): return lax.ppermute(value, ('chan', 'stn'), pairs)  3.21 us
    pallas_call x1, Pallas kernels, finish(): pl.pallas_call(functools.partial(finish_kernel, layout), out_shape=(jax.S...  1.76 us
    convert_element_type x1, other arithmetic, local(): kept = rotate(voltages.astype(jnp.float32), phase_index)  1 us
    pallas_call x1, Pallas kernels, prepare(): pl.pallas_call(prepare_kernel, out_shape=(jax.ShapeDtypeStruct((16, sampl...  0.59 us
  transfers between devices with their start and end apart: 9, of which 6 were waited for; matrix products, arithmetic and copies ran while one was open for 5% of the time, Pallas kernels for 3%

profile of v8, /device:TPU:0, one launch (start us, length us, event | category | flops | bytes accessed | tf_op | source)
XLA Modules:
  0.0 23.5 jit_solution(1014588721738395016)
XLA Ops:
  0.6 0.0 copy-start.2
  0.6 0.5 %collective-permute-start.1 = (bf16[16,2,8,512]{3,2,1,0:T(8,128)(2,1)}, bf16[16,2,8,512]{3,2,1,0:T(8,128)(2,1)S(1)}, u32[]{:S(2)}, u32[]{:S(2)}) collective-permute-start(bf16[16,2,8,512]{3,2,1,0:T(8,128)(2,1)} %param.4), channel_id=1, source_target_pairs={{0,2},{2,0},{4,6},{6,4},{8,10},{10,8},{12,14},{14,12},{16,18},{18,... | collective-permute-start | bytes 786440 | tf_op jit(solution)/shard_map/ppermute | solution.py:184
  1.2 0.1 collective-permute-start
  1.2 1.0 %convert_element_type.3.volt_ref = f32[16,2,8,512]{3,2,1,0:T(8,128)S(1)} convert(bf16[16,2,8,512]{3,2,1,0:T(8,128)(2,1)} %param.4) | non-fusion elementwise | flops 131072 | bytes 786432 | tf_op jit(solution)/shard_map/convert_element_type | solution.py:198
  2.2 0.0 copy-done.2
  2.3 0.1 broadcast_in_dim.4.step_ref
  2.3 0.1 shard_map.59
  2.5 0.1 collective-permute-done
  2.5 0.0 collective-permute-done.1.volt_ref
  2.5 0.1 broadcast_in_dim.5.step_ref
  2.6 0.1 shard_map.60
  2.8 4.0 %collective-permute-start.5 = (bf16[2,2,2,8,512]{4,3,2,1,0:T(8,128)(2,1)S(1)}, bf16[2,2,2,8,512]{4,3,2,1,0:T(8,128)(2,1)S(1)}, u32[]{:S(2)}, u32[]{:S(2)}) collective-permute-start(bf16[2,2,2,8,512]{4,3,2,1,0:T(8,128)(2,1)S(1)} %get-tuple-element.24), channel_id=1, source_target_pairs={{0,16},{2,18},{4,20},{6,22},{8,24},{10,26},{12,28},{14,30},{16,0},... | collective-permute-start | bytes 196616 | tf_op jit(solution)/shard_map/ppermute | solution.py:184
  6.8 1.3 %collective-permute-start.3 = (bf16[2,2,2,8,512]{4,3,2,1,0:T(8,128)(2,1)S(1)}, bf16[2,2,2,8,512]{4,3,2,1,0:T(8,128)(2,1)S(1)}, u32[]{:S(2)}, u32[]{:S(2)}) collective-permute-start(bf16[2,2,2,8,512]{4,3,2,1,0:T(8,128)(2,1)S(1)} %get-tuple-element.26), channel_id=1, source_target_pairs={{0,24},{2,26},{4,28},{6,30},{8,16},{10,18},{12,20},{14,22},{16,8},... | collective-permute-start | bytes 196616 | tf_op jit(solution)/shard_map/ppermute | solution.py:184
  8.2 0.2 collective-permute-start.4
  8.4 2.4 %collective-permute-start.2 = (bf16[2,2,8,512]{3,2,1,0:T(8,128)(2,1)S(1)}, bf16[2,2,8,512]{3,2,1,0:T(8,128)(2,1)S(1)}, u32[]{:S(2)}, u32[]{:S(2)}) collective-permute-start(bf16[2,2,8,512]{3,2,1,0:T(8,128)(2,1)S(1)} %maximum_bitcast_fusion), channel_id=1, source_target_pairs={{5,0},{4,1},{7,2},{6,3},{1,4},{0,5},{3,6},{2,7},{13,8},{12,9},{15,... | collective-permute-start | bytes 98312 | tf_op jit(solution)/shard_map/ppermute | solution.py:190
  10.9 0.0 collective-permute-done.5
  10.9 2.4 %collective-permute-done.3 = bf16[2,2,2,8,512]{4,3,2,1,0:T(8,128)(2,1)S(1)} collective-permute-done((bf16[2,2,2,8,512]{4,3,2,1,0:T(8,128)(2,1)S(1)}, bf16[2,2,2,8,512]{4,3,2,1,0:T(8,128)(2,1)S(1)}, u32[]{:S(2)}, u32[]{:S(2)}) %collective-permute-start.3) | collective-permute-done | bytes 65568 | tf_op jit(solution)/shard_map/ppermute | solution.py:184
  13.2 0.1 collective-permute-done.4
  13.4 0.0 copy-start
  13.5 2.7 %collective-permute-start.6 = (bf16[6,2,8,512]{3,2,1,0:T(8,128)(2,1)S(1)}, bf16[6,2,8,512]{3,2,1,0:T(8,128)(2,1)S(1)}, u32[]{:S(2)}, u32[]{:S(2)}) collective-permute-start(bf16[6,2,8,512]{3,2,1,0:T(8,128)(2,1)S(1)} %pad_maximum_fusion.2), channel_id=1, source_target_pairs={{5,0},{4,1},{7,2},{6,3},{1,4},{0,5},{3,6},{2,7},{13,8},{12,9},{15,... | collective-permute-start | bytes 294920 | tf_op jit(solution)/shard_map/ppermute | solution.py:190
  16.2 0.5 %collective-permute-start.7 = (bf16[8,2,8,512]{3,2,1,0:T(8,128)(2,1)S(1)}, bf16[8,2,8,512]{3,2,1,0:T(8,128)(2,1)S(1)}, u32[]{:S(2)}, u32[]{:S(2)}) collective-permute-start(bf16[8,2,8,512]{3,2,1,0:T(8,128)(2,1)S(1)} %pad_maximum_fusion.1), channel_id=1, source_target_pairs={{0,4},{2,6},{4,0},{6,2},{8,12},{10,14},{12,8},{14,10},{16,20},{18,... | collective-permute-start | bytes 393224 | tf_op jit(solution)/shard_map/ppermute | solution.py:184
  16.7 0.0 copy-start.1
  16.7 0.4 %collective-permute-start.8 = (bf16[8,2,8,512]{3,2,1,0:T(8,128)(2,1)S(1)}, bf16[8,2,8,512]{3,2,1,0:T(8,128)(2,1)S(1)}, u32[]{:S(2)}, u32[]{:S(2)}) collective-permute-start(bf16[8,2,8,512]{3,2,1,0:T(8,128)(2,1)S(1)} %pad_maximum_fusion.refs_2_), channel_id=1, source_target_pairs={{1,0},{0,1},{3,2},{2,3},{5,4},{4,5},{7,6},{6,7},{9,8},{8,9},{11,10... | collective-permute-start | bytes 393224 | tf_op jit(solution)/shard_map/ppermute | solution.py:190
  17.1 0.0 collective-permute-done.2.refs_0_
  17.1 2.8 %collective-permute-done.6.refs_1_ = bf16[6,2,8,512]{3,2,1,0:T(8,128)(2,1)S(1)} collective-permute-done((bf16[6,2,8,512]{3,2,1,0:T(8,128)(2,1)S(1)}, bf16[6,2,8,512]{3,2,1,0:T(8,128)(2,1)S(1)}, u32[]{:S(2)}, u32[]{:S(2)}) %collective-permute-start.6) | collective-permute-done | bytes 98336 | tf_op jit(solution)/shard_map/ppermute | solution.py:190
  19.9 0.0 copy-done
  19.9 0.0 copy-done.1
  19.9 0.6 %shard_map.61 = (f32[16,512]{1,0:T(8,128)S(1)}, f32[4,128]{1,0:T(4,128)S(1)}, bf16[2,256,256]{2,1,0:T(8,128)(2,1)S(1)}) custom-call(s32[4]{0:T(128)S(1)} %copy-done.1, bf16[2,256,256]{2,1,0:T(8,128)(2,1)S(1)} %copy-done), custom_call_target="tpu_custom_call" | custom-call | flops 3000000000 | tf_op jit(solution)/shard_map/pallas_call | solution.py:90
  20.5 0.8 %collective-permute-done.7.refs_3_ = bf16[8,2,8,512]{3,2,1,0:T(8,128)(2,1)S(1)} collective-permute-done((bf16[8,2,8,512]{3,2,1,0:T(8,128)(2,1)S(1)}, bf16[8,2,8,512]{3,2,1,0:T(8,128)(2,1)S(1)}, u32[]{:S(2)}, u32[]{:S(2)}) %collective-permute-start.7) | collective-permute-done | bytes 131104 | tf_op jit(solution)/shard_map/ppermute | solution.py:184
  21.3 0.4 %collective-permute-done.8.refs_4_ = bf16[8,2,8,512]{3,2,1,0:T(8,128)(2,1)S(1)} collective-permute-done((bf16[8,2,8,512]{3,2,1,0:T(8,128)(2,1)S(1)}, bf16[8,2,8,512]{3,2,1,0:T(8,128)(2,1)S(1)}, u32[]{:S(2)}, u32[]{:S(2)}) %collective-permute-start.8) | collective-permute-done | bytes 131104 | tf_op jit(solution)/shard_map/ppermute | solution.py:190
  21.8 1.8 %shard_map.62 = (bf16[1,2,4,1,2,128,128]{6,5,4,3,2,1,0:T(8,128)(2,1)}, f32[4,1,128]{2,1,0:T(1,128)}) custom-call(f32[16,512]{1,0:T(8,128)S(1)} %get-tuple-element.18.window_ref, f32[4,128]{1,0:T(4,128)S(1)} %get-tuple-element.19.inverse_ref, bf16[2,256,256]{2,1,0:T(8,128)(2,1)S(1)} %get-tuple-element.20.stacked_ref, ...), custom_call_target="tpu_custom_call" | custom-call | tf_op jit(solution)/shard_map/pallas_call | solution.py:168
  (7 shorter events, 0.1 us)
Async XLA Ops:
  0.6 1.6 %copy-start.2 = (s32[8]{0:T(128)S(1)}, s32[8]{0:T(128)}, u32[]{:S(2)}) copy-start(s32[8]{0:T(128)} %param.5) | copy-start | bytes 100
  0.6 1.9 %collective-permute-start.1 = (bf16[16,2,8,512]{3,2,1,0:T(8,128)(2,1)}, bf16[16,2,8,512]{3,2,1,0:T(8,128)(2,1)S(1)}, u32[]{:S(2)}, u32[]{:S(2)}) collective-permute-start(bf16[16,2,8,512]{3,2,1,0:T(8,128)(2,1)} %param.4), channel_id=1, source_target_pairs={{0,2},{2,0},{4,6},{6,4},{8,10},{10,8},{12,14},{14,12},{16,18},{18,... | collective-permute-start | bytes 786440 | tf_op jit(solution)/shard_map/ppermute | solution.py:184
  1.2 1.4 %collective-permute-start = (s32[8]{0:T(128)}, s32[8]{0:T(128)S(1)}, u32[]{:S(2)}, u32[]{:S(2)}) collective-permute-start(s32[8]{0:T(128)} %param.5), channel_id=1, source_target_pairs={{0,2},{2,0},{4,6},{6,4},{8,10},{10,8},{12,14},{14,12},{16,18},{18,... | collective-permute-start | bytes 104 | tf_op jit(solution)/shard_map/ppermute | solution.py:184
  2.8 8.1 %collective-permute-start.5 = (bf16[2,2,2,8,512]{4,3,2,1,0:T(8,128)(2,1)S(1)}, bf16[2,2,2,8,512]{4,3,2,1,0:T(8,128)(2,1)S(1)}, u32[]{:S(2)}, u32[]{:S(2)}) collective-permute-start(bf16[2,2,2,8,512]{4,3,2,1,0:T(8,128)(2,1)S(1)} %get-tuple-element.24), channel_id=1, source_target_pairs={{0,16},{2,18},{4,20},{6,22},{8,24},{10,26},{12,28},{14,30},{16,0},... | collective-permute-start | bytes 196616 | tf_op jit(solution)/shard_map/ppermute | solution.py:184
  6.8 6.4 %collective-permute-start.3 = (bf16[2,2,2,8,512]{4,3,2,1,0:T(8,128)(2,1)S(1)}, bf16[2,2,2,8,512]{4,3,2,1,0:T(8,128)(2,1)S(1)}, u32[]{:S(2)}, u32[]{:S(2)}) collective-permute-start(bf16[2,2,2,8,512]{4,3,2,1,0:T(8,128)(2,1)S(1)} %get-tuple-element.26), channel_id=1, source_target_pairs={{0,24},{2,26},{4,28},{6,30},{8,16},{10,18},{12,20},{14,22},{16,8},... | collective-permute-start | bytes 196616 | tf_op jit(solution)/shard_map/ppermute | solution.py:184
  8.2 5.2 %collective-permute-start.4 = (bf16[2,2,2,8,512]{4,3,2,1,0:T(8,128)(2,1)S(1)}, bf16[2,2,2,8,512]{4,3,2,1,0:T(8,128)(2,1)S(1)}, u32[]{:S(2)}, u32[]{:S(2)}) collective-permute-start(bf16[2,2,2,8,512]{4,3,2,1,0:T(8,128)(2,1)S(1)} %get-tuple-element.27), channel_id=1, source_target_pairs={{0,8},{2,10},{4,12},{6,14},{8,0},{10,2},{12,4},{14,6},{16,24},{18,... | collective-permute-start | bytes 196616 | tf_op jit(solution)/shard_map/ppermute | solution.py:184
  8.4 8.7 %collective-permute-start.2 = (bf16[2,2,8,512]{3,2,1,0:T(8,128)(2,1)S(1)}, bf16[2,2,8,512]{3,2,1,0:T(8,128)(2,1)S(1)}, u32[]{:S(2)}, u32[]{:S(2)}) collective-permute-start(bf16[2,2,8,512]{3,2,1,0:T(8,128)(2,1)S(1)} %maximum_bitcast_fusion), channel_id=1, source_target_pairs={{5,0},{4,1},{7,2},{6,3},{1,4},{0,5},{3,6},{2,7},{13,8},{12,9},{15,... | collective-permute-start | bytes 98312 | tf_op jit(solution)/shard_map/ppermute | solution.py:190
  13.4 6.5 %copy-start = (bf16[2,256,256]{2,1,0:T(8,128)(2,1)S(1)}, bf16[2,256,256]{2,1,0:T(8,128)(2,1)}, u32[]{:S(2)}) copy-start(bf16[2,256,256]{2,1,0:T(8,128)(2,1)} %weight_ref) | copy-start | bytes 786436
  13.5 6.4 %collective-permute-start.6 = (bf16[6,2,8,512]{3,2,1,0:T(8,128)(2,1)S(1)}, bf16[6,2,8,512]{3,2,1,0:T(8,128)(2,1)S(1)}, u32[]{:S(2)}, u32[]{:S(2)}) collective-permute-start(bf16[6,2,8,512]{3,2,1,0:T(8,128)(2,1)S(1)} %pad_maximum_fusion.2), channel_id=1, source_target_pairs={{5,0},{4,1},{7,2},{6,3},{1,4},{0,5},{3,6},{2,7},{13,8},{12,9},{15,... | collective-permute-start | bytes 294920 | tf_op jit(solution)/shard_map/ppermute | solution.py:190
  16.2 5.2 %collective-permute-start.7 = (bf16[8,2,8,512]{3,2,1,0:T(8,128)(2,1)S(1)}, bf16[8,2,8,512]{3,2,1,0:T(8,128)(2,1)S(1)}, u32[]{:S(2)}, u32[]{:S(2)}) collective-permute-start(bf16[8,2,8,512]{3,2,1,0:T(8,128)(2,1)S(1)} %pad_maximum_fusion.1), channel_id=1, source_target_pairs={{0,4},{2,6},{4,0},{6,2},{8,12},{10,14},{12,8},{14,10},{16,20},{18,... | collective-permute-start | bytes 393224 | tf_op jit(solution)/shard_map/ppermute | solution.py:184
  16.7 3.2 %copy-start.1 = (s32[4]{0:T(128)S(1)}, s32[4]{0:T(128)}, u32[]{:S(2)}) copy-start(s32[4]{0:T(128)} %length_ref) | copy-start | bytes 52
  16.7 5.0 %collective-permute-start.8 = (bf16[8,2,8,512]{3,2,1,0:T(8,128)(2,1)S(1)}, bf16[8,2,8,512]{3,2,1,0:T(8,128)(2,1)S(1)}, u32[]{:S(2)}, u32[]{:S(2)}) collective-permute-start(bf16[8,2,8,512]{3,2,1,0:T(8,128)(2,1)S(1)} %pad_maximum_fusion.refs_2_), channel_id=1, source_target_pairs={{1,0},{0,1},{3,2},{2,3},{5,4},{4,5},{7,6},{6,7},{9,8},{8,9},{11,10... | collective-permute-start | bytes 393224 | tf_op jit(solution)/shard_map/ppermute | solution.py:190

commit v9 on v6

--- a/solution.py
+++ b/solution.py
@@ -212,6 +212,8 @@
         for dx in (1, 0):
             pieces.append(exchanged(held(dx, (0,)), 2 * dx, dy))
             layout.append((dx, dy, (0,)))
+    pieces.append(exchanged(held(1, (0,)), 2, 0))
+    layout.append((1, 0, (0,)))
     order = (0, far - 1, *range(1, far - 1))
     waited = lax.optimization_barrier([arrived[k] for k in order])
     arrived = [waited[order.index(k)] for k in every]
@@ -224,7 +226,7 @@
     prepared = prepare(int_lengths, beam_weights, stations, channels * rows, samples)
     for dy in range(stations):
         for dx in range(1 if dy else 2):
-            ks = every[1:] if dy else every
+            ks = every[1:] if dx or dy else every
             piece = held(dx, ks)
             pieces.append(exchanged(piece, 2 * dx, dy) if dx or dy else piece)
             layout.append((dx, dy, ks))

time: 23.7 us -> 23.7 us (level)
  starting transfers between devices: 12.8 us -> 15 us
  waiting for transfers between devices: 6.02 us -> 3.83 us
    ppermute x6 -> x7, starting transfers between devices: 6.55 us -> 9.39 us  [exchanged(): lax.ppermute(value, 'chan', [(c, c ^ offset) for c in range(channels)])]
    ppermute x6 -> x7, waiting for transfers between devices: 2.86 us -> 0.08 us  [exchanged(): lax.ppermute(value, 'chan', [(c, c ^ offset) for c in range(channels)])]
    ppermute x4, starting transfers between devices: 6.29 us -> 5.63 us  [exchanged(): return lax.ppermute(value, ('chan', 'stn'), pairs)]
    ppermute x4, waiting for transfers between devices: 3.16 us -> 3.75 us  [exchanged(): return lax.ppermute(value, ('chan', 'stn'), pairs)]
  transfers between devices with their start and end apart: 10 -> 11, of which waited for: 6 -> 3; matrix products, arithmetic and copies ran while one was open for 5% -> 5% of each run, Pallas kernels for 3% -> 3%
where the time goes in v9:
time: 23.7 us; the launch traced here: 23.5 us
  starting transfers between devices  15 us (63%)
  waiting for transfers between devices  3.83 us (16%)
  Pallas kernels  2.64 us (11%)
  other arithmetic  1.08 us (5%)
  between operations  0.75 us (3%)
    ppermute x7, starting transfers between devices, exchanged(): lax.ppermute(value, 'chan', [(c, c ^ offset) for c in range(channels)])  9.39 us
    ppermute x4, starting transfers between devices, exchanged(): return lax.ppermute(value, ('chan', 'stn'), pairs)  5.63 us
    ppermute x4, waiting for transfers between devices, exchanged(): return lax.ppermute(value, ('chan', 'stn'), pairs)  3.75 us
    pallas_call x1, Pallas kernels, finish(): pl.pallas_call(functools.partial(finish_kernel, layout), out_shape=(jax.S...  1.76 us
    convert_element_type x1, other arithmetic, local(): kept = rotate(voltages.astype(jnp.float32), phase_index)  1 us
    pallas_call x1, Pallas kernels, prepare(): pl.pallas_call(prepare_kernel, out_shape=(jax.ShapeDtypeStruct((16, sampl...  0.59 us
  transfers between devices with their start and end apart: 11, of which 3 were waited for; matrix products, arithmetic and copies ran while one was open for 5% of the time, Pallas kernels for 3%

profile of v9, /device:TPU:0, one launch (start us, length us, event | category | flops | bytes accessed | tf_op | source)
XLA Modules:
  0.0 23.5 jit_solution(11772513557546788867)
XLA Ops:
  0.6 0.0 copy-start.2
  0.6 0.5 %collective-permute-start.1 = (bf16[16,2,8,512]{3,2,1,0:T(8,128)(2,1)}, bf16[16,2,8,512]{3,2,1,0:T(8,128)(2,1)S(1)}, u32[]{:S(2)}, u32[]{:S(2)}) collective-permute-start(bf16[16,2,8,512]{3,2,1,0:T(8,128)(2,1)} %param.4), channel_id=1, source_target_pairs={{0,2},{2,0},{4,6},{6,4},{8,10},{10,8},{12,14},{14,12},{16,18},{18,... | collective-permute-start | bytes 786440 | tf_op jit(solution)/shard_map/ppermute | solution.py:184
  1.2 0.1 collective-permute-start
  1.2 1.0 %convert_element_type.3.volt_ref = f32[16,2,8,512]{3,2,1,0:T(8,128)S(1)} convert(bf16[16,2,8,512]{3,2,1,0:T(8,128)(2,1)} %param.4) | non-fusion elementwise | flops 131072 | bytes 786432 | tf_op jit(solution)/shard_map/convert_element_type | solution.py:198
  2.2 0.0 copy-done.2
  2.3 0.1 broadcast_in_dim.4.step_ref
  2.3 0.1 shard_map.59
  2.5 0.1 collective-permute-done
  2.5 0.0 collective-permute-done.1.volt_ref
  2.5 0.1 broadcast_in_dim.5.step_ref
  2.6 0.1 shard_map.60
  2.8 4.0 %collective-permute-start.7 = (bf16[2,2,2,8,512]{4,3,2,1,0:T(8,128)(2,1)S(1)}, bf16[2,2,2,8,512]{4,3,2,1,0:T(8,128)(2,1)S(1)}, u32[]{:S(2)}, u32[]{:S(2)}) collective-permute-start(bf16[2,2,2,8,512]{4,3,2,1,0:T(8,128)(2,1)S(1)} %get-tuple-element.28), channel_id=1, source_target_pairs={{0,16},{2,18},{4,20},{6,22},{8,24},{10,26},{12,28},{14,30},{16,0},... | collective-permute-start | bytes 196616 | tf_op jit(solution)/shard_map/ppermute | solution.py:184
  6.8 1.3 %collective-permute-start.5 = (bf16[2,2,2,8,512]{4,3,2,1,0:T(8,128)(2,1)S(1)}, bf16[2,2,2,8,512]{4,3,2,1,0:T(8,128)(2,1)S(1)}, u32[]{:S(2)}, u32[]{:S(2)}) collective-permute-start(bf16[2,2,2,8,512]{4,3,2,1,0:T(8,128)(2,1)S(1)} %get-tuple-element.30), channel_id=1, source_target_pairs={{0,24},{2,26},{4,28},{6,30},{8,16},{10,18},{12,20},{14,22},{16,8},... | collective-permute-start | bytes 196616 | tf_op jit(solution)/shard_map/ppermute | solution.py:184
  8.2 0.2 collective-permute-start.6
  8.4 1.6 %collective-permute-start.4 = (bf16[2,2,8,512]{3,2,1,0:T(8,128)(2,1)S(1)}, bf16[2,2,8,512]{3,2,1,0:T(8,128)(2,1)S(1)}, u32[]{:S(2)}, u32[]{:S(2)}) collective-permute-start(bf16[2,2,8,512]{3,2,1,0:T(8,128)(2,1)S(1)} %get-tuple-element.33), channel_id=1, source_target_pairs={{0,4},{2,6},{4,0},{6,2},{8,12},{10,14},{12,8},{14,10},{16,20},{18,... | collective-permute-start | bytes 98312 | tf_op jit(solution)/shard_map/ppermute | solution.py:184
  10.0 1.5 %collective-permute-start.2 = (bf16[2,2,8,512]{3,2,1,0:T(8,128)(2,1)S(1)}, bf16[2,2,8,512]{3,2,1,0:T(8,128)(2,1)S(1)}, u32[]{:S(2)}, u32[]{:S(2)}) collective-permute-start(bf16[2,2,8,512]{3,2,1,0:T(8,128)(2,1)S(1)} %get-tuple-element.33), channel_id=1, source_target_pairs={{5,0},{4,1},{7,2},{6,3},{1,4},{0,5},{3,6},{2,7},{13,8},{12,9},{15,... | collective-permute-start | bytes 98312 | tf_op jit(solution)/shard_map/ppermute | solution.py:190
  11.5 0.0 collective-permute-done.7
  11.5 2.0 %collective-permute-start.3 = (bf16[2,2,8,512]{3,2,1,0:T(8,128)(2,1)S(1)}, bf16[2,2,8,512]{3,2,1,0:T(8,128)(2,1)S(1)}, u32[]{:S(2)}, u32[]{:S(2)}) collective-permute-start(bf16[2,2,8,512]{3,2,1,0:T(8,128)(2,1)S(1)} %get-tuple-element.32), channel_id=1, source_target_pairs={{1,0},{0,1},{3,2},{2,3},{5,4},{4,5},{7,6},{6,7},{9,8},{8,9},{11,10... | collective-permute-start | bytes 98312 | tf_op jit(solution)/shard_map/ppermute | solution.py:190
  13.5 0.0 collective-permute-done.5
  13.5 0.0 collective-permute-done.6
  13.5 0.0 copy-start
  13.5 1.6 %collective-permute-start.9 = (bf16[6,2,8,512]{3,2,1,0:T(8,128)(2,1)S(1)}, bf16[6,2,8,512]{3,2,1,0:T(8,128)(2,1)S(1)}, u32[]{:S(2)}, u32[]{:S(2)}) collective-permute-start(bf16[6,2,8,512]{3,2,1,0:T(8,128)(2,1)S(1)} %pad_maximum_fusion.1), channel_id=1, source_target_pairs={{0,4},{2,6},{4,0},{6,2},{8,12},{10,14},{12,8},{14,10},{16,20},{18,... | collective-permute-start | bytes 294920 | tf_op jit(solution)/shard_map/ppermute | solution.py:184
  15.2 1.5 %collective-permute-start.8 = (bf16[6,2,8,512]{3,2,1,0:T(8,128)(2,1)S(1)}, bf16[6,2,8,512]{3,2,1,0:T(8,128)(2,1)S(1)}, u32[]{:S(2)}, u32[]{:S(2)}) collective-permute-start(bf16[6,2,8,512]{3,2,1,0:T(8,128)(2,1)S(1)} %pad_maximum_fusion.1), channel_id=1, source_target_pairs={{5,0},{4,1},{7,2},{6,3},{1,4},{0,5},{3,6},{2,7},{13,8},{12,9},{15,... | collective-permute-start | bytes 294920 | tf_op jit(solution)/shard_map/ppermute | solution.py:190
  16.7 0.0 copy-start.1
  16.7 0.0 collective-permute-done.3.refs_1_
  16.7 0.6 %collective-permute-start.10 = (bf16[6,2,8,512]{3,2,1,0:T(8,128)(2,1)S(1)}, bf16[6,2,8,512]{3,2,1,0:T(8,128)(2,1)S(1)}, u32[]{:S(2)}, u32[]{:S(2)}) collective-permute-start(bf16[6,2,8,512]{3,2,1,0:T(8,128)(2,1)S(1)} %pad_maximum_fusion.2), channel_id=1, source_target_pairs={{1,0},{0,1},{3,2},{2,3},{5,4},{4,5},{7,6},{6,7},{9,8},{8,9},{11,10... | collective-permute-start | bytes 294920 | tf_op jit(solution)/shard_map/ppermute | solution.py:190
  17.4 0.0 collective-permute-done.4.refs_2_
  17.4 0.0 collective-permute-done.2.refs_0_
  17.4 3.3 %collective-permute-done.8.refs_3_ = bf16[6,2,8,512]{3,2,1,0:T(8,128)(2,1)S(1)} collective-permute-done((bf16[6,2,8,512]{3,2,1,0:T(8,128)(2,1)S(1)}, bf16[6,2,8,512]{3,2,1,0:T(8,128)(2,1)S(1)}, u32[]{:S(2)}, u32[]{:S(2)}) %collective-permute-start.8) | collective-permute-done | bytes 98336 | tf_op jit(solution)/shard_map/ppermute | solution.py:190
  20.7 0.0 copy-done
  20.7 0.0 copy-done.1
  20.7 0.6 %shard_map.61 = (f32[16,512]{1,0:T(8,128)S(1)}, f32[4,128]{1,0:T(4,128)S(1)}, bf16[2,256,256]{2,1,0:T(8,128)(2,1)S(1)}) custom-call(s32[4]{0:T(128)S(1)} %copy-done.1, bf16[2,256,256]{2,1,0:T(8,128)(2,1)S(1)} %copy-done), custom_call_target="tpu_custom_call" | custom-call | flops 3000000000 | tf_op jit(solution)/shard_map/pallas_call | solution.py:90
  21.3 0.4 %collective-permute-done.10.refs_6_ = bf16[6,2,8,512]{3,2,1,0:T(8,128)(2,1)S(1)} collective-permute-done((bf16[6,2,8,512]{3,2,1,0:T(8,128)(2,1)S(1)}, bf16[6,2,8,512]{3,2,1,0:T(8,128)(2,1)S(1)}, u32[]{:S(2)}, u32[]{:S(2)}) %collective-permute-start.10) | collective-permute-done | bytes 98336 | tf_op jit(solution)/shard_map/ppermute | solution.py:190
  21.7 0.0 collective-permute-done.9.refs_5_
  21.7 1.8 %shard_map.62 = (bf16[1,2,4,1,2,128,128]{6,5,4,3,2,1,0:T(8,128)(2,1)}, f32[4,1,128]{2,1,0:T(1,128)}) custom-call(f32[16,512]{1,0:T(8,128)S(1)} %get-tuple-element.20.window_ref, f32[4,128]{1,0:T(4,128)S(1)} %get-tuple-element.21.inverse_ref, bf16[2,256,256]{2,1,0:T(8,128)(2,1)S(1)} %get-tuple-element.22.stacked_ref, ...), custom_call_target="tpu_custom_call" | custom-call | tf_op jit(solution)/shard_map/pallas_call | solution.py:168
  (8 shorter events, 0.1 us)
Async XLA Ops:
  0.6 1.6 %copy-start.2 = (s32[8]{0:T(128)S(1)}, s32[8]{0:T(128)}, u32[]{:S(2)}) copy-start(s32[8]{0:T(128)} %param.5) | copy-start | bytes 100
  0.6 1.9 %collective-permute-start.1 = (bf16[16,2,8,512]{3,2,1,0:T(8,128)(2,1)}, bf16[16,2,8,512]{3,2,1,0:T(8,128)(2,1)S(1)}, u32[]{:S(2)}, u32[]{:S(2)}) collective-permute-start(bf16[16,2,8,512]{3,2,1,0:T(8,128)(2,1)} %param.4), channel_id=1, source_target_pairs={{0,2},{2,0},{4,6},{6,4},{8,10},{10,8},{12,14},{14,12},{16,18},{18,... | collective-permute-start | bytes 786440 | tf_op jit(solution)/shard_map/ppermute | solution.py:184
  1.2 1.4 %collective-permute-start = (s32[8]{0:T(128)}, s32[8]{0:T(128)S(1)}, u32[]{:S(2)}, u32[]{:S(2)}) collective-permute-start(s32[8]{0:T(128)} %param.5), channel_id=1, source_target_pairs={{0,2},{2,0},{4,6},{6,4},{8,10},{10,8},{12,14},{14,12},{16,18},{18,... | collective-permute-start | bytes 104 | tf_op jit(solution)/shard_map/ppermute | solution.py:184
  2.8 8.7 %collective-permute-start.7 = (bf16[2,2,2,8,512]{4,3,2,1,0:T(8,128)(2,1)S(1)}, bf16[2,2,2,8,512]{4,3,2,1,0:T(8,128)(2,1)S(1)}, u32[]{:S(2)}, u32[]{:S(2)}) collective-permute-start(bf16[2,2,2,8,512]{4,3,2,1,0:T(8,128)(2,1)S(1)} %get-tuple-element.28), channel_id=1, source_target_pairs={{0,16},{2,18},{4,20},{6,22},{8,24},{10,26},{12,28},{14,30},{16,0},... | collective-permute-start | bytes 196616 | tf_op jit(solution)/shard_map/ppermute | solution.py:184
  6.8 6.6 %collective-permute-start.5 = (bf16[2,2,2,8,512]{4,3,2,1,0:T(8,128)(2,1)S(1)}, bf16[2,2,2,8,512]{4,3,2,1,0:T(8,128)(2,1)S(1)}, u32[]{:S(2)}, u32[]{:S(2)}) collective-permute-start(bf16[2,2,2,8,512]{4,3,2,1,0:T(8,128)(2,1)S(1)} %get-tuple-element.30), channel_id=1, source_target_pairs={{0,24},{2,26},{4,28},{6,30},{8,16},{10,18},{12,20},{14,22},{16,8},... | collective-permute-start | bytes 196616 | tf_op jit(solution)/shard_map/ppermute | solution.py:184
  8.2 5.3 %collective-permute-start.6 = (bf16[2,2,2,8,512]{4,3,2,1,0:T(8,128)(2,1)S(1)}, bf16[2,2,2,8,512]{4,3,2,1,0:T(8,128)(2,1)S(1)}, u32[]{:S(2)}, u32[]{:S(2)}) collective-permute-start(bf16[2,2,2,8,512]{4,3,2,1,0:T(8,128)(2,1)S(1)} %get-tuple-element.31), channel_id=1, source_target_pairs={{0,8},{2,10},{4,12},{6,14},{8,0},{10,2},{12,4},{14,6},{16,24},{18,... | collective-permute-start | bytes 196616 | tf_op jit(solution)/shard_map/ppermute | solution.py:184
  8.4 9.0 %collective-permute-start.4 = (bf16[2,2,8,512]{3,2,1,0:T(8,128)(2,1)S(1)}, bf16[2,2,8,512]{3,2,1,0:T(8,128)(2,1)S(1)}, u32[]{:S(2)}, u32[]{:S(2)}) collective-permute-start(bf16[2,2,8,512]{3,2,1,0:T(8,128)(2,1)S(1)} %get-tuple-element.33), channel_id=1, source_target_pairs={{0,4},{2,6},{4,0},{6,2},{8,12},{10,14},{12,8},{14,10},{16,20},{18,... | collective-permute-start | bytes 98312 | tf_op jit(solution)/shard_map/ppermute | solution.py:184
  10.0 7.4 %collective-permute-start.2 = (bf16[2,2,8,512]{3,2,1,0:T(8,128)(2,1)S(1)}, bf16[2,2,8,512]{3,2,1,0:T(8,128)(2,1)S(1)}, u32[]{:S(2)}, u32[]{:S(2)}) collective-permute-start(bf16[2,2,8,512]{3,2,1,0:T(8,128)(2,1)S(1)} %get-tuple-element.33), channel_id=1, source_target_pairs={{5,0},{4,1},{7,2},{6,3},{1,4},{0,5},{3,6},{2,7},{13,8},{12,9},{15,... | collective-permute-start | bytes 98312 | tf_op jit(solution)/shard_map/ppermute | solution.py:190
  11.5 5.3 %collective-permute-start.3 = (bf16[2,2,8,512]{3,2,1,0:T(8,128)(2,1)S(1)}, bf16[2,2,8,512]{3,2,1,0:T(8,128)(2,1)S(1)}, u32[]{:S(2)}, u32[]{:S(2)}) collective-permute-start(bf16[2,2,8,512]{3,2,1,0:T(8,128)(2,1)S(1)} %get-tuple-element.32), channel_id=1, source_target_pairs={{1,0},{0,1},{3,2},{2,3},{5,4},{4,5},{7,6},{6,7},{9,8},{8,9},{11,10... | collective-permute-start | bytes 98312 | tf_op jit(solution)/shard_map/ppermute | solution.py:190
  13.5 7.2 %copy-start = (bf16[2,256,256]{2,1,0:T(8,128)(2,1)S(1)}, bf16[2,256,256]{2,1,0:T(8,128)(2,1)}, u32[]{:S(2)}) copy-start(bf16[2,256,256]{2,1,0:T(8,128)(2,1)} %weight_ref) | copy-start | bytes 786436
  13.5 8.2 %collective-permute-start.9 = (bf16[6,2,8,512]{3,2,1,0:T(8,128)(2,1)S(1)}, bf16[6,2,8,512]{3,2,1,0:T(8,128)(2,1)S(1)}, u32[]{:S(2)}, u32[]{:S(2)}) collective-permute-start(bf16[6,2,8,512]{3,2,1,0:T(8,128)(2,1)S(1)} %pad_maximum_fusion.1), channel_id=1, source_target_pairs={{0,4},{2,6},{4,0},{6,2},{8,12},{10,14},{12,8},{14,10},{16,20},{18,... | collective-permute-start | bytes 294920 | tf_op jit(solution)/shard_map/ppermute | solution.py:184
  15.2 5.5 %collective-permute-start.8 = (bf16[6,2,8,512]{3,2,1,0:T(8,128)(2,1)S(1)}, bf16[6,2,8,512]{3,2,1,0:T(8,128)(2,1)S(1)}, u32[]{:S(2)}, u32[]{:S(2)}) collective-permute-start(bf16[6,2,8,512]{3,2,1,0:T(8,128)(2,1)S(1)} %pad_maximum_fusion.1), channel_id=1, source_target_pairs={{5,0},{4,1},{7,2},{6,3},{1,4},{0,5},{3,6},{2,7},{13,8},{12,9},{15,... | collective-permute-start | bytes 294920 | tf_op jit(solution)/shard_map/ppermute | solution.py:190
  16.7 4.0 %copy-start.1 = (s32[4]{0:T(128)S(1)}, s32[4]{0:T(128)}, u32[]{:S(2)}) copy-start(s32[4]{0:T(128)} %length_ref) | copy-start | bytes 52
  16.7 5.0 %collective-permute-start.10 = (bf16[6,2,8,512]{3,2,1,0:T(8,128)(2,1)S(1)}, bf16[6,2,8,512]{3,2,1,0:T(8,128)(2,1)S(1)}, u32[]{:S(2)}, u32[]{:S(2)}) collective-permute-start(bf16[6,2,8,512]{3,2,1,0:T(8,128)(2,1)S(1)} %pad_maximum_fusion.2), channel_id=1, source_target_pairs={{1,0},{0,1},{3,2},{2,3},{5,4},{4,5},{7,6},{6,7},{9,8},{8,9},{11,10... | collective-permute-start | bytes 294920 | tf_op jit(solution)/shard_map/ppermute | solution.py:190
